TPU v7x, 512 devices: a whole 4x4x16 slice. The times are simulated.
512 devices in a mesh: tok: 32 (over x, y, core), fsdp: 16 (over z).
Axes of the slice: x: 4, y: 4, z: 16, core: 2. Of those that a mesh axis runs over, the one named last changes fastest.
Arguments:
- hidden: bfloat16 [65536, 4096], P(('fsdp', 'tok')), may hold values from -6 to 6
- queries: bfloat16 [65536, 4096], P(('fsdp', 'tok')), may hold values from -64 to 64
- upstream: bfloat16 [65536, 4096], P(('fsdp', 'tok')), may hold values from -6 to 6
- context_weight: bfloat16 [4096, 1024], P('fsdp'), may hold values from -0.09375 to 0.09375
- lengths: int32 [16, 16], P('fsdp'), may hold values from 1 to 512, 4096 in all within a row
Outputs:
- log_totals: float32 [32, 65536], P(None, ('fsdp', 'tok'))
- query_slopes: bfloat16 [65536, 4096], P(('fsdp', 'tok'))
- context_slopes: bfloat16 [65536, 1024], P(('fsdp', 'tok'))
Inputs may be any that keep to these rules, and one draw needn't show every extreme that they name: Row p holds the lengths of pack p's documents in order; each row sums to 4096 and its longest document has exactly 512 tokens.
All inputs are finite; a program needn't handle non-finite values.
Results may differ from a plain program's by a relative error of at most 0.03.
The roundings to bfloat16 on the way count: a program that leaves them out, or rounds other values in their place, can miss the bound.
Values may be sent and summed in bfloat16 or wider, within the bound.
No kernel may reach another device: no remote copies, remote signals or barrier semaphores. Data moves between devices by JAX's collectives and lax.ppermute only.
A program may use at most 64 MiB of HBM per device.

v0:
```python
import math

import jax
import jax.numpy as jnp
from jax import lax
from jax.sharding import PartitionSpec as P

QH = 32
KVH = 4
HD = 128
SPAN = 4


def passed_along(block, axis, distance):
    devices = range(lax.axis_size(axis))
    route = [(i - distance, i) for i in devices if i - distance in devices]
    return lax.ppermute(block, axis, route)


def document_of(places, bounds):
    return jnp.sum((places[:, None] >= bounds[None, :]).astype(jnp.int32), axis=1)


def permitted(query_places, key_places, bounds):
    same_document = (
        document_of(query_places, bounds)[:, None] == document_of(key_places, bounds)[None, :]
    )
    return (
        same_document & (key_places[None, :] >= 0) & (key_places[None, :] <= query_places[:, None])
    )


def attend(query_block, key_block, value_block, upstream_block, allowed, score_scale):
    scores = (
        jnp.einsum("rkge,cke->kgrc", query_block, key_block, preferred_element_type=jnp.float32)
        * score_scale
    )
    scores = jnp.where(allowed, scores, -jnp.inf)
    highest = jnp.max(scores, axis=-1)
    totals = jnp.sum(jnp.exp(scores - highest[..., None]), axis=-1)
    log_total = highest + jnp.log(totals)
    weights = jnp.exp(scores - log_total[..., None])
    rounded = weights.astype(jnp.bfloat16)
    attended = lax.optimization_barrier(
        jnp.einsum(
            "kgrc,cke->rkge", rounded, value_block, preferred_element_type=jnp.float32
        ).astype(jnp.bfloat16)
    )
    inner_sum = jnp.sum(upstream_block.astype(jnp.float32) * attended.astype(jnp.float32), axis=-1)
    pushed = jnp.einsum(
        "rkge,cke->kgrc", upstream_block, value_block, preferred_element_type=jnp.float32
    )
    score_change = (weights * (pushed - jnp.transpose(inner_sum, (1, 2, 0))[..., None])).astype(
        jnp.bfloat16
    )
    query_slope = (
        jnp.einsum("kgrc,cke->rkge", score_change, key_block, preferred_element_type=jnp.float32)
        * score_scale
    )
    key_slope = (
        jnp.einsum("kgrc,rkge->cke", score_change, query_block, preferred_element_type=jnp.float32)
        * score_scale
    )
    value_slope = jnp.einsum(
        "kgrc,rkge->cke", rounded, upstream_block, preferred_element_type=jnp.float32
    )
    return (log_total, query_slope, key_slope, value_slope)


def body(hidden, queries, upstream, context_weight, lengths):
    row_count = hidden.shape[0]
    context = jnp.dot(
        hidden,
        lax.all_gather(context_weight, "fsdp", axis=0, tiled=True),
        preferred_element_type=jnp.float32,
    ).astype(jnp.bfloat16)
    bounds = jnp.cumsum(lengths[0])
    score_scale = 1.0 / math.sqrt(HD)
    group_size = QH // KVH
    device = lax.axis_index("tok")
    pieces = []
    for distance in range(SPAN, 0, -1):
        pieces.append(passed_along(context, "tok", distance))
    window = jnp.concatenate(pieces + [context], axis=0)
    key_count = window.shape[0]
    query_places = device * row_count + jnp.arange(row_count, dtype=jnp.int32)
    key_places = device * row_count - SPAN * row_count + jnp.arange(key_count, dtype=jnp.int32)
    allowed = permitted(query_places, key_places, bounds)
    halves = window.reshape(key_count, 2, KVH, HD)
    log_total, query_slope, key_slope, value_slope = attend(
        queries.reshape(row_count, KVH, group_size, HD),
        halves[:, 0],
        halves[:, 1],
        upstream.reshape(row_count, KVH, group_size, HD),
        allowed,
        score_scale,
    )
    log_totals = log_total.reshape(QH, row_count)
    query_slopes = query_slope.reshape(row_count, QH * HD).astype(jnp.bfloat16)
    partial_value = jnp.concatenate(
        [key_slope.reshape(key_count, KVH * HD), value_slope.reshape(key_count, KVH * HD)], axis=1
    )
    collected = partial_value[SPAN * row_count :]
    for distance in range(1, SPAN + 1):
        offset = (SPAN - distance) * row_count
        collected = collected + passed_along(
            partial_value[offset : offset + row_count], "tok", -distance
        )
    context_slopes = collected.astype(jnp.bfloat16)
    return (log_totals, query_slopes, context_slopes)


def solution(mesh):
    in_specs = (
        P(("fsdp", "tok"), None),
        P(("fsdp", "tok"), None),
        P(("fsdp", "tok"), None),
        P("fsdp", None),
        P("fsdp", None),
    )
    out_specs = (P(None, ("fsdp", "tok")), P(("fsdp", "tok"), None), P(("fsdp", "tok"), None))
    return jax.shard_map(body, mesh=mesh, in_specs=in_specs, out_specs=out_specs, check_vma=False)
```

profile of v0, /device:TPU:27, one launch (start us, length us, event | category | flops | bytes accessed | tf_op | source)
XLA Modules:
  0.0 234.8 jit_solution(8822931044933762849)
XLA Ops:
  7.2 0.0 copy-start
  7.2 0.0 all-gather.2.cloned.1.call-start
  7.2 0.7 all-gather.2.cloned.1.call-update
  7.9 0.7 copy.40
  8.7 0.1 reduce
  8.8 0.1 convert_reduce_fusion.1
  8.9 0.1 convert_reduce_fusion
  9.0 0.0 copy-start.3
  9.0 111.2 %all-gather.2.cloned.1.call-done = bf16[4096,1024]{1,0:T(8,128)(2,1)} async-done(((bf16[256,1024]{1,0:T(8,128)(2,1)}), bf16[4096,1024]{1,0:T(8,128)(2,1)}) %all-gather.2.cloned.1.call-update) | async-done | bytes 8388624 | tf_op jit(solution)/shard_map/all_gather | solution.py:74
  120.3 0.0 copy-done
  120.3 5.3 %convolution_convert_fusion.1 = bf16[128,1024]{1,0:T(8,128)(2,1)} fusion(bf16[128,4096]{1,0:T(8,128)(2,1)S(1)} %copy-done, bf16[4096,1024]{1,0:T(8,128)(2,1)} %all-gather.2.cloned.1.call-done), kind=kOutput, calls=%fused_computation.22 | convolution fusion | flops 1073872896 | bytes 9699328 | tf_op jit(solution)/shard_map/dot_general | solution.py:72
  125.6 3.9 %collective-permute-start = (bf16[128,1024]{1,0:T(8,128)(2,1)}, bf16[128,1024]{1,0:T(8,128)(2,1)}, u32[]{:S(2)}, u32[]{:S(2)}) collective-permute-start(bf16[128,1024]{1,0:T(8,128)(2,1)} %convolution_convert_fusion.1), channel_id=1, source_target_pairs={{0,64},{16,80},{32,96},{48,112},{64,128},{80,144},{96,160},{112,17... | collective-permute-start | bytes 786440 | tf_op jit(solution)/shard_map/ppermute | solution.py:17
  129.6 4.6 %collective-permute-start.1 = (bf16[128,1024]{1,0:T(8,128)(2,1)}, bf16[128,1024]{1,0:T(8,128)(2,1)}, u32[]{:S(2)}, u32[]{:S(2)}) collective-permute-start(bf16[128,1024]{1,0:T(8,128)(2,1)} %convolution_convert_fusion.1), channel_id=1, source_target_pairs={{0,48},{16,64},{32,80},{48,96},{64,112},{80,128},{96,144},{112,160... | collective-permute-start | bytes 786440 | tf_op jit(solution)/shard_map/ppermute | solution.py:17
  134.1 2.7 %collective-permute-start.2 = (bf16[128,1024]{1,0:T(8,128)(2,1)}, bf16[128,1024]{1,0:T(8,128)(2,1)}, u32[]{:S(2)}, u32[]{:S(2)}) collective-permute-start(bf16[128,1024]{1,0:T(8,128)(2,1)} %convolution_convert_fusion.1), channel_id=1, source_target_pairs={{0,32},{16,48},{32,64},{48,80},{64,96},{80,112},{96,128},{112,144}... | collective-permute-start | bytes 786440 | tf_op jit(solution)/shard_map/ppermute | solution.py:17
  136.9 0.3 compare_and_fusion
  137.2 0.0 copy-done.3
  137.2 0.7 copy.73
  137.9 2.3 copy.44
  140.2 2.1 collective-permute-start.3
  142.3 0.0 collective-permute-done
  142.3 1.0 constant_dynamic-update-slice_fusion.4
  143.2 1.1 collective-permute-done.1
  144.4 1.0 constant_dynamic-update-slice_fusion.3
  145.3 0.9 collective-permute-done.2
  146.3 1.0 constant_dynamic-update-slice_fusion.2
  147.2 2.8 %collective-permute-done.3 = bf16[128,1024]{1,0:T(8,128)(2,1)S(1)} collective-permute-done((bf16[128,1024]{1,0:T(8,128)(2,1)}, bf16[128,1024]{1,0:T(8,128)(2,1)S(1)}, u32[]{:S(2)}, u32[]{:S(2)}) %collective-permute-start.3) | collective-permute-done | bytes 262176 | tf_op jit(solution)/shard_map/ppermute | solution.py:17
  150.0 1.0 constant_dynamic-update-slice_fusion
  151.0 1.8 reshape.80
  152.8 1.7 fusion.23
  154.5 1.5 fusion.3
  156.1 2.2 exponential_reduce_fusion
  158.3 0.0 copy-start.4
  158.3 0.0 copy-start.2
  158.3 2.8 %fusion.5 = bf16[128,4,8,128]{0,3,2,1:T(8,128)(2,1)S(1)} fusion(bf16[640,1,4,128]{3,2,1,0:T(4,128)(2,1)S(1)} %get-tuple-element.16, f32[4,640,128,8]{2,1,3,0:T(8,128)S(1)} %get-tuple-element.19, f32[4,8,128]{2,1,0:T(8,128)S(1)} %log_add_fusion, pred[128,640]{0,1:T(8,128)(4,1)S(1)} %compare_and_fusion), kind=kOutput, calls=%fused_computation.21 | convolution fusion | flops 682098688 | bytes 12288000 | tf_op jit(solution)/shard_map/kgrc,cke->rkge/dot_general | solution.py:45
  161.1 0.0 copy-done.2
  161.1 0.4 multiply_reduce_fusion
  161.5 3.6 %fusion.16 = f32[4,640,128,1]{1,2,3,0:T(8,128)} fusion(bf16[128,4,8,128]{0,3,2,1:T(8,128)(2,1)S(1)} %bitcast.78, f32[4,640,128,8]{2,1,3,0:T(8,128)S(1)} %get-tuple-element.19, f32[4,8,128]{2,1,0:T(8,128)S(1)} %log_add_fusion, pred[128,640]{0,1:T(8,128)(4,1)S(1)} %compare_and_fusion), kind=kOutput, calls=%fused_computation.37 | convolution fusion | flops 681574400 | bytes 12943360 | tf_op jit(solution)/shard_map/kgrc,rkge->cke/dot_general | solution.py:64
  165.1 0.0 copy-done.4
  165.1 3.5 %fusion.1 = bf16[4,8,128,640]{2,3,1,0:T(8,128)(2,1)S(1)} fusion(f32[4,640,128,8]{2,1,3,0:T(8,128)S(1)} %get-tuple-element.19, f32[4,8,128]{2,1,0:T(8,128)S(1)} %bitcast.82, f32[4,8,128]{2,1,0:T(8,128)S(1)} %log_add_fusion, pred[128,640]{0,1:T(8,128)(4,1)S(1)} %compare_and_fusion, bf16[128,4,8,128]{0,3,2,1:T(8,128)(2,1)S(1)} %bitcast.79, ...), kind=kOutput, calls=%fused_computation.2 | convolution fusion | flops 686817280 | bytes 17547264 | tf_op jit(solution)/shard_map/rkge,cke->kgrc/dot_general | solution.py:50
  168.6 0.0 copy-start.1
  168.7 2.8 %fusion.4 = f32[4,640,128]{1,2,0:T(8,128)} fusion(bf16[4,8,128,640]{2,3,1,0:T(8,128)(2,1)S(1)} %fusion.1, bf16[128,4,8,128]{0,3,2,1:T(8,128)(2,1)S(1)} %bitcast.76), kind=kOutput, calls=%fused_computation.20 | convolution fusion | flops 671416320 | bytes 7602176 | tf_op jit(solution)/shard_map/kgrc,rkge->cke/dot_general | solution.py:61
  171.5 0.0 copy-done.1
  171.5 1.7 copy.53
  173.2 2.8 %copy.54 = f32[640,512]{1,0:T(8,128)} copy(f32[640,512]{0,1:T(8,128)} %bitcast.81) | data formatting | bytes 2621440 | tf_op jit(solution)/shard_map/reshape | solution.py:101
  176.0 2.6 %fusion.14 = (f32[128,1024]{1,0:T(8,128)}, f32[128,1024]{1,0:T(8,128)}, f32[128,1024]{1,0:T(8,128)}, f32[128,1024]{1,0:T(8,128)}) fusion(f32[640,512]{1,0:T(8,128)S(1)} %copy.53, f32[640,512]{1,0:T(8,128)} %copy.54), kind=kLoop, calls=%fused_computation.33 | loop fusion | flops 524288 | bytes 4718592 | tf_op jit(solution)/shard_map/concatenate | solution.py:100
  178.6 3.7 %collective-permute-start.7 = (f32[128,1024]{1,0:T(8,128)}, f32[128,1024]{1,0:T(8,128)S(1)}, u32[]{:S(2)}, u32[]{:S(2)}) collective-permute-start(f32[128,1024]{1,0:T(8,128)} %get-tuple-element.14), channel_id=1, source_target_pairs={{64,0},{80,16},{96,32},{112,48},{128,64},{144,80},{160,96},{176,11... | collective-permute-start | bytes 1572872 | tf_op jit(solution)/shard_map/ppermute | solution.py:17
  182.3 4.5 %collective-permute-start.6 = (f32[128,1024]{1,0:T(8,128)}, f32[128,1024]{1,0:T(8,128)}, u32[]{:S(2)}, u32[]{:S(2)}) collective-permute-start(f32[128,1024]{1,0:T(8,128)} %get-tuple-element.15), channel_id=1, source_target_pairs={{48,0},{64,16},{80,32},{96,48},{112,64},{128,80},{144,96},{160,112... | collective-permute-start | bytes 1572872 | tf_op jit(solution)/shard_map/ppermute | solution.py:17
  186.9 1.9 collective-permute-start.5
  188.8 2.3 collective-permute-start.4
  191.1 4.5 %multiply_convert_fusion = bf16[4,128,8,128]{3,1,2,0:T(8,128)(2,1)} fusion(bf16[4,8,128,640]{2,3,1,0:T(8,128)(2,1)} %copy-done.1, bf16[640,1,4,128]{3,2,1,0:T(4,128)(2,1)S(1)} %get-tuple-element.17), kind=kOutput, calls=%fused_computation.16 | convolution fusion | flops 672137216 | bytes 6946816 | tf_op jit(solution)/shard_map/kgrc,cke->rkge/dot_general | solution.py:57
  195.6 2.3 copy.55
  197.9 0.0 collective-permute-done.7
  197.9 12.9 %collective-permute-done.6 = f32[128,1024]{1,0:T(8,128)} collective-permute-done((f32[128,1024]{1,0:T(8,128)}, f32[128,1024]{1,0:T(8,128)}, u32[]{:S(2)}, u32[]{:S(2)}) %collective-permute-start.6) | collective-permute-done | bytes 524320 | tf_op jit(solution)/shard_map/ppermute | solution.py:17
  210.9 5.2 %collective-permute-done.5 = f32[128,1024]{1,0:T(8,128)} collective-permute-done((f32[128,1024]{1,0:T(8,128)}, f32[128,1024]{1,0:T(8,128)}, u32[]{:S(2)}, u32[]{:S(2)}) %collective-permute-start.5) | collective-permute-done | bytes 524320 | tf_op jit(solution)/shard_map/ppermute | solution.py:17
  216.0 9.6 %collective-permute-done.4 = f32[128,1024]{1,0:T(8,128)} collective-permute-done((f32[128,1024]{1,0:T(8,128)}, f32[128,1024]{1,0:T(8,128)}, u32[]{:S(2)}, u32[]{:S(2)}) %collective-permute-start.4) | collective-permute-done | bytes 524320 | tf_op jit(solution)/shard_map/ppermute | solution.py:17
  225.6 2.3 fusion.13
  (6 shorter events, 0.1 us)
Async XLA Ops:
  7.2 113.1 %copy-start = (bf16[128,4096]{1,0:T(8,128)(2,1)S(1)}, bf16[128,4096]{1,0:T(8,128)(2,1)}, u32[]{:S(2)}) copy-start(bf16[128,4096]{1,0:T(8,128)(2,1)} %param.5) | copy-start | bytes 3145732
  7.2 113.1 %all-gather.2.cloned.1.call-start = ((), (), s32[]{:S(2)}) async-start(), calls=%async_computation | async-start | bytes 8912896 | tf_op jit(solution)/shard_map/all_gather | solution.py:74
  9.0 128.2 %copy-start.3 = (bf16[128,4096]{1,0:T(8,128)(2,1)S(1)}, bf16[128,4096]{1,0:T(8,128)(2,1)}, u32[]{:S(2)}) copy-start(bf16[128,4096]{1,0:T(8,128)(2,1)} %param.6) | copy-start | bytes 3145732
  125.6 16.7 %collective-permute-start = (bf16[128,1024]{1,0:T(8,128)(2,1)}, bf16[128,1024]{1,0:T(8,128)(2,1)}, u32[]{:S(2)}, u32[]{:S(2)}) collective-permute-start(bf16[128,1024]{1,0:T(8,128)(2,1)} %convolution_convert_fusion.1), channel_id=1, source_target_pairs={{0,64},{16,80},{32,96},{48,112},{64,128},{80,144},{96,160},{112,17... | collective-permute-start | bytes 786440 | tf_op jit(solution)/shard_map/ppermute | solution.py:17
  129.6 14.8 %collective-permute-start.1 = (bf16[128,1024]{1,0:T(8,128)(2,1)}, bf16[128,1024]{1,0:T(8,128)(2,1)}, u32[]{:S(2)}, u32[]{:S(2)}) collective-permute-start(bf16[128,1024]{1,0:T(8,128)(2,1)} %convolution_convert_fusion.1), channel_id=1, source_target_pairs={{0,48},{16,64},{32,80},{48,96},{64,112},{80,128},{96,144},{112,160... | collective-permute-start | bytes 786440 | tf_op jit(solution)/shard_map/ppermute | solution.py:17
  134.1 12.1 %collective-permute-start.2 = (bf16[128,1024]{1,0:T(8,128)(2,1)}, bf16[128,1024]{1,0:T(8,128)(2,1)}, u32[]{:S(2)}, u32[]{:S(2)}) collective-permute-start(bf16[128,1024]{1,0:T(8,128)(2,1)} %convolution_convert_fusion.1), channel_id=1, source_target_pairs={{0,32},{16,48},{32,64},{48,80},{64,96},{80,112},{96,128},{112,144}... | collective-permute-start | bytes 786440 | tf_op jit(solution)/shard_map/ppermute | solution.py:17
  140.2 9.8 %collective-permute-start.3 = (bf16[128,1024]{1,0:T(8,128)(2,1)}, bf16[128,1024]{1,0:T(8,128)(2,1)S(1)}, u32[]{:S(2)}, u32[]{:S(2)}) collective-permute-start(bf16[128,1024]{1,0:T(8,128)(2,1)} %convolution_convert_fusion.1), channel_id=1, source_target_pairs={{0,16},{16,32},{32,48},{48,64},{64,80},{80,96},{96,112},{112,128},... | collective-permute-start | bytes 786440 | tf_op jit(solution)/shard_map/ppermute | solution.py:17
  158.3 6.9 %copy-start.4 = (f32[4,8,128]{2,1,0:T(8,128)}, f32[4,8,128]{2,1,0:T(8,128)S(1)}, u32[]{:S(2)}) copy-start(f32[4,8,128]{2,1,0:T(8,128)S(1)} %log_add_fusion) | copy-start | bytes 49156
  158.3 2.8 %copy-start.2 = (bf16[128,4096]{0,1:T(8,128)(2,1)S(1)}, bf16[128,4096]{0,1:T(8,128)(2,1)}, u32[]{:S(2)}) copy-start(bf16[128,4096]{0,1:T(8,128)(2,1)} %copy.44) | copy-start | bytes 3145732
  168.6 2.8 %copy-start.1 = (bf16[4,8,128,640]{2,3,1,0:T(8,128)(2,1)}, bf16[4,8,128,640]{2,3,1,0:T(8,128)(2,1)S(1)}, u32[]{:S(2)}) copy-start(bf16[4,8,128,640]{2,3,1,0:T(8,128)(2,1)S(1)} %fusion.1) | copy-start | bytes 15728644
  178.6 19.3 %collective-permute-start.7 = (f32[128,1024]{1,0:T(8,128)}, f32[128,1024]{1,0:T(8,128)S(1)}, u32[]{:S(2)}, u32[]{:S(2)}) collective-permute-start(f32[128,1024]{1,0:T(8,128)} %get-tuple-element.14), channel_id=1, source_target_pairs={{64,0},{80,16},{96,32},{112,48},{128,64},{144,80},{160,96},{176,11... | collective-permute-start | bytes 1572872 | tf_op jit(solution)/shard_map/ppermute | solution.py:17
  182.3 28.5 %collective-permute-start.6 = (f32[128,1024]{1,0:T(8,128)}, f32[128,1024]{1,0:T(8,128)}, u32[]{:S(2)}, u32[]{:S(2)}) collective-permute-start(f32[128,1024]{1,0:T(8,128)} %get-tuple-element.15), channel_id=1, source_target_pairs={{48,0},{64,16},{80,32},{96,48},{112,64},{128,80},{144,96},{160,112... | collective-permute-start | bytes 1572872 | tf_op jit(solution)/shard_map/ppermute | solution.py:17
  186.9 29.1 %collective-permute-start.5 = (f32[128,1024]{1,0:T(8,128)}, f32[128,1024]{1,0:T(8,128)}, u32[]{:S(2)}, u32[]{:S(2)}) collective-permute-start(f32[128,1024]{1,0:T(8,128)} %get-tuple-element.13), channel_id=1, source_target_pairs={{32,0},{48,16},{64,32},{80,48},{96,64},{112,80},{128,96},{144,112}... | collective-permute-start | bytes 1572872 | tf_op jit(solution)/shard_map/ppermute | solution.py:17
  188.8 36.8 %collective-permute-start.4 = (f32[128,1024]{1,0:T(8,128)}, f32[128,1024]{1,0:T(8,128)}, u32[]{:S(2)}, u32[]{:S(2)}) collective-permute-start(f32[128,1024]{1,0:T(8,128)} %get-tuple-element.12), channel_id=1, source_target_pairs={{16,0},{32,16},{48,32},{64,48},{80,64},{96,80},{112,96},{128,112},... | collective-permute-start | bytes 1572872 | tf_op jit(solution)/shard_map/ppermute | solution.py:17
Sparse Core Ops, SparseCore 0:
  10.1 110.1 all-gather.1
where the time goes:
time: 235 us
  waiting for transfers between devices  144 us (61%)
  starting transfers between devices  25.9 us (11%)
  matrix products  24.1 us (10%)
  local copies, waits for them, and re-layouts  17.9 us (8%)
  between operations  14.3 us (6%)
  other arithmetic  8.14 us (3%)
    all_gather x1, waiting for transfers between devices, body(): lax.all_gather(context_weight, 'fsdp', axis=0, tiled=True)  111 us
    ppermute x8, waiting for transfers between devices, passed_along(): return lax.ppermute(block, axis, route)  32.6 us
    ppermute x8, starting transfers between devices, passed_along(): return lax.ppermute(block, axis, route)  25.8 us
    unnamed x16, local copies, waits for them, and re-layouts  7.48 us
    dot_general x1, matrix products, body(): jnp.dot(hidden, lax.all_gather(context_weight, 'fsdp', axis=0, tiled=True...  5.34 us
  transfers between devices with their start and end apart: 9, of which 7 were waited for; matrix products, arithmetic and copies ran while one was open for 6% of the time, Pallas kernels for 0%

commit v1 on v0

v1 whole, which is shorter than its diff:
```python
import functools
import math

import jax
import jax.numpy as jnp
from jax import lax
from jax.experimental import pallas as pl
from jax.experimental.pallas import tpu as pltpu
from jax.sharding import PartitionSpec as P

QH = 32
KVH = 4
HD = 128
CORES = 2
BLOCK = 128
CHIP = CORES * BLOCK
GROUPS = KVH // CORES
HEADS = QH // KVH
SPAN = 4 * BLOCK
KEYS = SPAN + BLOCK
SCALE = 1.0 / math.sqrt(HD)
LOG2E = math.log2(math.e)


def shifted(block, distance):
    count = lax.axis_size("tok")
    route = [(i, i + distance) for i in range(count) if 0 <= i + distance < count]
    return lax.ppermute(block, "tok", route)


def swapped(block):
    count = lax.axis_size("tok")
    return lax.ppermute(block, "tok", [(i, i ^ 1) for i in range(count)])


def by_core(core, mine, other, axis):
    return jnp.where(
        core == 0,
        jnp.concatenate([mine, other], axis=axis),
        jnp.concatenate([other, mine], axis=axis),
    )


def half(block, index, axis):
    size = block.shape[axis] // 2
    return lax.dynamic_slice_in_dim(block, index * size, size, axis)


def attention_kernel(
    start_ref, q_ref, qt_ref, u_ref, ut_ref, far_ref, near_ref, here_ref,
    log_ref, dq_ref, dfar_ref, dnear_ref, dhere_ref,
    keys, values, sums, bias, weight_rows, change_rows,
):
    part = pl.program_id(1)

    @pl.when(part == 0)
    def _():
        for i, ref in enumerate((far_ref, near_ref, here_ref)):
            keys[i * CHIP : (i + 1) * CHIP, :] = ref[:, :HD]
            values[i * CHIP : (i + 1) * CHIP, :] = ref[:, HD:]
        sums[...] = jnp.zeros_like(sums)

    first = pl.multiple_of(part * BLOCK, BLOCK)
    key_window = keys[pl.ds(first, KEYS), :]
    value_window = values[pl.ds(first, KEYS), :]
    places = first - SPAN + lax.broadcasted_iota(jnp.int32, (BLOCK, KEYS), 1)
    own = first + lax.broadcasted_iota(jnp.int32, (BLOCK, KEYS), 0)
    bias[...] = jnp.where((places <= own) & (places >= start_ref[...]), 0.0, -jnp.inf)
    logs = jnp.zeros((BLOCK, HD), jnp.float32)
    lane = lax.broadcasted_iota(jnp.int32, (BLOCK, HD), 1)
    over_rows = (((1,), (1,)), ((), ()))
    for pair in range(HEADS // 2):
        rows = slice(pair * 2 * BLOCK, (pair + 1) * 2 * BLOCK)
        scores = lax.dot_general(
            q_ref[0, 0, rows, :], key_window, over_rows, preferred_element_type=jnp.float32
        )
        scores = scores + jnp.concatenate([bias[...], bias[...]], axis=0)
        highest = jnp.max(scores, axis=1, keepdims=True)
        raised = jnp.exp2((scores - highest) * (SCALE * LOG2E))
        total = jnp.sum(raised, axis=1, keepdims=True)
        log_total = highest * SCALE + jnp.log(total)
        weights = raised * (1.0 / total)
        rounded = weights.astype(jnp.bfloat16)
        weight_rows[rows, :] = rounded
        attended = jnp.dot(rounded, value_window, preferred_element_type=jnp.float32)
        attended = attended.astype(jnp.bfloat16).astype(jnp.float32)
        upstream = u_ref[0, 0, rows, :]
        inner = jnp.sum(upstream.astype(jnp.float32) * attended, axis=1, keepdims=True)
        pushed = lax.dot_general(
            upstream, value_window, over_rows, preferred_element_type=jnp.float32
        )
        change = (weights * (pushed - inner)).astype(jnp.bfloat16)
        change_rows[rows, :] = change
        slope = jnp.dot(change, key_window, preferred_element_type=jnp.float32) * SCALE
        for i in range(2):
            head = pair * 2 + i
            part_rows = slice(i * BLOCK, (i + 1) * BLOCK)
            dq_ref[:, head * HD : (head + 1) * HD] = slope[part_rows].astype(jnp.bfloat16)
            logs = jnp.where(lane == head, log_total[part_rows], logs)
    log_ref[0] = logs.T[:HEADS]
    key_slope = jnp.dot(qt_ref[0, 0], change_rows[...], preferred_element_type=jnp.float32)
    value_slope = jnp.dot(ut_ref[0, 0], weight_rows[...], preferred_element_type=jnp.float32)
    sums[pl.ds(first, KEYS), :HD] += key_slope.T * SCALE
    sums[pl.ds(first, KEYS), HD:] += value_slope.T

    @pl.when(part == CORES - 1)
    def _():
        for i, ref in enumerate((dfar_ref, dnear_ref, dhere_ref)):
            ref[...] = sums[i * CHIP : (i + 1) * CHIP, :].astype(ref.dtype)


def attention(starts, q, qt, u, ut, far, near, here):
    stacked = HEADS * BLOCK
    rows = pl.BlockSpec((1, 1, stacked, HD), lambda g, b: (b, g, 0, 0))
    columns = pl.BlockSpec((1, 1, HD, stacked), lambda g, b: (b, g, 0, 0))
    context = pl.BlockSpec((CHIP, 2 * HD), lambda g, b: (0, g))
    wide = GROUPS * 2 * HD
    return pl.pallas_call(
        attention_kernel,
        grid=(GROUPS, CORES),
        in_specs=[
            pl.BlockSpec((BLOCK, 1), lambda g, b: (b, 0)),
            rows, columns, rows, columns, context, context, context,
        ],
        out_specs=[
            pl.BlockSpec((1, HEADS, BLOCK), lambda g, b: (b, g, 0)),
            pl.BlockSpec((BLOCK, HEADS * HD), lambda g, b: (b, g)),
            context, context, context,
        ],
        out_shape=[
            jax.ShapeDtypeStruct((CORES, GROUPS * HEADS, BLOCK), jnp.float32),
            jax.ShapeDtypeStruct((CHIP, GROUPS * HEADS * HD), jnp.bfloat16),
            jax.ShapeDtypeStruct((CHIP, wide), jnp.bfloat16),
            jax.ShapeDtypeStruct((CHIP, wide), jnp.bfloat16),
            jax.ShapeDtypeStruct((CHIP, wide), jnp.float32),
        ],
        scratch_shapes=[
            pltpu.VMEM((SPAN + CHIP, HD), jnp.bfloat16),
            pltpu.VMEM((SPAN + CHIP, HD), jnp.bfloat16),
            pltpu.VMEM((SPAN + CHIP, 2 * HD), jnp.float32),
            pltpu.VMEM((BLOCK, KEYS), jnp.float32),
            pltpu.VMEM((stacked, KEYS), jnp.bfloat16),
            pltpu.VMEM((stacked, KEYS), jnp.bfloat16),
        ],
        compiler_params=pltpu.CompilerParams(vmem_limit_bytes=48 * 2**20),
        cost_estimate=pl.CostEstimate(
            flops=12 * CHIP * KEYS * HD * GROUPS * HEADS,
            bytes_accessed=8 * 2**20,
            transcendentals=CHIP * KEYS * GROUPS * HEADS,
        ),
        name="attention",
    )(starts, q, qt, u, ut, far, near, here)


def body(hidden, queries, upstream, context_weight, lengths):
    device = lax.axis_index("tok")
    core, chip = device % CORES, device // CORES
    ordered = context_weight.reshape(-1, 2, CORES, GROUPS, HD)
    ordered = lax.dynamic_slice_in_dim(ordered, core, 1, 2)[:, :, 0]
    ordered = ordered.transpose(0, 2, 1, 3).reshape(-1, GROUPS * 2 * HD)
    weight = lax.all_gather(ordered, "fsdp", axis=0, tiled=True)

    both = by_core(core, hidden, swapped(hidden), 0)

    def heads_of(block):
        mine = half(block, core, 1)
        other = swapped(half(block, 1 - core, 1))
        whole = by_core(core, mine, other, 0).reshape(CORES, BLOCK, GROUPS, HEADS, HD)
        rows = whole.transpose(0, 2, 3, 1, 4).reshape(CORES, GROUPS, HEADS * BLOCK, HD)
        columns = whole.transpose(0, 2, 4, 3, 1).reshape(CORES, GROUPS, HD, HEADS * BLOCK)
        return rows, columns

    q, qt = heads_of(queries)
    u, ut = heads_of(upstream)
    bounds = jnp.cumsum(lengths[0])
    places = chip * CHIP + jnp.arange(CHIP, dtype=jnp.int32)
    starts = jnp.max(jnp.where(bounds[None, :] <= places[:, None], bounds[None, :], 0), axis=1)
    starts = (starts - chip * CHIP).astype(jnp.int32)[:, None]

    here = jnp.dot(both, weight, preferred_element_type=jnp.float32).astype(jnp.bfloat16)
    near = shifted(here, CORES)
    far = shifted(here, 2 * CORES)
    logs, dq, dfar, dnear, dhere = attention(starts, q, qt, u, ut, far, near, here)

    context_slopes = (
        dhere
        + shifted(dnear, -CORES).astype(jnp.float32)
        + shifted(dfar, -2 * CORES).astype(jnp.float32)
    ).astype(jnp.bfloat16)
    query_slopes = by_core(core, half(dq, core, 0), swapped(half(dq, 1 - core, 0)), 1)
    log_totals = by_core(core, half(logs, core, 0)[0], swapped(half(logs, 1 - core, 0)[0]), 0)
    context_slopes = by_core(
        core, half(context_slopes, core, 0), swapped(half(context_slopes, 1 - core, 0)), 1
    )
    context_slopes = context_slopes.reshape(BLOCK, KVH, 2, HD).transpose(0, 2, 1, 3)
    return log_totals, query_slopes, context_slopes.reshape(BLOCK, 2 * KVH * HD)


def solution(mesh):
    in_specs = (
        P(("fsdp", "tok"), None),
        P(("fsdp", "tok"), None),
        P(("fsdp", "tok"), None),
        P("fsdp", None),
        P("fsdp", None),
    )
    out_specs = (P(None, ("fsdp", "tok")), P(("fsdp", "tok"), None), P(("fsdp", "tok"), None))
    return jax.shard_map(body, mesh=mesh, in_specs=in_specs, out_specs=out_specs, check_vma=False)
```

time: 235 us -> 187 us (0.80)
  the two profiles are of different devices: /device:TPU:27 before, /device:TPU:7 now
where the time goes in v1:
time: 187 us
  waiting for transfers between devices  82.9 us (44%)
  starting transfers between devices  43.5 us (23%)
  Pallas kernels  18.6 us (10%)
  local copies, waits for them, and re-layouts  18.1 us (10%)
  between operations  14.4 us (8%)
  matrix products  4.76 us (3%)
  other arithmetic  4.31 us (2%)
    all_gather x1, waiting for transfers between devices, body(): weight = lax.all_gather(ordered, 'fsdp', axis=0, tiled=True)  81.7 us
    ppermute x6, starting transfers between devices, swapped(): return lax.ppermute(block, 'tok', [(i, i ^ 1) for i in range(count)])  29.4 us
    pallas_call x1, Pallas kernels, attention(): pl.pallas_call(attention_kernel, grid=(GROUPS, CORES), in_specs=[pl.Block...  18.6 us
    ppermute x4, starting transfers between devices, shifted(): return lax.ppermute(block, 'tok', route)  14.1 us
    dot_general x1, matrix products, body(): jnp.dot(both, weight, preferred_element_type=jnp.float32)  4.76 us
    select_n x4, local copies, waits for them, and re-layouts, by_core(): jnp.where(core == 0, jnp.concatenate([mine, other], axis=axis), jnp.conca...  4.52 us
    unnamed x15, local copies, waits for them, and re-layouts  4.04 us
    reshape x2, local copies, waits for them, and re-layouts, heads_of(): whole.transpose(0, 2, 4, 3, 1).reshape(CORES, GROUPS, HD, HEADS * BLOCK)  3.83 us
  transfers between devices with their start and end apart: 11, of which 2 were waited for; matrix products, arithmetic and copies ran while one was open for 11% of the time, Pallas kernels for 0%

profile of v1, /device:TPU:7, one launch (start us, length us, event | category | flops | bytes accessed | tf_op | source)
XLA Modules:
  0.0 186.6 jit_solution(7537000006410123528)
XLA Ops:
  7.2 0.0 copy-start.4
  7.2 0.0 all-gather.2.cloned.1.call-start
  7.2 1.5 reshape.85
  8.7 0.2 constant_dynamic-slice_fusion.4
  8.9 0.9 copy.30
  9.8 0.0 all-gather.2.cloned.1.call-update
  9.8 2.6 %collective-permute-start.2 = (bf16[128,4096]{1,0:T(8,128)(2,1)}, bf16[128,4096]{1,0:T(8,128)(2,1)}, u32[]{:S(2)}, u32[]{:S(2)}) collective-permute-start(bf16[128,4096]{1,0:T(8,128)(2,1)} %param.5), channel_id=1, source_target_pairs={{0,16},{16,0},{32,48},{48,32},{64,80},{80,64},{96,112},{112,96},{1... | collective-permute-start | bytes 3145736 | tf_op jit(solution)/shard_map/ppermute | solution.py:33
  12.4 0.0 copy-done.4
  12.4 0.0 copy-start.5
  12.4 0.1 constant_dynamic-slice_fusion.6
  12.6 1.9 %collective-permute-start.1 = (bf16[128,2048]{1,0:T(8,128)(2,1)S(1)}, bf16[128,2048]{1,0:T(8,128)(2,1)S(1)}, u32[]{:S(2)}, u32[]{:S(2)}) collective-permute-start(bf16[128,2048]{1,0:T(8,128)(2,1)S(1)} %get-tuple-element.16), channel_id=1, source_target_pairs={{0,16},{16,0},{32,48},{48,32},{64,80},{80,64},{96,112},{112,96},{1... | collective-permute-start | bytes 1572872 | tf_op jit(solution)/shard_map/ppermute | solution.py:33
  14.5 1.3 constant_dynamic-slice_fusion.8
  15.8 2.4 %collective-permute-start = (bf16[128,2048]{1,0:T(8,128)(2,1)S(1)}, bf16[128,2048]{1,0:T(8,128)(2,1)S(1)}, u32[]{:S(2)}, u32[]{:S(2)}) collective-permute-start(bf16[128,2048]{1,0:T(8,128)(2,1)S(1)} %get-tuple-element.18), channel_id=1, source_target_pairs={{0,16},{16,0},{32,48},{48,32},{64,80},{80,64},{96,112},{112,96},{1... | collective-permute-start | bytes 1572872 | tf_op jit(solution)/shard_map/ppermute | solution.py:33
  18.2 0.0 copy-done.5
  18.2 0.1 copy.22
  18.4 0.1 reduce
  18.5 0.1 select_reduce_fusion
  18.6 0.0 collective-permute-done.2
  18.6 81.7 %all-gather.2.cloned.1.call-done = bf16[4096,512]{0,1:T(8,128)(2,1)} async-done(((bf16[256,512]{0,1:T(8,128)(2,1)}), bf16[4096,512]{0,1:T(8,128)(2,1)}) %all-gather.2.cloned.1.call-update) | async-done | bytes 4194320 | tf_op jit(solution)/shard_map/all_gather | solution.py:161
  100.3 4.8 %fusion.7.here_ref = bf16[256,512]{1,0:T(8,128)(2,1)S(1)} fusion(bf16[4096,512]{0,1:T(8,128)(2,1)} %all-gather.2.cloned.1.call-done, bf16[128,4096]{1,0:T(8,128)(2,1)} %collective-permute-done.2, bf16[128,4096]{1,0:T(8,128)(2,1)} %param.5, pred[]{:T(512)S(6)} %eq.4), kind=kOutput, calls=%fused_computation.8 | convolution fusion | flops 1083310080 | bytes 6553601 | tf_op jit(solution)/shard_map/dot_general | solution.py:180
  105.1 4.6 %collective-permute-start.3 = (bf16[256,512]{1,0:T(8,128)(2,1)S(1)}, bf16[256,512]{1,0:T(8,128)(2,1)}, u32[]{:S(2)}, u32[]{:S(2)}) collective-permute-start(bf16[256,512]{1,0:T(8,128)(2,1)S(1)} %fusion.7.here_ref), channel_id=1, source_target_pairs={{0,64},{16,80},{32,96},{48,112},{64,128},{80,144},{96,160},{112,17... | collective-permute-start | bytes 786440 | tf_op jit(solution)/shard_map/ppermute | solution.py:28
  109.7 2.2 %collective-permute-start.4 = (bf16[256,512]{1,0:T(8,128)(2,1)S(1)}, bf16[256,512]{1,0:T(8,128)(2,1)}, u32[]{:S(2)}, u32[]{:S(2)}) collective-permute-start(bf16[256,512]{1,0:T(8,128)(2,1)S(1)} %fusion.7.here_ref), channel_id=1, source_target_pairs={{0,32},{16,48},{32,64},{48,80},{64,96},{80,112},{96,128},{112,144}... | collective-permute-start | bytes 786440 | tf_op jit(solution)/shard_map/ppermute | solution.py:28
  112.0 0.1 copy.28.start_ref
  112.1 0.0 collective-permute-done.1
  112.1 0.0 collective-permute-done
  112.1 1.8 fusion.8
  113.9 0.2 copy.31
  114.1 2.0 %copy.24 = bf16[2,128,2,8,128]{1,3,4,2,0:T(8,128)(2,1)} copy(bf16[2,128,2,8,128]{4,3,2,1,0:T(8,128)(2,1)S(1)} %bitcast.36) | data formatting | bytes 2097152 | tf_op jit(solution)/shard_map/jit(_where)/select_n | solution.py:37
  116.1 0.0 copy-start.3
  116.1 0.3 copy.23
  116.4 0.9 copy-done.3
  117.3 0.2 copy.32
  117.6 2.0 %copy.26 = bf16[2,128,2,8,128]{1,3,4,2,0:T(8,128)(2,1)} copy(bf16[2,128,2,8,128]{4,3,2,1,0:T(8,128)(2,1)S(1)} %bitcast.38) | data formatting | bytes 2097152 | tf_op jit(solution)/shard_map/jit(_where)/select_n | solution.py:37
  119.5 0.3 copy.25
  119.8 1.5 reshape.82.qt_ref
  121.3 2.3 %reshape.84.ut_ref = bf16[2,2,128,1024]{3,2,1,0:T(8,128)(2,1)} reshape(bf16[2,2,128,8,128]{4,3,2,1,0:T(8,128)(2,1)} %bitcast.41) | data formatting | bytes 2097152 | tf_op jit(solution)/shard_map/reshape | solution.py:170
  123.7 0.0 collective-permute-done.3.far_ref
  123.7 0.0 collective-permute-done.4.near_ref
  123.7 18.6 %attention.1 = (f32[2,16,128]{2,1,0:T(8,128)S(1)}, bf16[256,2048]{1,0:T(8,128)(2,1)S(1)}, bf16[256,512]{1,0:T(8,128)(2,1)}, bf16[256,512]{1,0:T(8,128)(2,1)}, f32[256,512]{1,0:T(8,128)S(1)}) custom-call(s32[256,1]{1,0:T(8,128)S(1)} %copy.28.start_ref, bf16[2,2,1024,128]{3,2,1,0:T(8,128)(2,1)S(1)} %bitcast.34, bf16[2,2,128,1024]{3,2,1,0:T(8,128)(2,1)S(1)} %reshape.82.qt_ref, ...), custom_call_target="tpu_custom_call" | custom-call | flops 4026531840 | bytes 8388608 | tf_op jit(solution)/shard_map/attention/pallas_call | solution.py:118
  142.3 0.0 copy-start
  142.3 1.0 copy-done
  143.2 0.0 copy-start.1
  143.2 0.8 copy-done.1
  144.0 0.0 copy-start.2
  144.0 5.3 %collective-permute-start.7 = (bf16[256,512]{1,0:T(8,128)(2,1)}, bf16[256,512]{1,0:T(8,128)(2,1)S(1)}, u32[]{:S(2)}, u32[]{:S(2)}) collective-permute-start(bf16[256,512]{1,0:T(8,128)(2,1)} %get-tuple-element.11), channel_id=1, source_target_pairs={{32,0},{48,16},{64,32},{80,48},{96,64},{112,80},{128,96},{144,112}... | collective-permute-start | bytes 786440 | tf_op jit(solution)/shard_map/ppermute | solution.py:28
  149.3 1.9 %collective-permute-start.8 = (bf16[256,512]{1,0:T(8,128)(2,1)}, bf16[256,512]{1,0:T(8,128)(2,1)S(1)}, u32[]{:S(2)}, u32[]{:S(2)}) collective-permute-start(bf16[256,512]{1,0:T(8,128)(2,1)} %get-tuple-element.12), channel_id=1, source_target_pairs={{64,0},{80,16},{96,32},{112,48},{128,64},{144,80},{160,96},{176,11... | collective-permute-start | bytes 786440 | tf_op jit(solution)/shard_map/ppermute | solution.py:28
  151.3 1.3 constant_dynamic-slice_fusion.3
  152.6 13.9 %collective-permute-start.6 = (bf16[128,2048]{1,0:T(8,128)(2,1)S(1)}, bf16[128,2048]{1,0:T(8,128)(2,1)S(1)}, u32[]{:S(2)}, u32[]{:S(2)}) collective-permute-start(bf16[128,2048]{1,0:T(8,128)(2,1)S(1)} %get-tuple-element.14), channel_id=1, source_target_pairs={{0,16},{16,0},{32,48},{48,32},{64,80},{80,64},{96,112},{112,96},{1... | collective-permute-start | bytes 1572872 | tf_op jit(solution)/shard_map/ppermute | solution.py:33
  166.5 0.0 collective-permute-done.7
  166.5 0.0 collective-permute-done.8
  166.5 0.0 copy-done.2
  166.6 0.1 add_convert_fusion
  166.7 6.7 %collective-permute-start.9 = (bf16[128,512]{1,0:T(8,128)(2,1)S(1)}, bf16[128,512]{1,0:T(8,128)(2,1)S(1)}, u32[]{:S(2)}, u32[]{:S(2)}) collective-permute-start(bf16[128,512]{1,0:T(8,128)(2,1)S(1)} %get-tuple-element.20), channel_id=1, source_target_pairs={{0,16},{16,0},{32,48},{48,32},{64,80},{80,64},{96,112},{112,96},{1... | collective-permute-start | bytes 393224 | tf_op jit(solution)/shard_map/ppermute | solution.py:33
  173.4 1.9 %collective-permute-start.5 = (f32[16,128]{1,0:T(8,128)S(1)}, f32[16,128]{1,0:T(8,128)S(1)}, u32[]{:S(2)}, u32[]{:S(2)}) collective-permute-start(f32[16,128]{1,0:T(8,128)S(1)} %get-tuple-element.22), channel_id=1, source_target_pairs={{0,16},{16,0},{32,48},{48,32},{64,80},{80,64},{96,112},{112,96},{1... | collective-permute-start | bytes 24584 | tf_op jit(solution)/shard_map/ppermute | solution.py:33
  175.3 1.1 collective-permute-done.5
  176.5 0.6 maximum_select_fusion.7
  177.1 0.0 collective-permute-done.9
  177.2 0.4 fusion.10
  177.6 0.1 copy.29
  177.7 0.9 reshape.87
  178.5 0.0 collective-permute-done.6
  178.5 1.2 maximum_select_fusion.6
  (7 shorter events, 0.2 us)
Async XLA Ops:
  7.2 5.3 %copy-start.4 = (bf16[128,4096]{1,0:T(8,128)(2,1)S(1)}, bf16[128,4096]{1,0:T(8,128)(2,1)}, u32[]{:S(2)}) copy-start(bf16[128,4096]{1,0:T(8,128)(2,1)} %param.7) | copy-start | bytes 3145732
  7.2 93.1 %all-gather.2.cloned.1.call-start = ((), (), s32[]{:S(2)}) async-start(), calls=%async_computation | async-start | bytes 4456448 | tf_op jit(solution)/shard_map/all_gather | solution.py:161
  9.8 8.8 %collective-permute-start.2 = (bf16[128,4096]{1,0:T(8,128)(2,1)}, bf16[128,4096]{1,0:T(8,128)(2,1)}, u32[]{:S(2)}, u32[]{:S(2)}) collective-permute-start(bf16[128,4096]{1,0:T(8,128)(2,1)} %param.5), channel_id=1, source_target_pairs={{0,16},{16,0},{32,48},{48,32},{64,80},{80,64},{96,112},{112,96},{1... | collective-permute-start | bytes 3145736 | tf_op jit(solution)/shard_map/ppermute | solution.py:33
  12.4 5.8 %copy-start.5 = (s32[1,16]{1,0:T(1,128)S(1)}, s32[1,16]{1,0:T(1,128)}, u32[]{:S(2)}) copy-start(s32[1,16]{1,0:T(1,128)} %param.9) | copy-start | bytes 196
  12.6 99.6 %collective-permute-start.1 = (bf16[128,2048]{1,0:T(8,128)(2,1)S(1)}, bf16[128,2048]{1,0:T(8,128)(2,1)S(1)}, u32[]{:S(2)}, u32[]{:S(2)}) collective-permute-start(bf16[128,2048]{1,0:T(8,128)(2,1)S(1)} %get-tuple-element.16), channel_id=1, source_target_pairs={{0,16},{16,0},{32,48},{48,32},{64,80},{80,64},{96,112},{112,96},{1... | collective-permute-start | bytes 1572872 | tf_op jit(solution)/shard_map/ppermute | solution.py:33
  15.8 96.3 %collective-permute-start = (bf16[128,2048]{1,0:T(8,128)(2,1)S(1)}, bf16[128,2048]{1,0:T(8,128)(2,1)S(1)}, u32[]{:S(2)}, u32[]{:S(2)}) collective-permute-start(bf16[128,2048]{1,0:T(8,128)(2,1)S(1)} %get-tuple-element.18), channel_id=1, source_target_pairs={{0,16},{16,0},{32,48},{48,32},{64,80},{80,64},{96,112},{112,96},{1... | collective-permute-start | bytes 1572872 | tf_op jit(solution)/shard_map/ppermute | solution.py:33
  105.1 18.6 %collective-permute-start.3 = (bf16[256,512]{1,0:T(8,128)(2,1)S(1)}, bf16[256,512]{1,0:T(8,128)(2,1)}, u32[]{:S(2)}, u32[]{:S(2)}) collective-permute-start(bf16[256,512]{1,0:T(8,128)(2,1)S(1)} %fusion.7.here_ref), channel_id=1, source_target_pairs={{0,64},{16,80},{32,96},{48,112},{64,128},{80,144},{96,160},{112,17... | collective-permute-start | bytes 786440 | tf_op jit(solution)/shard_map/ppermute | solution.py:28
  109.7 13.9 %collective-permute-start.4 = (bf16[256,512]{1,0:T(8,128)(2,1)S(1)}, bf16[256,512]{1,0:T(8,128)(2,1)}, u32[]{:S(2)}, u32[]{:S(2)}) collective-permute-start(bf16[256,512]{1,0:T(8,128)(2,1)S(1)} %fusion.7.here_ref), channel_id=1, source_target_pairs={{0,32},{16,48},{32,64},{48,80},{64,96},{80,112},{96,128},{112,144}... | collective-permute-start | bytes 786440 | tf_op jit(solution)/shard_map/ppermute | solution.py:28
  116.1 1.2 copy-start.3
  142.3 1.0 copy-start
  143.2 0.8 copy-start.1
  144.0 22.5 %copy-start.2 = (f32[256,512]{1,0:T(8,128)S(1)}, f32[256,512]{1,0:T(8,128)}, u32[]{:S(2)}) copy-start(f32[256,512]{1,0:T(8,128)} %copy-done.1) | copy-start | bytes 1572868
  144.0 22.5 %collective-permute-start.7 = (bf16[256,512]{1,0:T(8,128)(2,1)}, bf16[256,512]{1,0:T(8,128)(2,1)S(1)}, u32[]{:S(2)}, u32[]{:S(2)}) collective-permute-start(bf16[256,512]{1,0:T(8,128)(2,1)} %get-tuple-element.11), channel_id=1, source_target_pairs={{32,0},{48,16},{64,32},{80,48},{96,64},{112,80},{128,96},{144,112}... | collective-permute-start | bytes 786440 | tf_op jit(solution)/shard_map/ppermute | solution.py:28
  149.3 17.2 %collective-permute-start.8 = (bf16[256,512]{1,0:T(8,128)(2,1)}, bf16[256,512]{1,0:T(8,128)(2,1)S(1)}, u32[]{:S(2)}, u32[]{:S(2)}) collective-permute-start(bf16[256,512]{1,0:T(8,128)(2,1)} %get-tuple-element.12), channel_id=1, source_target_pairs={{64,0},{80,16},{96,32},{112,48},{128,64},{144,80},{160,96},{176,11... | collective-permute-start | bytes 786440 | tf_op jit(solution)/shard_map/ppermute | solution.py:28
  152.6 25.9 %collective-permute-start.6 = (bf16[128,2048]{1,0:T(8,128)(2,1)S(1)}, bf16[128,2048]{1,0:T(8,128)(2,1)S(1)}, u32[]{:S(2)}, u32[]{:S(2)}) collective-permute-start(bf16[128,2048]{1,0:T(8,128)(2,1)S(1)} %get-tuple-element.14), channel_id=1, source_target_pairs={{0,16},{16,0},{32,48},{48,32},{64,80},{80,64},{96,112},{112,96},{1... | collective-permute-start | bytes 1572872 | tf_op jit(solution)/shard_map/ppermute | solution.py:33
  166.7 10.4 %collective-permute-start.9 = (bf16[128,512]{1,0:T(8,128)(2,1)S(1)}, bf16[128,512]{1,0:T(8,128)(2,1)S(1)}, u32[]{:S(2)}, u32[]{:S(2)}) collective-permute-start(bf16[128,512]{1,0:T(8,128)(2,1)S(1)} %get-tuple-element.20), channel_id=1, source_target_pairs={{0,16},{16,0},{32,48},{48,32},{64,80},{80,64},{96,112},{112,96},{1... | collective-permute-start | bytes 393224 | tf_op jit(solution)/shard_map/ppermute | solution.py:33
  173.4 3.1 %collective-permute-start.5 = (f32[16,128]{1,0:T(8,128)S(1)}, f32[16,128]{1,0:T(8,128)S(1)}, u32[]{:S(2)}, u32[]{:S(2)}) collective-permute-start(f32[16,128]{1,0:T(8,128)S(1)} %get-tuple-element.22), channel_id=1, source_target_pairs={{0,16},{16,0},{32,48},{48,32},{64,80},{80,64},{96,112},{112,96},{1... | collective-permute-start | bytes 24584 | tf_op jit(solution)/shard_map/ppermute | solution.py:33
Sparse Core Ops, SparseCore 0:
  10.6 89.6 all-gather.1

commit v2 on v1

--- a/solution.py
+++ b/solution.py
@@ -18,6 +18,9 @@
 HEADS = QH // KVH
 SPAN = 4 * BLOCK
 KEYS = SPAN + BLOCK
+SHARDS = 16
+SLICES = 16
+ROWS = 16
 SCALE = 1.0 / math.sqrt(HD)
 LOG2E = math.log2(math.e)
 
@@ -152,15 +155,110 @@
     )(starts, q, qt, u, ut, far, near, here)
 
 
+def projection_kernel(
+    place_ref, mine_ref, other_ref, own_ref, left_ref, right_ref, far_ref, out_ref, tokens, weight, sems
+):
+    core, a = place_ref[0], place_ref[1]
+    pieces = ((own_ref, 0), (left_ref, 3), (right_ref, 1), (far_ref, 2))
+
+    def copies(z):
+        return [
+            pltpu.make_async_copy(
+                ref.at[:, z], weight.at[z, pl.ds(lax.rem(a + turn, 4) * 4, 4)], sems.at[z, i]
+            )
+            for i, (ref, turn) in enumerate(pieces)
+        ]
+
+    for z in range(SHARDS):
+        for copy in copies(z):
+            copy.start()
+    mine = pl.multiple_of(core * BLOCK, BLOCK)
+    tokens[pl.ds(mine, BLOCK), :] = mine_ref[...]
+    tokens[pl.ds(BLOCK - mine, BLOCK), :] = other_ref[...]
+    total = jnp.zeros(out_ref.shape, jnp.float32)
+    for z in range(SHARDS):
+        for copy in copies(z):
+            copy.wait()
+        depth = SLICES * ROWS
+        total += jnp.dot(
+            tokens[:, z * depth : (z + 1) * depth],
+            weight[z].reshape(depth, out_ref.shape[1]),
+            preferred_element_type=jnp.float32,
+        )
+    out_ref[...] = total.astype(out_ref.dtype)
+
+
+def projection(place, mine, other, own, left, right, far):
+    width = own.shape[-1]
+    depth = mine.shape[1]
+    vmem = pl.BlockSpec(memory_space=pltpu.VMEM)
+    away = pl.BlockSpec(memory_space=pl.ANY)
+    return pl.pallas_call(
+        projection_kernel,
+        in_specs=[pl.BlockSpec(memory_space=pltpu.SMEM), vmem, vmem, away, away, away, away],
+        out_specs=vmem,
+        out_shape=jax.ShapeDtypeStruct((CHIP, width), jnp.bfloat16),
+        scratch_shapes=[
+            pltpu.VMEM((CHIP, depth), jnp.bfloat16),
+            pltpu.VMEM((SHARDS, SLICES, ROWS, width), jnp.bfloat16),
+            pltpu.SemaphoreType.DMA((SHARDS, 4)),
+        ],
+        compiler_params=pltpu.CompilerParams(vmem_limit_bytes=32 * 2**20),
+        cost_estimate=pl.CostEstimate(
+            flops=2 * CHIP * depth * width, bytes_accessed=6 * 2**20, transcendentals=0
+        ),
+        name="projection",
+    )(place, mine, other, own, left, right, far)
+
+
+def ring_of(core, x, y, turn, first):
+    if (core == 0) == first:
+        return x, (y + turn) % 4
+    return (x + turn) % 4, y
+
+
+def number(x, y, core):
+    return (x * 4 + y) * CORES + core
+
+
+def in_plane():
+    return [(x, y, core) for x in range(4) for y in range(4) for core in range(CORES)]
+
+
+def gathered(rows, device):
+    chip, core = device // CORES, device % CORES
+    x, y = chip // 4, chip % 4
+    a, b = jnp.where(core == 0, x, y), jnp.where(core == 0, y, x)
+    piece = lax.dynamic_slice_in_dim(rows, (a * 4 + b) * ROWS, ROWS, 0)
+    piece = jnp.broadcast_to(piece[None], (SHARDS,) + piece.shape)
+    piece = lax.all_to_all(piece, "fsdp", 0, 0)
+    groups = {}
+    for place in in_plane():
+        members = [number(*ring_of(place[2], *place[:2], turn, True), place[2]) for turn in range(4)]
+        groups[tuple(sorted(members))] = None
+    piece = jnp.broadcast_to(piece[None], (4,) + piece.shape)
+    own = lax.all_to_all(piece, "tok", 0, 0, axis_index_groups=[list(g) for g in groups])
+
+    def turned(turn):
+        route = [
+            (number(*place), number(*ring_of(place[2], *place[:2], turn, False), place[2]))
+            for place in in_plane()
+        ]
+        return lax.ppermute(own, "tok", route)
+
+    return a, own, turned(1), turned(-1), turned(2)
+
+
 def body(hidden, queries, upstream, context_weight, lengths):
     device = lax.axis_index("tok")
     core, chip = device % CORES, device // CORES
     ordered = context_weight.reshape(-1, 2, CORES, GROUPS, HD)
     ordered = lax.dynamic_slice_in_dim(ordered, core, 1, 2)[:, :, 0]
     ordered = ordered.transpose(0, 2, 1, 3).reshape(-1, GROUPS * 2 * HD)
-    weight = lax.all_gather(ordered, "fsdp", axis=0, tiled=True)
-
-    both = by_core(core, hidden, swapped(hidden), 0)
+    a, own, left, right, opposite = gathered(ordered, device)
+
+    hidden, queries, upstream, _ = lax.optimization_barrier((hidden, queries, upstream, own))
+    other_hidden = swapped(hidden)
 
     def heads_of(block):
         mine = half(block, core, 1)
@@ -176,8 +274,12 @@
     places = chip * CHIP + jnp.arange(CHIP, dtype=jnp.int32)
     starts = jnp.max(jnp.where(bounds[None, :] <= places[:, None], bounds[None, :], 0), axis=1)
     starts = (starts - chip * CHIP).astype(jnp.int32)[:, None]
-
-    here = jnp.dot(both, weight, preferred_element_type=jnp.float32).astype(jnp.bfloat16)
+    place = jnp.stack([core, a]).astype(jnp.int32)
+    place, q, qt, u, ut, starts, opposite = lax.optimization_barrier(
+        (place, q, qt, u, ut, starts, opposite)
+    )
+
+    here = projection(place, hidden, other_hidden, own, left, right, opposite)
     near = shifted(here, CORES)
     far = shifted(here, 2 * CORES)
     logs, dq, dfar, dnear, dhere = attention(starts, q, qt, u, ut, far, near, here)

time: 187 us -> 164 us (0.88)
  the two profiles are of different devices: /device:TPU:7 before, /device:TPU:19 now
where the time goes in v2:
time: 164 us; the launch traced here: 163 us
  starting transfers between devices  49.5 us (30%)
  waiting for transfers between devices  30.2 us (18%)
  blocking collectives  27.9 us (17%)
  local copies, waits for them, and re-layouts  25.2 us (15%)
  Pallas kernels  23.6 us (14%)
  other arithmetic  5.5 us (3%)
    all_to_all x1, blocking collectives, gathered(): piece = lax.all_to_all(piece, 'fsdp', 0, 0)  27.9 us
    ppermute x6, starting transfers between devices, swapped(): return lax.ppermute(block, 'tok', [(i, i ^ 1) for i in range(count)])  21.6 us
    ppermute x4, waiting for transfers between devices, shifted(): return lax.ppermute(block, 'tok', route)  19.2 us
    pallas_call x1, Pallas kernels, attention(): pl.pallas_call(attention_kernel, grid=(GROUPS, CORES), in_specs=[pl.Block...  18.4 us
    ppermute x4, starting transfers between devices, shifted(): return lax.ppermute(block, 'tok', route)  13.6 us
    ppermute x3, starting transfers between devices, turned(): return lax.ppermute(own, 'tok', route)  9.88 us
    unnamed x25, local copies, waits for them, and re-layouts  8.97 us
    all_to_all x1, waiting for transfers between devices, gathered(): lax.all_to_all(piece, 'tok', 0, 0, axis_index_groups=[list(g) for g in gr...  8.56 us
  transfers between devices with their start and end apart: 14, of which 6 were waited for; matrix products, arithmetic and copies ran while one was open for 12% of the time, Pallas kernels for 0%

profile of v2, /device:TPU:19, one launch (start us, length us, event | category | flops | bytes accessed | tf_op | source)
XLA Modules:
  0.0 162.9 jit_solution(15098258470549520850)
XLA Ops:
  0.7 1.2 copy.32
  2.0 0.1 constant_dynamic-slice_fusion.8
  2.1 0.1 copy.35
  2.3 27.9 %all_to_all.10 = bf16[16,16,512]{2,1,0:T(8,128)(2,1)S(1)} all-to-all(bf16[16,16,512]{2,1,0:T(8,128)(2,1)S(1)} %broadcast_in_dim.10), channel_id=1, replica_groups=mesh['tok'=32,'fsdp'=16] {'fsdp'}, dimensions={0} | all-to-all | bytes 524288 | tf_op jit(solution)/shard_map/all_to_all | solution.py:234
  30.1 1.1 broadcast_in_dim.11
  31.2 4.4 %all-to-all-start.1 = ((bf16[4,16,16,512]{3,2,1,0:T(8,128)(2,1)}), bf16[4,16,16,512]{3,2,1,0:T(8,128)(2,1)S(1)}, u32[]{:S(2)}, u32[]{:S(2)}) async-start(bf16[4,16,16,512]{3,2,1,0:T(8,128)(2,1)} %broadcast_in_dim.11), calls=%async_computation.1 | async-start | bytes 2097152 | tf_op jit(solution)/shard_map/all_to_all | solution.py:240
  35.6 8.6 %all-to-all-done.1.own_ref = bf16[4,16,16,512]{3,2,1,0:T(8,128)(2,1)S(1)} async-done(((bf16[4,16,16,512]{3,2,1,0:T(8,128)(2,1)}), bf16[4,16,16,512]{3,2,1,0:T(8,128)(2,1)S(1)}, u32[]{:S(2)}, u32[]{:S(2)}) %all-to-all-start.1) | async-done | bytes 1048608 | tf_op jit(solution)/shard_map/all_to_all | solution.py:240
  44.2 0.9 constant_dynamic-slice_fusion.5
  45.1 8.0 %collective-permute-start.1 = (bf16[128,2048]{1,0:T(8,128)(2,1)}, bf16[128,2048]{1,0:T(8,128)(2,1)S(1)}, u32[]{:S(2)}, u32[]{:S(2)}) collective-permute-start(bf16[128,2048]{1,0:T(8,128)(2,1)} %get-tuple-element.36), channel_id=1, source_target_pairs={{0,16},{16,0},{32,48},{48,32},{64,80},{80,64},{96,112},{112,96},{1... | collective-permute-start | bytes 1572872 | tf_op jit(solution)/shard_map/ppermute | solution.py:36
  53.0 4.6 %collective-permute-start.2 = (bf16[4,16,16,512]{3,2,1,0:T(8,128)(2,1)S(1)}, bf16[4,16,16,512]{3,2,1,0:T(8,128)(2,1)}, u32[]{:S(2)}, u32[]{:S(2)}) collective-permute-start(bf16[4,16,16,512]{3,2,1,0:T(8,128)(2,1)S(1)} %all-to-all-done.1.own_ref), channel_id=1, source_target_pairs={{0,256},{16,80},{32,288},{48,112},{64,320},{80,16},{96,352},{112,4... | collective-permute-start | bytes 3145736 | tf_op jit(solution)/shard_map/ppermute | solution.py:247
  57.6 1.9 %collective-permute-start.3 = (bf16[128,4096]{1,0:T(8,128)(2,1)}, bf16[128,4096]{1,0:T(8,128)(2,1)}, u32[]{:S(2)}, u32[]{:S(2)}) collective-permute-start(bf16[128,4096]{1,0:T(8,128)(2,1)} %mine_ref), channel_id=1, source_target_pairs={{0,16},{16,0},{32,48},{48,32},{64,80},{80,64},{96,112},{112,96},{1... | collective-permute-start | bytes 3145736 | tf_op jit(solution)/shard_map/ppermute | solution.py:36
  59.6 3.1 %collective-permute-start.4 = (bf16[4,16,16,512]{3,2,1,0:T(8,128)(2,1)S(1)}, bf16[4,16,16,512]{3,2,1,0:T(8,128)(2,1)}, u32[]{:S(2)}, u32[]{:S(2)}) collective-permute-start(bf16[4,16,16,512]{3,2,1,0:T(8,128)(2,1)S(1)} %all-to-all-done.1.own_ref), channel_id=1, source_target_pairs={{0,128},{16,48},{32,160},{48,80},{64,192},{80,112},{96,224},{112,1... | collective-permute-start | bytes 3145736 | tf_op jit(solution)/shard_map/ppermute | solution.py:247
  62.7 2.1 %collective-permute-start.5 = (bf16[4,16,16,512]{3,2,1,0:T(8,128)(2,1)S(1)}, bf16[4,16,16,512]{3,2,1,0:T(8,128)(2,1)}, u32[]{:S(2)}, u32[]{:S(2)}) collective-permute-start(bf16[4,16,16,512]{3,2,1,0:T(8,128)(2,1)S(1)} %all-to-all-done.1.own_ref), channel_id=1, source_target_pairs={{0,384},{16,112},{32,416},{48,16},{64,448},{80,48},{96,480},{112,8... | collective-permute-start | bytes 3145736 | tf_op jit(solution)/shard_map/ppermute | solution.py:247
  64.9 0.1 copy.40
  65.0 0.1 reduce
  65.1 1.3 constant_dynamic-slice_fusion.7
  66.4 0.0 collective-permute-done.1
  66.4 3.0 %collective-permute-start = (bf16[128,2048]{1,0:T(8,128)(2,1)S(1)}, bf16[128,2048]{1,0:T(8,128)(2,1)S(1)}, u32[]{:S(2)}, u32[]{:S(2)}) collective-permute-start(bf16[128,2048]{1,0:T(8,128)(2,1)S(1)} %get-tuple-element.38), channel_id=1, source_target_pairs={{0,16},{16,0},{32,48},{48,32},{64,80},{80,64},{96,112},{112,96},{1... | collective-permute-start | bytes 1572872 | tf_op jit(solution)/shard_map/ppermute | solution.py:36
  69.4 0.1 pad_add_fusion.place_ref
  69.5 0.1 select_reduce_fusion
  69.6 1.3 collective-permute-done
  70.9 2.9 %fusion = (bf16[32,8,16,128]{3,1,2,0:T(8,128)(2,1)}, bf16[32,8,16,128]{3,1,2,0:T(8,128)(2,1)S(1)}) fusion(bf16[128,2048]{1,0:T(8,128)(2,1)S(1)} %collective-permute-done, bf16[128,2048]{1,0:T(8,128)(2,1)S(1)} %get-tuple-element.37, pred[]{:T(512)S(6)} %eq.6, bf16[128,2048]{1,0:T(8,128)(2,1)S(1)} %get-tuple-element.35, bf16[128,2048]{1,0:T(8,128)(2,1)} %copy-done.9), kind=kLoop, calls=%fused_computation.1 | loop fusion | flops 9437184 | bytes 4194305
  73.8 0.2 copy.45
  74.0 2.0 %copy.39 = bf16[2,128,2,8,128]{1,3,4,2,0:T(8,128)(2,1)} copy(bf16[2,128,2,8,128]{4,3,2,1,0:T(8,128)(2,1)S(1)} %bitcast.38) | data formatting | bytes 2097152 | tf_op jit(solution)/shard_map/jit(_where)/select_n | solution.py:40
  76.0 0.3 copy.38
  76.3 0.9 copy-done.7
  77.2 1.2 copy.44
  78.4 2.9 %copy.37 = bf16[2,128,2,8,128]{1,3,4,2,0:T(8,128)(2,1)} copy(bf16[2,128,2,8,128]{4,3,2,1,0:T(8,128)(2,1)} %bitcast.22) | data formatting | bytes 2097152 | tf_op jit(solution)/shard_map/jit(_where)/select_n | solution.py:40
  81.3 1.5 copy.36
  82.8 2.3 %reshape.84.qt_ref = bf16[2,2,128,1024]{3,2,1,0:T(8,128)(2,1)} reshape(bf16[2,2,128,8,128]{4,3,2,1,0:T(8,128)(2,1)} %bitcast.41) | data formatting | bytes 2097152 | tf_op jit(solution)/shard_map/reshape | solution.py:268
  85.1 2.3 %reshape.86.ut_ref = bf16[2,2,128,1024]{3,2,1,0:T(8,128)(2,1)} reshape(bf16[2,2,128,8,128]{4,3,2,1,0:T(8,128)(2,1)} %bitcast.40) | data formatting | bytes 2097152 | tf_op jit(solution)/shard_map/reshape | solution.py:268
  87.5 0.0 collective-permute-done.2.far_ref
  87.5 0.0 collective-permute-done.3.other_ref
  87.5 0.0 collective-permute-done.4.left_ref
  87.5 0.0 collective-permute-done.5.right_ref
  87.5 5.2 %projection.1.here_ref = bf16[256,512]{1,0:T(8,128)(2,1)S(1)} custom-call(s32[2]{0:T(128)S(1)} %pad_add_fusion.place_ref, bf16[128,4096]{1,0:T(8,128)(2,1)} %mine_ref, bf16[128,4096]{1,0:T(8,128)(2,1)} %collective-permute-done.3.other_ref, bf16[4,16,16,512]{3,2,1,0:T(8,128)(2,1)S(1)} %all-to-all-done.1.own_ref, ...), custom_call_target="tpu_custom_call" | custom-call | flops 1073741824 | bytes 6291456 | tf_op jit(solution)/shard_map/projection/pallas_call | solution.py:196
  92.7 3.9 %collective-permute-start.6 = (bf16[256,512]{1,0:T(8,128)(2,1)S(1)}, bf16[256,512]{1,0:T(8,128)(2,1)S(1)}, u32[]{:S(2)}, u32[]{:S(2)}) collective-permute-start(bf16[256,512]{1,0:T(8,128)(2,1)S(1)} %projection.1.here_ref), channel_id=1, source_target_pairs={{0,64},{16,80},{32,96},{48,112},{64,128},{80,144},{96,160},{112,17... | collective-permute-start | bytes 786440 | tf_op jit(solution)/shard_map/ppermute | solution.py:31
  96.6 3.0 %collective-permute-start.7 = (bf16[256,512]{1,0:T(8,128)(2,1)S(1)}, bf16[256,512]{1,0:T(8,128)(2,1)S(1)}, u32[]{:S(2)}, u32[]{:S(2)}) collective-permute-start(bf16[256,512]{1,0:T(8,128)(2,1)S(1)} %projection.1.here_ref), channel_id=1, source_target_pairs={{0,32},{16,48},{32,64},{48,80},{64,96},{80,112},{96,128},{112,144}... | collective-permute-start | bytes 786440 | tf_op jit(solution)/shard_map/ppermute | solution.py:31
  99.5 0.1 copy.41.start_ref
  99.7 4.0 %collective-permute-done.6.far_ref = bf16[256,512]{1,0:T(8,128)(2,1)S(1)} collective-permute-done((bf16[256,512]{1,0:T(8,128)(2,1)S(1)}, bf16[256,512]{1,0:T(8,128)(2,1)S(1)}, u32[]{:S(2)}, u32[]{:S(2)}) %collective-permute-start.6) | collective-permute-done | bytes 262176 | tf_op jit(solution)/shard_map/ppermute | solution.py:31
  103.7 0.7 copy-done.3
  104.4 5.6 %collective-permute-done.7.near_ref = bf16[256,512]{1,0:T(8,128)(2,1)S(1)} collective-permute-done((bf16[256,512]{1,0:T(8,128)(2,1)S(1)}, bf16[256,512]{1,0:T(8,128)(2,1)S(1)}, u32[]{:S(2)}, u32[]{:S(2)}) %collective-permute-start.7) | collective-permute-done | bytes 262176 | tf_op jit(solution)/shard_map/ppermute | solution.py:31
  109.9 0.7 copy-done.5
  110.6 1.2 copy-done
  111.9 0.9 copy-done.4
  112.8 0.9 copy-done.6
  113.8 18.4 %attention.1 = (f32[2,16,128]{2,1,0:T(8,128)S(1)}, bf16[256,2048]{1,0:T(8,128)(2,1)S(1)}, bf16[256,512]{1,0:T(8,128)(2,1)}, bf16[256,512]{1,0:T(8,128)(2,1)}, f32[256,512]{1,0:T(8,128)S(1)}) custom-call(s32[256,1]{1,0:T(8,128)S(1)} %copy.41.start_ref, bf16[2,2,1024,128]{3,2,1,0:T(8,128)(2,1)S(1)} %bitcast.37, bf16[2,2,128,1024]{3,2,1,0:T(8,128)(2,1)S(1)} %copy-done, ...), custom_call_target="tpu_custom_call" | custom-call | flops 4026531840 | bytes 8388608 | tf_op jit(solution)/shard_map/attention/pallas_call | solution.py:121
  132.2 0.8 copy-done.1
  133.0 1.9 %collective-permute-start.10 = (bf16[256,512]{1,0:T(8,128)(2,1)}, bf16[256,512]{1,0:T(8,128)(2,1)S(1)}, u32[]{:S(2)}, u32[]{:S(2)}) collective-permute-start(bf16[256,512]{1,0:T(8,128)(2,1)} %get-tuple-element.31), channel_id=1, source_target_pairs={{32,0},{48,16},{64,32},{80,48},{96,64},{112,80},{128,96},{144,112}... | collective-permute-start | bytes 786440 | tf_op jit(solution)/shard_map/ppermute | solution.py:31
  134.9 4.9 %collective-permute-start.11 = (bf16[256,512]{1,0:T(8,128)(2,1)}, bf16[256,512]{1,0:T(8,128)(2,1)S(1)}, u32[]{:S(2)}, u32[]{:S(2)}) collective-permute-start(bf16[256,512]{1,0:T(8,128)(2,1)} %get-tuple-element.32), channel_id=1, source_target_pairs={{64,0},{80,16},{96,32},{112,48},{128,64},{144,80},{160,96},{176,11... | collective-permute-start | bytes 786440 | tf_op jit(solution)/shard_map/ppermute | solution.py:31
  139.8 0.0 copy-start.2
  139.8 0.1 constant_dynamic-slice_fusion.3
  139.9 3.6 %collective-permute-start.9 = (bf16[128,2048]{1,0:T(8,128)(2,1)S(1)}, bf16[128,2048]{1,0:T(8,128)(2,1)S(1)}, u32[]{:S(2)}, u32[]{:S(2)}) collective-permute-start(bf16[128,2048]{1,0:T(8,128)(2,1)S(1)} %get-tuple-element.34), channel_id=1, source_target_pairs={{0,16},{16,0},{32,48},{48,32},{64,80},{80,64},{96,112},{112,96},{1... | collective-permute-start | bytes 1572872 | tf_op jit(solution)/shard_map/ppermute | solution.py:36
  143.5 9.6 %collective-permute-done.11 = bf16[256,512]{1,0:T(8,128)(2,1)S(1)} collective-permute-done((bf16[256,512]{1,0:T(8,128)(2,1)}, bf16[256,512]{1,0:T(8,128)(2,1)S(1)}, u32[]{:S(2)}, u32[]{:S(2)}) %collective-permute-start.11) | collective-permute-done | bytes 262176 | tf_op jit(solution)/shard_map/ppermute | solution.py:31
  153.1 0.1 add_convert_fusion
  153.2 3.3 %collective-permute-start.12 = (bf16[128,512]{1,0:T(8,128)(2,1)S(1)}, bf16[128,512]{1,0:T(8,128)(2,1)S(1)}, u32[]{:S(2)}, u32[]{:S(2)}) collective-permute-start(bf16[128,512]{1,0:T(8,128)(2,1)S(1)} %get-tuple-element.40), channel_id=1, source_target_pairs={{0,16},{16,0},{32,48},{48,32},{64,80},{80,64},{96,112},{112,96},{1... | collective-permute-start | bytes 393224 | tf_op jit(solution)/shard_map/ppermute | solution.py:36
  156.5 1.9 %collective-permute-start.8 = (f32[16,128]{1,0:T(8,128)S(1)}, f32[16,128]{1,0:T(8,128)S(1)}, u32[]{:S(2)}, u32[]{:S(2)}) collective-permute-start(f32[16,128]{1,0:T(8,128)S(1)} %get-tuple-element.42), channel_id=1, source_target_pairs={{0,16},{16,0},{32,48},{48,32},{64,80},{80,64},{96,112},{112,96},{1... | collective-permute-start | bytes 24584 | tf_op jit(solution)/shard_map/ppermute | solution.py:36
  158.5 1.1 collective-permute-done.8
  159.6 0.6 maximum_select_fusion.3
  160.3 0.4 fusion.2
  160.7 0.1 copy.42
  160.8 0.9 reshape.89
  161.6 0.0 collective-permute-done.9
  161.6 1.2 maximum_select_fusion.2
  (26 shorter events, 0.3 us)
Async XLA Ops:
  31.2 13.0 %copy-start.8 = (bf16[128,4096]{1,0:T(8,128)(2,1)S(1)}, bf16[128,4096]{1,0:T(8,128)(2,1)}, u32[]{:S(2)}) copy-start(bf16[128,4096]{1,0:T(8,128)(2,1)} %param.7) | copy-start | bytes 3145732
  31.2 13.0 %all-to-all-start.1 = ((bf16[4,16,16,512]{3,2,1,0:T(8,128)(2,1)}), bf16[4,16,16,512]{3,2,1,0:T(8,128)(2,1)S(1)}, u32[]{:S(2)}, u32[]{:S(2)}) async-start(bf16[4,16,16,512]{3,2,1,0:T(8,128)(2,1)} %broadcast_in_dim.11), calls=%async_computation.1 | async-start | bytes 2097152 | tf_op jit(solution)/shard_map/all_to_all | solution.py:240
  35.6 29.3 %copy-start.10 = (s32[1,16]{1,0:T(1,128)S(1)}, s32[1,16]{1,0:T(1,128)}, u32[]{:S(2)}) copy-start(s32[1,16]{1,0:T(1,128)} %param.9) | copy-start | bytes 196
  45.1 21.3 %collective-permute-start.1 = (bf16[128,2048]{1,0:T(8,128)(2,1)}, bf16[128,2048]{1,0:T(8,128)(2,1)S(1)}, u32[]{:S(2)}, u32[]{:S(2)}) collective-permute-start(bf16[128,2048]{1,0:T(8,128)(2,1)} %get-tuple-element.36), channel_id=1, source_target_pairs={{0,16},{16,0},{32,48},{48,32},{64,80},{80,64},{96,112},{112,96},{1... | collective-permute-start | bytes 1572872 | tf_op jit(solution)/shard_map/ppermute | solution.py:36
  53.0 34.4 %collective-permute-start.2 = (bf16[4,16,16,512]{3,2,1,0:T(8,128)(2,1)S(1)}, bf16[4,16,16,512]{3,2,1,0:T(8,128)(2,1)}, u32[]{:S(2)}, u32[]{:S(2)}) collective-permute-start(bf16[4,16,16,512]{3,2,1,0:T(8,128)(2,1)S(1)} %all-to-all-done.1.own_ref), channel_id=1, source_target_pairs={{0,256},{16,80},{32,288},{48,112},{64,320},{80,16},{96,352},{112,4... | collective-permute-start | bytes 3145736 | tf_op jit(solution)/shard_map/ppermute | solution.py:247
  57.6 29.8 %collective-permute-start.3 = (bf16[128,4096]{1,0:T(8,128)(2,1)}, bf16[128,4096]{1,0:T(8,128)(2,1)}, u32[]{:S(2)}, u32[]{:S(2)}) collective-permute-start(bf16[128,4096]{1,0:T(8,128)(2,1)} %mine_ref), channel_id=1, source_target_pairs={{0,16},{16,0},{32,48},{48,32},{64,80},{80,64},{96,112},{112,96},{1... | collective-permute-start | bytes 3145736 | tf_op jit(solution)/shard_map/ppermute | solution.py:36
  59.6 27.9 %collective-permute-start.4 = (bf16[4,16,16,512]{3,2,1,0:T(8,128)(2,1)S(1)}, bf16[4,16,16,512]{3,2,1,0:T(8,128)(2,1)}, u32[]{:S(2)}, u32[]{:S(2)}) collective-permute-start(bf16[4,16,16,512]{3,2,1,0:T(8,128)(2,1)S(1)} %all-to-all-done.1.own_ref), channel_id=1, source_target_pairs={{0,128},{16,48},{32,160},{48,80},{64,192},{80,112},{96,224},{112,1... | collective-permute-start | bytes 3145736 | tf_op jit(solution)/shard_map/ppermute | solution.py:247
  62.7 24.8 %collective-permute-start.5 = (bf16[4,16,16,512]{3,2,1,0:T(8,128)(2,1)S(1)}, bf16[4,16,16,512]{3,2,1,0:T(8,128)(2,1)}, u32[]{:S(2)}, u32[]{:S(2)}) collective-permute-start(bf16[4,16,16,512]{3,2,1,0:T(8,128)(2,1)S(1)} %all-to-all-done.1.own_ref), channel_id=1, source_target_pairs={{0,384},{16,112},{32,416},{48,16},{64,448},{80,48},{96,480},{112,8... | collective-permute-start | bytes 3145736 | tf_op jit(solution)/shard_map/ppermute | solution.py:247
  66.4 4.5 %copy-start.9 = (bf16[128,2048]{1,0:T(8,128)(2,1)}, bf16[128,2048]{1,0:T(8,128)(2,1)S(1)}, u32[]{:S(2)}) copy-start(bf16[128,2048]{1,0:T(8,128)(2,1)S(1)} %collective-permute-done.1) | copy-start | bytes 1572868
  66.4 4.5 %collective-permute-start = (bf16[128,2048]{1,0:T(8,128)(2,1)S(1)}, bf16[128,2048]{1,0:T(8,128)(2,1)S(1)}, u32[]{:S(2)}, u32[]{:S(2)}) collective-permute-start(bf16[128,2048]{1,0:T(8,128)(2,1)S(1)} %get-tuple-element.38), channel_id=1, source_target_pairs={{0,16},{16,0},{32,48},{48,32},{64,80},{80,64},{96,112},{112,96},{1... | collective-permute-start | bytes 1572872 | tf_op jit(solution)/shard_map/ppermute | solution.py:36
  76.0 1.2 copy-start.7
  92.7 11.0 %collective-permute-start.6 = (bf16[256,512]{1,0:T(8,128)(2,1)S(1)}, bf16[256,512]{1,0:T(8,128)(2,1)S(1)}, u32[]{:S(2)}, u32[]{:S(2)}) collective-permute-start(bf16[256,512]{1,0:T(8,128)(2,1)S(1)} %projection.1.here_ref), channel_id=1, source_target_pairs={{0,64},{16,80},{32,96},{48,112},{64,128},{80,144},{96,160},{112,17... | collective-permute-start | bytes 786440 | tf_op jit(solution)/shard_map/ppermute | solution.py:31
  96.6 13.4 %collective-permute-start.7 = (bf16[256,512]{1,0:T(8,128)(2,1)S(1)}, bf16[256,512]{1,0:T(8,128)(2,1)S(1)}, u32[]{:S(2)}, u32[]{:S(2)}) collective-permute-start(bf16[256,512]{1,0:T(8,128)(2,1)S(1)} %projection.1.here_ref), channel_id=1, source_target_pairs={{0,32},{16,48},{32,64},{48,80},{64,96},{80,112},{96,128},{112,144}... | collective-permute-start | bytes 786440 | tf_op jit(solution)/shard_map/ppermute | solution.py:31
  103.7 0.7 copy-start.3
  109.9 0.7 copy-start.5
  110.6 1.2 copy-start
  111.9 0.9 copy-start.4
  112.8 0.9 copy-start.6
  132.2 0.8 copy-start.1
  133.0 10.5 %collective-permute-start.10 = (bf16[256,512]{1,0:T(8,128)(2,1)}, bf16[256,512]{1,0:T(8,128)(2,1)S(1)}, u32[]{:S(2)}, u32[]{:S(2)}) collective-permute-start(bf16[256,512]{1,0:T(8,128)(2,1)} %get-tuple-element.31), channel_id=1, source_target_pairs={{32,0},{48,16},{64,32},{80,48},{96,64},{112,80},{128,96},{144,112}... | collective-permute-start | bytes 786440 | tf_op jit(solution)/shard_map/ppermute | solution.py:31
  134.9 18.2 %collective-permute-start.11 = (bf16[256,512]{1,0:T(8,128)(2,1)}, bf16[256,512]{1,0:T(8,128)(2,1)S(1)}, u32[]{:S(2)}, u32[]{:S(2)}) collective-permute-start(bf16[256,512]{1,0:T(8,128)(2,1)} %get-tuple-element.32), channel_id=1, source_target_pairs={{64,0},{80,16},{96,32},{112,48},{128,64},{144,80},{160,96},{176,11... | collective-permute-start | bytes 786440 | tf_op jit(solution)/shard_map/ppermute | solution.py:31
  139.8 13.3 %copy-start.2 = (f32[256,512]{1,0:T(8,128)S(1)}, f32[256,512]{1,0:T(8,128)}, u32[]{:S(2)}) copy-start(f32[256,512]{1,0:T(8,128)} %copy-done.1) | copy-start | bytes 1572868
  139.9 21.7 %collective-permute-start.9 = (bf16[128,2048]{1,0:T(8,128)(2,1)S(1)}, bf16[128,2048]{1,0:T(8,128)(2,1)S(1)}, u32[]{:S(2)}, u32[]{:S(2)}) collective-permute-start(bf16[128,2048]{1,0:T(8,128)(2,1)S(1)} %get-tuple-element.34), channel_id=1, source_target_pairs={{0,16},{16,0},{32,48},{48,32},{64,80},{80,64},{96,112},{112,96},{1... | collective-permute-start | bytes 1572872 | tf_op jit(solution)/shard_map/ppermute | solution.py:36
  153.2 7.0 %collective-permute-start.12 = (bf16[128,512]{1,0:T(8,128)(2,1)S(1)}, bf16[128,512]{1,0:T(8,128)(2,1)S(1)}, u32[]{:S(2)}, u32[]{:S(2)}) collective-permute-start(bf16[128,512]{1,0:T(8,128)(2,1)S(1)} %get-tuple-element.40), channel_id=1, source_target_pairs={{0,16},{16,0},{32,48},{48,32},{64,80},{80,64},{96,112},{112,96},{1... | collective-permute-start | bytes 393224 | tf_op jit(solution)/shard_map/ppermute | solution.py:36
  156.5 3.1 %collective-permute-start.8 = (f32[16,128]{1,0:T(8,128)S(1)}, f32[16,128]{1,0:T(8,128)S(1)}, u32[]{:S(2)}, u32[]{:S(2)}) collective-permute-start(f32[16,128]{1,0:T(8,128)S(1)} %get-tuple-element.42), channel_id=1, source_target_pairs={{0,16},{16,0},{32,48},{48,32},{64,80},{80,64},{96,112},{112,96},{1... | collective-permute-start | bytes 24584 | tf_op jit(solution)/shard_map/ppermute | solution.py:36

commit v3 on v2

v3 whole, which is shorter than its diff:
```python
import functools
import math

import jax
import jax.numpy as jnp
from jax import lax
from jax.experimental import pallas as pl
from jax.experimental.pallas import tpu as pltpu
from jax.sharding import PartitionSpec as P

QH = 32
KVH = 4
HD = 128
CORES = 2
BLOCK = 128
CHIP = CORES * BLOCK
GROUPS = KVH // CORES
HEADS = QH // KVH
DOCS = 16
LENGTHS = 3
SPAN = 4 * BLOCK
KEYS = SPAN + BLOCK
SHARDS = 16
SLICES = 16
ROWS = 16
SCALE = 1.0 / math.sqrt(HD)
LOG2E = math.log2(math.e)


def shifted(block, distance, across=False):
    count = lax.axis_size("tok")
    route = [(i, i + distance) for i in range(count) if 0 <= i + distance < count]
    if across:
        route = [(i, j ^ 1) for i, j in route]
    return lax.ppermute(block, "tok", route)


def swapped(block):
    count = lax.axis_size("tok")
    return lax.ppermute(block, "tok", [(i, i ^ 1) for i in range(count)])


def half(block, index, axis):
    size = block.shape[axis] // 2
    return lax.dynamic_slice_in_dim(block, index * size, size, axis)


def attention_kernel(
    place_ref, q_mine, q_other, u_mine, u_other, far_ref, near_ref, here_ref,
    log_mine, dq_mine, to_core, here_mine, near_mine, near_other, far_mine, far_other,
    keys, values, sums, bias, q_rows, u_rows, weight_rows, change_rows,
):
    group, part = pl.program_id(0), pl.program_id(1)
    core, chip = place_ref[0], place_ref[1]
    first = pl.multiple_of(jnp.where(part == 0, core, 1 - core) * BLOCK, BLOCK)

    def stack(q_ref, u_ref):
        for head in range(HEADS):
            rows, columns = slice(head * BLOCK, (head + 1) * BLOCK), slice(head * HD, (head + 1) * HD)
            q_rows[rows, :] = q_ref[:, columns]
            u_rows[rows, :] = u_ref[:, columns]

    @pl.when(part == 0)
    def _():
        for i, ref in enumerate((far_ref, near_ref, here_ref)):
            keys[i * CHIP : (i + 1) * CHIP, :] = ref[:, :HD]
            values[i * CHIP : (i + 1) * CHIP, :] = ref[:, HD:]
        sums[...] = jnp.zeros_like(sums)
        stack(q_mine, u_mine)

    @pl.when(part == 1)
    def _():
        stack(q_other, u_other)

    key_window = keys[pl.ds(first, KEYS), :]
    value_window = values[pl.ds(first, KEYS), :]
    places = first - SPAN + lax.broadcasted_iota(jnp.int32, (BLOCK, KEYS), 1)
    own = first + lax.broadcasted_iota(jnp.int32, (BLOCK, KEYS), 0)
    token = first + lax.broadcasted_iota(jnp.int32, (BLOCK, 1), 0)
    start, bound = jnp.zeros((BLOCK, 1), jnp.int32) - chip * CHIP, -chip * CHIP
    for i in range(DOCS):
        bound = bound + place_ref[LENGTHS + i]
        start = jnp.where(token >= bound, bound, start)
    bias[...] = jnp.where((places <= own) & (places >= start), 0.0, -jnp.inf)
    over_rows = (((1,), (1,)), ((), ()))
    dot = functools.partial(jnp.dot, preferred_element_type=jnp.float32)
    dot_rows = functools.partial(
        lax.dot_general, dimension_numbers=over_rows, preferred_element_type=jnp.float32
    )
    count = HEADS // 2
    stripes = [slice(i * count * BLOCK, (i + 1) * count * BLOCK) for i in range(2)]
    scores = [dot_rows(q_rows[rows, :], key_window) for rows in stripes]
    pushed = [dot_rows(u_rows[rows, :], value_window) for rows in stripes]
    weights, logs, attended = [], [], []
    for i, rows in enumerate(stripes):
        masked = scores[i].reshape(count, BLOCK, KEYS) + bias[...][None]
        masked = masked.reshape(count * BLOCK, KEYS)
        highest = jnp.max(masked, axis=1, keepdims=True)
        raised = jnp.exp2((masked - highest) * (SCALE * LOG2E))
        total = jnp.sum(raised, axis=1, keepdims=True)
        logs.append(highest * SCALE + jnp.log(total))
        weights.append(raised * (1.0 / total))
        weight_rows[rows, :] = weights[i].astype(jnp.bfloat16)
        attended.append(dot(weights[i].astype(jnp.bfloat16), value_window).astype(jnp.bfloat16))
    value_slope, key_slope = [], []
    for i, rows in enumerate(stripes):
        product = u_rows[rows, :].astype(jnp.float32) * attended[i].astype(jnp.float32)
        inner = jnp.sum(product, axis=1, keepdims=True)
        change_rows[rows, :] = (weights[i] * (pushed[i] - inner)).astype(jnp.bfloat16)
        value_slope.append(dot(u_rows[rows, :].T, weight_rows[rows, :]))
    slopes = [dot(change_rows[rows, :], key_window) * SCALE for rows in stripes]
    for rows in stripes:
        key_slope.append(dot(q_rows[rows, :].T, change_rows[rows, :]))
    sums[pl.ds(first, KEYS), :HD] += (key_slope[0] + key_slope[1]).T * SCALE
    sums[pl.ds(first, KEYS), HD:] += (value_slope[0] + value_slope[1]).T
    lane = lax.broadcasted_iota(jnp.int32, (BLOCK, HD), 1)
    columns = jnp.zeros((BLOCK, HD), jnp.float32)
    for head in range(HEADS):
        rows = slice(head % count * BLOCK, (head % count + 1) * BLOCK)
        columns = jnp.where(lane % HEADS == head, logs[head // count][rows], columns)

    def head_slope(head):
        rows = slice(head % count * BLOCK, (head % count + 1) * BLOCK)
        return slopes[head // count][rows].astype(jnp.bfloat16)

    @pl.when(part == 0)
    def _():
        log_mine[...] = columns.T[:HEADS]
        for head in range(HEADS):
            dq_mine[:, head * HD : (head + 1) * HD] = head_slope(head)

    @pl.when(part == 1)
    def _():
        high = columns.astype(jnp.bfloat16).astype(jnp.float32)
        middle = (columns - high).astype(jnp.bfloat16).astype(jnp.float32)
        terms = jnp.where(lane < HEADS, high, jnp.where(lane < 2 * HEADS, middle, columns - high - middle))
        mine = pl.multiple_of(core * BLOCK, BLOCK)
        others = pl.multiple_of(BLOCK - mine, BLOCK)

        def rows_of(first, which):
            return sums[pl.ds(first + which, BLOCK), :]

        here_mine[...] = rows_of(SPAN, mine)
        near_mine[...] = rows_of(CHIP, mine).astype(jnp.bfloat16)
        near_other[...] = rows_of(CHIP, others).astype(jnp.bfloat16)
        far_mine[...] = rows_of(0, mine).astype(jnp.bfloat16)
        far_other[...] = rows_of(0, others).astype(jnp.bfloat16)
        here_other = rows_of(SPAN, others).astype(jnp.bfloat16)
        for g in range(GROUPS):

            @pl.when(group == g)
            def _():
                for head in range(HEADS):
                    at = (g * HEADS + head) * HD
                    to_core[:, at : at + HD] = head_slope(head)
                at = GROUPS * HEADS * HD + g * 3 * HD
                to_core[:, at : at + 2 * HD] = here_other
                to_core[:, at + 2 * HD : at + 3 * HD] = terms.astype(jnp.bfloat16)


def attention(place, queries, q_other, upstream, u_other, far, near, here):
    stacked = HEADS * BLOCK
    mine = pl.BlockSpec((BLOCK, HEADS * HD), lambda g, b, place: (0, place[0] * GROUPS + g))
    other = pl.BlockSpec((BLOCK, HEADS * HD), lambda g, b, place: (0, g))
    context = pl.BlockSpec((CHIP, 2 * HD), lambda g, b, place: (0, g))
    block = pl.BlockSpec((BLOCK, 2 * HD), lambda g, b, place: (0, g))
    log = pl.BlockSpec((HEADS, BLOCK), lambda g, b, place: (g, 0))
    wide, packed, heads = GROUPS * 2 * HD, GROUPS * 3 * HD, GROUPS * HEADS
    term = jax.ShapeDtypeStruct((BLOCK, wide), jnp.bfloat16)
    return pl.pallas_call(
        attention_kernel,
        grid_spec=pltpu.PrefetchScalarGridSpec(
            num_scalar_prefetch=1,
            grid=(GROUPS, CORES),
            in_specs=[
                mine, other, mine, other, context, context, context,
            ],
            out_specs=[
                log, other,
                pl.BlockSpec((BLOCK, heads * HD + packed), lambda g, b, place: (0, 0)),
                block, block, block, block, block,
            ],
            scratch_shapes=[
                pltpu.VMEM((SPAN + CHIP, HD), jnp.bfloat16),
                pltpu.VMEM((SPAN + CHIP, HD), jnp.bfloat16),
                pltpu.VMEM((SPAN + CHIP, 2 * HD), jnp.float32),
                pltpu.VMEM((BLOCK, KEYS), jnp.float32),
                pltpu.VMEM((stacked, HD), jnp.bfloat16),
                pltpu.VMEM((stacked, HD), jnp.bfloat16),
                pltpu.VMEM((stacked, KEYS), jnp.bfloat16),
                pltpu.VMEM((stacked, KEYS), jnp.bfloat16),
            ],
        ),
        out_shape=[
            jax.ShapeDtypeStruct((heads, BLOCK), jnp.float32),
            jax.ShapeDtypeStruct((BLOCK, heads * HD), jnp.bfloat16),
            jax.ShapeDtypeStruct((BLOCK, heads * HD + packed), jnp.bfloat16),
            jax.ShapeDtypeStruct((BLOCK, wide), jnp.float32),
            term, term, term, term,
        ],
        compiler_params=pltpu.CompilerParams(vmem_limit_bytes=48 * 2**20),
        cost_estimate=pl.CostEstimate(
            flops=12 * CHIP * KEYS * HD * GROUPS * HEADS,
            bytes_accessed=8 * 2**20,
            transcendentals=CHIP * KEYS * GROUPS * HEADS,
        ),
        name="attention",
    )(place, queries, q_other, upstream, u_other, far, near, here)


def finish_kernel(
    place_ref, dq_mine, from_core, log_mine, here_mine, near_mine, far_mine, near_other, far_other,
    log_ref, dq_ref, context_ref,
):
    width, heads = dq_mine.shape[1], log_mine.shape[0]

    def put(which, dq, log, slopes):
        dq_ref[:, which * width : (which + 1) * width] = dq
        for g in range(GROUPS):
            row = which * heads + g * HEADS
            log_ref[row : row + HEADS, :] = log[g]
            for kind in range(2):
                to = (kind * KVH + which * GROUPS + g) * HD
                context_ref[:, to : to + HD] = slopes[g][:, kind * HD : (kind + 1) * HD]

    def total(here, near, far, g):
        at = slice(g * 2 * HD, (g + 1) * 2 * HD)
        terms = here + near[:, at].astype(jnp.float32) + far[:, at].astype(jnp.float32)
        return terms.astype(jnp.bfloat16)

    mine, other, logs = [], [], []
    for g in range(GROUPS):
        at = width + g * 3 * HD
        mine.append(total(here_mine[:, g * 2 * HD : (g + 1) * 2 * HD], near_mine, far_mine, g))
        here = from_core[:, at : at + 2 * HD].astype(jnp.float32)
        other.append(total(here, near_other, far_other, g))
        terms = from_core[:, at + 2 * HD : at + 3 * HD].astype(jnp.float32).T
        logs.append(terms[:HEADS] + terms[HEADS : 2 * HEADS] + terms[2 * HEADS : 3 * HEADS])
    own_logs = [log_mine[g * HEADS : (g + 1) * HEADS, :] for g in range(GROUPS)]
    for core in range(CORES):

        @pl.when(place_ref[0] == core)
        def _():
            put(core, dq_mine[...], own_logs, mine)
            put(1 - core, from_core[:, :width], logs, other)


def finish(place, *terms):
    vmem = pl.BlockSpec(memory_space=pltpu.VMEM)
    return pl.pallas_call(
        finish_kernel,
        in_specs=[pl.BlockSpec(memory_space=pltpu.SMEM)] + [vmem] * len(terms),
        out_specs=[vmem] * 3,
        out_shape=[
            jax.ShapeDtypeStruct((QH, BLOCK), jnp.float32),
            jax.ShapeDtypeStruct((BLOCK, QH * HD), jnp.bfloat16),
            jax.ShapeDtypeStruct((BLOCK, 2 * KVH * HD), jnp.bfloat16),
        ],
        compiler_params=pltpu.CompilerParams(vmem_limit_bytes=32 * 2**20),
        cost_estimate=pl.CostEstimate(flops=0, bytes_accessed=4 * 2**20, transcendentals=0),
        name="finish",
    )(place, *terms)


def projection_kernel(
    place_ref, mine_ref, other_ref, own_ref, left_ref, right_ref, far_ref, out_ref, tokens, weight, sems
):
    core, a = place_ref[0], place_ref[2]
    pieces = ((own_ref, 0), (left_ref, 3), (right_ref, 1), (far_ref, 2))

    copies = [
        pltpu.make_async_copy(
            ref.at[b], weight.at[lax.rem(a + turn, 4) * 4 + b], sems.at[i, b]
        )
        for i, (ref, turn) in enumerate(pieces)
        for b in range(4)
    ]
    for copy in copies:
        copy.start()
    mine = pl.multiple_of(core * BLOCK, BLOCK)
    tokens[pl.ds(mine, BLOCK), :] = mine_ref[...]
    tokens[pl.ds(BLOCK - mine, BLOCK), :] = other_ref[...]
    for copy in copies:
        copy.wait()
    total = jnp.zeros(out_ref.shape, jnp.float32)
    depth = SLICES * ROWS
    for z in range(SHARDS):
        total += jnp.dot(
            tokens[:, z * depth : (z + 1) * depth],
            weight[:, z].reshape(depth, out_ref.shape[1]),
            preferred_element_type=jnp.float32,
        )
    out_ref[...] = total.astype(out_ref.dtype)


def projection(place, mine, other, own, left, right, far):
    width = own.shape[-1]
    depth = mine.shape[1]
    vmem = pl.BlockSpec(memory_space=pltpu.VMEM)
    away = pl.BlockSpec(memory_space=pl.ANY)
    return pl.pallas_call(
        projection_kernel,
        in_specs=[pl.BlockSpec(memory_space=pltpu.SMEM), vmem, vmem, away, away, away, away],
        out_specs=vmem,
        out_shape=jax.ShapeDtypeStruct((CHIP, width), jnp.bfloat16),
        scratch_shapes=[
            pltpu.VMEM((CHIP, depth), jnp.bfloat16),
            pltpu.VMEM((SLICES, SHARDS, ROWS, width), jnp.bfloat16),
            pltpu.SemaphoreType.DMA((4, 4)),
        ],
        compiler_params=pltpu.CompilerParams(vmem_limit_bytes=32 * 2**20),
        cost_estimate=pl.CostEstimate(
            flops=2 * CHIP * depth * width, bytes_accessed=6 * 2**20, transcendentals=0
        ),
        name="projection",
    )(place, mine, other, own, left, right, far)


def ring_of(core, x, y, turn, first):
    if (core == 0) == first:
        return x, (y + turn) % 4
    return (x + turn) % 4, y


def number(x, y, core):
    return (x * 4 + y) * CORES + core


def in_plane():
    return [(x, y, core) for x in range(4) for y in range(4) for core in range(CORES)]


def gathered(rows, device):
    chip, core = device // CORES, device % CORES
    x, y = chip // 4, chip % 4
    a, b = jnp.where(core == 0, x, y), jnp.where(core == 0, y, x)
    piece = lax.dynamic_slice_in_dim(rows, (a * 4 + b) * ROWS, ROWS, 0)
    piece = jnp.broadcast_to(piece[None], (SHARDS,) + piece.shape)
    piece = lax.all_to_all(piece, "fsdp", 0, 0)
    groups = {}
    for place in in_plane():
        members = [number(*ring_of(place[2], *place[:2], turn, True), place[2]) for turn in range(4)]
        groups[tuple(sorted(members))] = None
    piece = jnp.broadcast_to(piece[None], (4,) + piece.shape)
    own = lax.all_to_all(piece, "tok", 0, 0, axis_index_groups=[list(g) for g in groups])

    def turned(turn):
        route = [
            (number(*place), number(*ring_of(place[2], *place[:2], turn, False), place[2]))
            for place in in_plane()
        ]
        return lax.ppermute(own, "tok", route)

    return a, own, turned(1), turned(-1), turned(2)


def body(hidden, queries, upstream, context_weight, lengths):
    device = lax.axis_index("tok")
    core, chip = device % CORES, device // CORES
    ordered = context_weight.reshape(-1, 2, CORES, GROUPS, HD)
    ordered = lax.dynamic_slice_in_dim(ordered, core, 1, 2)[:, :, 0]
    ordered = ordered.transpose(0, 2, 1, 3).reshape(-1, GROUPS * 2 * HD)
    a, own, left, right, opposite = gathered(ordered, device)

    hidden, queries, upstream, _ = lax.optimization_barrier((hidden, queries, upstream, own))
    other_hidden = swapped(hidden)
    q_other = swapped(half(queries, 1 - core, 1))
    u_other = swapped(half(upstream, 1 - core, 1))
    place = jnp.concatenate([jnp.stack([core, chip, a]).astype(jnp.int32), lengths[0]])
    place, q_other, u_other, opposite = lax.optimization_barrier((place, q_other, u_other, opposite))

    here = projection(place, hidden, other_hidden, own, left, right, opposite)
    near = shifted(here, CORES)
    far = shifted(here, 2 * CORES)
    (
        log_mine, dq_mine, to_core, here_mine, near_mine, near_other, far_mine, far_other,
    ) = attention(place, queries, q_other, upstream, u_other, far, near, here)
    far_mine, far_other = shifted(far_mine, -2 * CORES), shifted(far_other, -2 * CORES, True)
    near_mine, near_other = shifted(near_mine, -CORES), shifted(near_other, -CORES, True)
    from_core = swapped(to_core)
    return tuple(
        finish(
            place, dq_mine, from_core, log_mine, here_mine, near_mine, far_mine, near_other, far_other
        )
    )


def solution(mesh):
    in_specs = (
        P(("fsdp", "tok"), None),
        P(("fsdp", "tok"), None),
        P(("fsdp", "tok"), None),
        P("fsdp", None),
        P("fsdp", None),
    )
    out_specs = (P(None, ("fsdp", "tok")), P(("fsdp", "tok"), None), P(("fsdp", "tok"), None))
    return jax.shard_map(body, mesh=mesh, in_specs=in_specs, out_specs=out_specs, check_vma=False)
```

time: 164 us -> 140 us (0.85)
  the two profiles are of different devices: /device:TPU:19 before, /device:TPU:7 now
where the time goes in v3:
time: 140 us; the launch traced here: 139 us
  starting transfers between devices  50.2 us (36%)
  waiting for transfers between devices  39.1 us (28%)
  blocking collectives  27.9 us (20%)
  Pallas kernels  16.8 us (12%)
  local copies, waits for them, and re-layouts  4.39 us (3%)
    all_to_all x1, blocking collectives, gathered(): piece = lax.all_to_all(piece, 'fsdp', 0, 0)  27.9 us
    ppermute x4, starting transfers between devices, swapped(): return lax.ppermute(block, 'tok', [(i, i ^ 1) for i in range(count)])  20 us
    ppermute x6, waiting for transfers between devices, shifted(): return lax.ppermute(block, 'tok', route)  18.1 us
    ppermute x6, starting transfers between devices, shifted(): return lax.ppermute(block, 'tok', route)  17.2 us
    pallas_call x1, Pallas kernels, attention(): pl.pallas_call(attention_kernel, grid_spec=pltpu.PrefetchScalarGridSpec(n...  12.6 us
    ppermute x3, waiting for transfers between devices, turned(): return lax.ppermute(own, 'tok', route)  11.9 us
    ppermute x3, starting transfers between devices, turned(): return lax.ppermute(own, 'tok', route)  8.68 us
    all_to_all x1, waiting for transfers between devices, gathered(): lax.all_to_all(piece, 'tok', 0, 0, axis_index_groups=[list(g) for g in gr...  7.95 us
  transfers between devices with their start and end apart: 14, of which 8 were waited for; matrix products, arithmetic and copies ran while one was open for 1% of the time, Pallas kernels for 0%

profile of v3, /device:TPU:7, one launch (start us, length us, event | category | flops | bytes accessed | tf_op | source)
XLA Modules:
  0.0 139.4 jit_solution(7859100171613035463)
XLA Ops:
  0.7 1.2 copy.8
  2.0 0.1 constant_dynamic-slice_fusion.2
  2.1 0.1 copy.11
  2.2 27.9 %all_to_all.10 = bf16[16,16,512]{2,1,0:T(8,128)(2,1)S(1)} all-to-all(bf16[16,16,512]{2,1,0:T(8,128)(2,1)S(1)} %broadcast_in_dim.4), channel_id=1, replica_groups=mesh['tok'=32,'fsdp'=16] {'fsdp'}, dimensions={0} | all-to-all | bytes 524288 | tf_op jit(solution)/shard_map/all_to_all | solution.py:339
  30.1 1.1 broadcast_in_dim.5
  31.2 0.0 copy-start.1
  31.2 4.3 %all-to-all-start.1 = ((bf16[4,16,16,512]{3,2,1,0:T(8,128)(2,1)}), bf16[4,16,16,512]{3,2,1,0:T(8,128)(2,1)S(1)}, u32[]{:S(2)}, u32[]{:S(2)}) async-start(bf16[4,16,16,512]{3,2,1,0:T(8,128)(2,1)} %broadcast_in_dim.5), calls=%async_computation.1 | async-start | bytes 2097152 | tf_op jit(solution)/shard_map/all_to_all | solution.py:345
  35.5 0.0 copy-start
  35.5 8.0 %all-to-all-done.1.own_ref = bf16[4,16,16,512]{3,2,1,0:T(8,128)(2,1)S(1)} async-done(((bf16[4,16,16,512]{3,2,1,0:T(8,128)(2,1)}), bf16[4,16,16,512]{3,2,1,0:T(8,128)(2,1)S(1)}, u32[]{:S(2)}, u32[]{:S(2)}) %all-to-all-start.1) | async-done | bytes 1048608 | tf_op jit(solution)/shard_map/all_to_all | solution.py:345
  43.5 0.0 copy-done.1
  43.5 11.3 %collective-permute-start = (bf16[128,2048]{1,0:T(8,128)(2,1)S(1)}, bf16[128,2048]{1,0:T(8,128)(2,1)S(1)}, u32[]{:S(2)}, u32[]{:S(2)}) collective-permute-start(bf16[128,2048]{1,0:T(8,128)(2,1)S(1)} %constant_dynamic-slice_fusion.1), channel_id=1, source_target_pairs={{0,16},{16,0},{32,48},{48,32},{64,80},{80,64},{96,112},{112,96},{1... | collective-permute-start | bytes 1572872 | tf_op jit(solution)/shard_map/ppermute | solution.py:40
  54.8 2.2 %collective-permute-start.2 = (bf16[4,16,16,512]{3,2,1,0:T(8,128)(2,1)S(1)}, bf16[4,16,16,512]{3,2,1,0:T(8,128)(2,1)S(1)}, u32[]{:S(2)}, u32[]{:S(2)}) collective-permute-start(bf16[4,16,16,512]{3,2,1,0:T(8,128)(2,1)S(1)} %all-to-all-done.1.own_ref), channel_id=1, source_target_pairs={{0,256},{16,80},{32,288},{48,112},{64,320},{80,16},{96,352},{112,4... | collective-permute-start | bytes 3145736 | tf_op jit(solution)/shard_map/ppermute | solution.py:352
  57.0 0.0 copy-done
  57.0 3.0 %collective-permute-start.3 = (bf16[128,4096]{1,0:T(8,128)(2,1)S(1)}, bf16[128,4096]{1,0:T(8,128)(2,1)S(1)}, u32[]{:S(2)}, u32[]{:S(2)}) collective-permute-start(bf16[128,4096]{1,0:T(8,128)(2,1)S(1)} %copy-done), channel_id=1, source_target_pairs={{0,16},{16,0},{32,48},{48,32},{64,80},{80,64},{96,112},{112,96},{1... | collective-permute-start | bytes 3145736 | tf_op jit(solution)/shard_map/ppermute | solution.py:40
  60.1 2.2 %collective-permute-start.4 = (bf16[4,16,16,512]{3,2,1,0:T(8,128)(2,1)S(1)}, bf16[4,16,16,512]{3,2,1,0:T(8,128)(2,1)S(1)}, u32[]{:S(2)}, u32[]{:S(2)}) collective-permute-start(bf16[4,16,16,512]{3,2,1,0:T(8,128)(2,1)S(1)} %all-to-all-done.1.own_ref), channel_id=1, source_target_pairs={{0,128},{16,48},{32,160},{48,80},{64,192},{80,112},{96,224},{112,1... | collective-permute-start | bytes 3145736 | tf_op jit(solution)/shard_map/ppermute | solution.py:352
  62.3 4.3 %collective-permute-start.5 = (bf16[4,16,16,512]{3,2,1,0:T(8,128)(2,1)S(1)}, bf16[4,16,16,512]{3,2,1,0:T(8,128)(2,1)S(1)}, u32[]{:S(2)}, u32[]{:S(2)}) collective-permute-start(bf16[4,16,16,512]{3,2,1,0:T(8,128)(2,1)S(1)} %all-to-all-done.1.own_ref), channel_id=1, source_target_pairs={{0,384},{16,112},{32,416},{48,16},{64,448},{80,48},{96,480},{112,8... | collective-permute-start | bytes 3145736 | tf_op jit(solution)/shard_map/ppermute | solution.py:352
  66.6 1.1 constant_dynamic-slice_fusion
  67.7 0.0 collective-permute-done.q_other
  67.7 1.9 %collective-permute-start.1 = (bf16[128,2048]{1,0:T(8,128)(2,1)S(1)}, bf16[128,2048]{1,0:T(8,128)(2,1)S(1)}, u32[]{:S(2)}, u32[]{:S(2)}) collective-permute-start(bf16[128,2048]{1,0:T(8,128)(2,1)S(1)} %constant_dynamic-slice_fusion), channel_id=1, source_target_pairs={{0,16},{16,0},{32,48},{48,32},{64,80},{80,64},{96,112},{112,96},{1... | collective-permute-start | bytes 1572872 | tf_op jit(solution)/shard_map/ppermute | solution.py:40
  69.6 0.0 copy-start.3
  69.7 0.6 copy-done.3
  70.3 0.1 pad_add_fusion.place_ref
  70.4 0.0 copy-start.2
  70.4 1.1 collective-permute-done.1.u_other
  71.5 0.7 collective-permute-done.2.far_ref
  72.2 0.0 collective-permute-done.3.other_ref
  72.2 11.2 %collective-permute-done.4.left_ref = bf16[4,16,16,512]{3,2,1,0:T(8,128)(2,1)S(1)} collective-permute-done((bf16[4,16,16,512]{3,2,1,0:T(8,128)(2,1)S(1)}, bf16[4,16,16,512]{3,2,1,0:T(8,128)(2,1)S(1)}, u32[]{:S(2)}, u32[]{:S(2)}) %collective-permute-start.4) | collective-permute-done | bytes 1048608 | tf_op jit(solution)/shard_map/ppermute | solution.py:352
  83.4 0.0 collective-permute-done.5.right_ref
  83.4 2.4 %projection.1.here_ref = bf16[256,512]{1,0:T(8,128)(2,1)S(1)} custom-call(s32[19]{0:T(128)S(1)} %pad_add_fusion.place_ref, bf16[128,4096]{1,0:T(8,128)(2,1)S(1)} %copy-done, bf16[128,4096]{1,0:T(8,128)(2,1)S(1)} %collective-permute-done.3.other_ref, bf16[4,16,16,512]{3,2,1,0:T(8,128)(2,1)S(1)} %all-to-all-done.1.own_ref, ...), custom_call_target="tpu_custom_call" | custom-call | flops 1073741824 | bytes 6291456 | tf_op jit(solution)/shard_map/projection/pallas_call | solution.py:301
  85.8 2.7 %collective-permute-start.6 = (bf16[256,512]{1,0:T(8,128)(2,1)S(1)}, bf16[256,512]{1,0:T(8,128)(2,1)S(1)}, u32[]{:S(2)}, u32[]{:S(2)}) collective-permute-start(bf16[256,512]{1,0:T(8,128)(2,1)S(1)} %projection.1.here_ref), channel_id=1, source_target_pairs={{0,64},{16,80},{32,96},{48,112},{64,128},{80,144},{96,160},{112,17... | collective-permute-start | bytes 786440 | tf_op jit(solution)/shard_map/ppermute | solution.py:35
  88.5 2.6 %collective-permute-start.7 = (bf16[256,512]{1,0:T(8,128)(2,1)S(1)}, bf16[256,512]{1,0:T(8,128)(2,1)S(1)}, u32[]{:S(2)}, u32[]{:S(2)}) collective-permute-start(bf16[256,512]{1,0:T(8,128)(2,1)S(1)} %projection.1.here_ref), channel_id=1, source_target_pairs={{0,32},{16,48},{32,64},{48,80},{64,96},{80,112},{96,128},{112,144}... | collective-permute-start | bytes 786440 | tf_op jit(solution)/shard_map/ppermute | solution.py:35
  91.1 6.1 %collective-permute-done.6.far_ref = bf16[256,512]{1,0:T(8,128)(2,1)S(1)} collective-permute-done((bf16[256,512]{1,0:T(8,128)(2,1)S(1)}, bf16[256,512]{1,0:T(8,128)(2,1)S(1)}, u32[]{:S(2)}, u32[]{:S(2)}) %collective-permute-start.6) | collective-permute-done | bytes 262176 | tf_op jit(solution)/shard_map/ppermute | solution.py:35
  97.2 5.6 %collective-permute-done.7.near_ref = bf16[256,512]{1,0:T(8,128)(2,1)S(1)} collective-permute-done((bf16[256,512]{1,0:T(8,128)(2,1)S(1)}, bf16[256,512]{1,0:T(8,128)(2,1)S(1)}, u32[]{:S(2)}, u32[]{:S(2)}) %collective-permute-start.7) | collective-permute-done | bytes 262176 | tf_op jit(solution)/shard_map/ppermute | solution.py:35
  102.7 0.0 copy-done.2
  102.7 12.6 %attention.1 = (f32[16,128]{1,0:T(8,128)S(1)}, bf16[128,2048]{1,0:T(8,128)(2,1)S(1)}, bf16[128,2816]{1,0:T(8,128)(2,1)S(1)}, f32[128,512]{1,0:T(8,128)S(1)}, bf1...) custom-call(s32[19]{0:T(128)S(1)} %pad_add_fusion.place_ref, ...), custom_call_target="tpu_custom_call" | custom-call | flops 4026531840 | bytes 8388608 | tf_op jit(solution)/shard_map/attention/pallas_call | solution.py:170
  115.3 3.7 %collective-permute-start.8 = (bf16[128,2816]{1,0:T(8,128)(2,1)S(1)}, bf16[128,2816]{1,0:T(8,128)(2,1)S(1)}, u32[]{:S(2)}, u32[]{:S(2)}) collective-permute-start(bf16[128,2816]{1,0:T(8,128)(2,1)S(1)} %get-tuple-element.26), channel_id=1, source_target_pairs={{0,16},{16,0},{32,48},{48,32},{64,80},{80,64},{96,112},{112,96},{1... | collective-permute-start | bytes 2162696 | tf_op jit(solution)/shard_map/ppermute | solution.py:40
  119.1 2.1 %collective-permute-start.9 = (bf16[128,512]{1,0:T(8,128)(2,1)S(1)}, bf16[128,512]{1,0:T(8,128)(2,1)S(1)}, u32[]{:S(2)}, u32[]{:S(2)}) collective-permute-start(bf16[128,512]{1,0:T(8,128)(2,1)S(1)} %get-tuple-element.29), channel_id=1, source_target_pairs={{32,0},{48,16},{64,32},{80,48},{96,64},{112,80},{128,96},{144,112}... | collective-permute-start | bytes 393224 | tf_op jit(solution)/shard_map/ppermute | solution.py:35
  121.2 2.1 %collective-permute-start.10 = (bf16[128,512]{1,0:T(8,128)(2,1)S(1)}, bf16[128,512]{1,0:T(8,128)(2,1)S(1)}, u32[]{:S(2)}, u32[]{:S(2)}) collective-permute-start(bf16[128,512]{1,0:T(8,128)(2,1)S(1)} %get-tuple-element.30), channel_id=1, source_target_pairs={{64,0},{80,16},{96,32},{112,48},{128,64},{144,80},{160,96},{176,11... | collective-permute-start | bytes 393224 | tf_op jit(solution)/shard_map/ppermute | solution.py:35
  123.2 5.9 %collective-permute-start.11 = (bf16[128,512]{1,0:T(8,128)(2,1)S(1)}, bf16[128,512]{1,0:T(8,128)(2,1)S(1)}, u32[]{:S(2)}, u32[]{:S(2)}) collective-permute-start(bf16[128,512]{1,0:T(8,128)(2,1)S(1)} %get-tuple-element.31), channel_id=1, source_target_pairs={{32,16},{48,0},{64,48},{80,32},{96,80},{112,64},{128,112},{144,96}... | collective-permute-start | bytes 393224 | tf_op jit(solution)/shard_map/ppermute | solution.py:35
  129.1 1.9 %collective-permute-start.12 = (bf16[128,512]{1,0:T(8,128)(2,1)S(1)}, bf16[128,512]{1,0:T(8,128)(2,1)S(1)}, u32[]{:S(2)}, u32[]{:S(2)}) collective-permute-start(bf16[128,512]{1,0:T(8,128)(2,1)S(1)} %get-tuple-element.32), channel_id=1, source_target_pairs={{64,16},{80,0},{96,48},{112,32},{128,80},{144,64},{160,112},{176,9... | collective-permute-start | bytes 393224 | tf_op jit(solution)/shard_map/ppermute | solution.py:35
  131.0 0.0 collective-permute-done.9.near_mine
  131.1 0.0 collective-permute-done.10.far_mine
  131.1 1.2 collective-permute-done.11.near_other
  132.3 5.3 %collective-permute-done.12.far_other = bf16[128,512]{1,0:T(8,128)(2,1)S(1)} collective-permute-done((bf16[128,512]{1,0:T(8,128)(2,1)S(1)}, bf16[128,512]{1,0:T(8,128)(2,1)S(1)}, u32[]{:S(2)}, u32[]{:S(2)}) %collective-permute-start.12) | collective-permute-done | bytes 131104 | tf_op jit(solution)/shard_map/ppermute | solution.py:35
  137.6 0.0 collective-permute-done.8.from_core
  137.6 1.8 %finish.1 = (f32[32,128]{1,0:T(8,128)}, bf16[128,4096]{1,0:T(8,128)(2,1)}, bf16[128,1024]{1,0:T(8,128)(2,1)}) custom-call(s32[19]{0:T(128)S(1)} %pad_add_fusion.place_ref, bf16[128,2048]{1,0:T(8,128)(2,1)S(1)} %get-tuple-element.25.dq_mine, bf16[128,2816]{1,0:T(8,128)(2,1)S(1)} %collective-permute-done.8.from_core, ...), custom_call_target="tpu_custom_call" | custom-call | bytes 4194304 | tf_op jit(solution)/shard_map/finish/pallas_call | solution.py:250
  (4 shorter events, 0.1 us)
Async XLA Ops:
  31.2 12.3 %copy-start.1 = (bf16[128,4096]{1,0:T(8,128)(2,1)S(1)}, bf16[128,4096]{1,0:T(8,128)(2,1)}, u32[]{:S(2)}) copy-start(bf16[128,4096]{1,0:T(8,128)(2,1)} %q_mine) | copy-start | bytes 3145732
  31.2 12.3 %all-to-all-start.1 = ((bf16[4,16,16,512]{3,2,1,0:T(8,128)(2,1)}), bf16[4,16,16,512]{3,2,1,0:T(8,128)(2,1)S(1)}, u32[]{:S(2)}, u32[]{:S(2)}) async-start(bf16[4,16,16,512]{3,2,1,0:T(8,128)(2,1)} %broadcast_in_dim.5), calls=%async_computation.1 | async-start | bytes 2097152 | tf_op jit(solution)/shard_map/all_to_all | solution.py:345
  35.5 21.5 %copy-start = (bf16[128,4096]{1,0:T(8,128)(2,1)S(1)}, bf16[128,4096]{1,0:T(8,128)(2,1)}, u32[]{:S(2)}) copy-start(bf16[128,4096]{1,0:T(8,128)(2,1)} %mine_ref) | copy-start | bytes 3145732
  43.5 24.2 %collective-permute-start = (bf16[128,2048]{1,0:T(8,128)(2,1)S(1)}, bf16[128,2048]{1,0:T(8,128)(2,1)S(1)}, u32[]{:S(2)}, u32[]{:S(2)}) collective-permute-start(bf16[128,2048]{1,0:T(8,128)(2,1)S(1)} %constant_dynamic-slice_fusion.1), channel_id=1, source_target_pairs={{0,16},{16,0},{32,48},{48,32},{64,80},{80,64},{96,112},{112,96},{1... | collective-permute-start | bytes 1572872 | tf_op jit(solution)/shard_map/ppermute | solution.py:40
  54.8 17.4 %collective-permute-start.2 = (bf16[4,16,16,512]{3,2,1,0:T(8,128)(2,1)S(1)}, bf16[4,16,16,512]{3,2,1,0:T(8,128)(2,1)S(1)}, u32[]{:S(2)}, u32[]{:S(2)}) collective-permute-start(bf16[4,16,16,512]{3,2,1,0:T(8,128)(2,1)S(1)} %all-to-all-done.1.own_ref), channel_id=1, source_target_pairs={{0,256},{16,80},{32,288},{48,112},{64,320},{80,16},{96,352},{112,4... | collective-permute-start | bytes 3145736 | tf_op jit(solution)/shard_map/ppermute | solution.py:352
  57.0 15.2 %collective-permute-start.3 = (bf16[128,4096]{1,0:T(8,128)(2,1)S(1)}, bf16[128,4096]{1,0:T(8,128)(2,1)S(1)}, u32[]{:S(2)}, u32[]{:S(2)}) collective-permute-start(bf16[128,4096]{1,0:T(8,128)(2,1)S(1)} %copy-done), channel_id=1, source_target_pairs={{0,16},{16,0},{32,48},{48,32},{64,80},{80,64},{96,112},{112,96},{1... | collective-permute-start | bytes 3145736 | tf_op jit(solution)/shard_map/ppermute | solution.py:40
  60.1 23.3 %collective-permute-start.4 = (bf16[4,16,16,512]{3,2,1,0:T(8,128)(2,1)S(1)}, bf16[4,16,16,512]{3,2,1,0:T(8,128)(2,1)S(1)}, u32[]{:S(2)}, u32[]{:S(2)}) collective-permute-start(bf16[4,16,16,512]{3,2,1,0:T(8,128)(2,1)S(1)} %all-to-all-done.1.own_ref), channel_id=1, source_target_pairs={{0,128},{16,48},{32,160},{48,80},{64,192},{80,112},{96,224},{112,1... | collective-permute-start | bytes 3145736 | tf_op jit(solution)/shard_map/ppermute | solution.py:352
  62.3 21.1 %collective-permute-start.5 = (bf16[4,16,16,512]{3,2,1,0:T(8,128)(2,1)S(1)}, bf16[4,16,16,512]{3,2,1,0:T(8,128)(2,1)S(1)}, u32[]{:S(2)}, u32[]{:S(2)}) collective-permute-start(bf16[4,16,16,512]{3,2,1,0:T(8,128)(2,1)S(1)} %all-to-all-done.1.own_ref), channel_id=1, source_target_pairs={{0,384},{16,112},{32,416},{48,16},{64,448},{80,48},{96,480},{112,8... | collective-permute-start | bytes 3145736 | tf_op jit(solution)/shard_map/ppermute | solution.py:352
  67.7 3.8 %collective-permute-start.1 = (bf16[128,2048]{1,0:T(8,128)(2,1)S(1)}, bf16[128,2048]{1,0:T(8,128)(2,1)S(1)}, u32[]{:S(2)}, u32[]{:S(2)}) collective-permute-start(bf16[128,2048]{1,0:T(8,128)(2,1)S(1)} %constant_dynamic-slice_fusion), channel_id=1, source_target_pairs={{0,16},{16,0},{32,48},{48,32},{64,80},{80,64},{96,112},{112,96},{1... | collective-permute-start | bytes 1572872 | tf_op jit(solution)/shard_map/ppermute | solution.py:40
  69.6 0.7 copy-start.3
  70.4 32.4 %copy-start.2 = (bf16[128,4096]{1,0:T(8,128)(2,1)S(1)}, bf16[128,4096]{1,0:T(8,128)(2,1)}, u32[]{:S(2)}) copy-start(bf16[128,4096]{1,0:T(8,128)(2,1)} %u_mine) | copy-start | bytes 3145732
  85.8 11.3 %collective-permute-start.6 = (bf16[256,512]{1,0:T(8,128)(2,1)S(1)}, bf16[256,512]{1,0:T(8,128)(2,1)S(1)}, u32[]{:S(2)}, u32[]{:S(2)}) collective-permute-start(bf16[256,512]{1,0:T(8,128)(2,1)S(1)} %projection.1.here_ref), channel_id=1, source_target_pairs={{0,64},{16,80},{32,96},{48,112},{64,128},{80,144},{96,160},{112,17... | collective-permute-start | bytes 786440 | tf_op jit(solution)/shard_map/ppermute | solution.py:35
  88.5 14.2 %collective-permute-start.7 = (bf16[256,512]{1,0:T(8,128)(2,1)S(1)}, bf16[256,512]{1,0:T(8,128)(2,1)S(1)}, u32[]{:S(2)}, u32[]{:S(2)}) collective-permute-start(bf16[256,512]{1,0:T(8,128)(2,1)S(1)} %projection.1.here_ref), channel_id=1, source_target_pairs={{0,32},{16,48},{32,64},{48,80},{64,96},{80,112},{96,128},{112,144}... | collective-permute-start | bytes 786440 | tf_op jit(solution)/shard_map/ppermute | solution.py:35
  115.3 22.2 %collective-permute-start.8 = (bf16[128,2816]{1,0:T(8,128)(2,1)S(1)}, bf16[128,2816]{1,0:T(8,128)(2,1)S(1)}, u32[]{:S(2)}, u32[]{:S(2)}) collective-permute-start(bf16[128,2816]{1,0:T(8,128)(2,1)S(1)} %get-tuple-element.26), channel_id=1, source_target_pairs={{0,16},{16,0},{32,48},{48,32},{64,80},{80,64},{96,112},{112,96},{1... | collective-permute-start | bytes 2162696 | tf_op jit(solution)/shard_map/ppermute | solution.py:40
  119.1 12.0 %collective-permute-start.9 = (bf16[128,512]{1,0:T(8,128)(2,1)S(1)}, bf16[128,512]{1,0:T(8,128)(2,1)S(1)}, u32[]{:S(2)}, u32[]{:S(2)}) collective-permute-start(bf16[128,512]{1,0:T(8,128)(2,1)S(1)} %get-tuple-element.29), channel_id=1, source_target_pairs={{32,0},{48,16},{64,32},{80,48},{96,64},{112,80},{128,96},{144,112}... | collective-permute-start | bytes 393224 | tf_op jit(solution)/shard_map/ppermute | solution.py:35
  121.2 9.9 %collective-permute-start.10 = (bf16[128,512]{1,0:T(8,128)(2,1)S(1)}, bf16[128,512]{1,0:T(8,128)(2,1)S(1)}, u32[]{:S(2)}, u32[]{:S(2)}) collective-permute-start(bf16[128,512]{1,0:T(8,128)(2,1)S(1)} %get-tuple-element.30), channel_id=1, source_target_pairs={{64,0},{80,16},{96,32},{112,48},{128,64},{144,80},{160,96},{176,11... | collective-permute-start | bytes 393224 | tf_op jit(solution)/shard_map/ppermute | solution.py:35
  123.2 9.1 %collective-permute-start.11 = (bf16[128,512]{1,0:T(8,128)(2,1)S(1)}, bf16[128,512]{1,0:T(8,128)(2,1)S(1)}, u32[]{:S(2)}, u32[]{:S(2)}) collective-permute-start(bf16[128,512]{1,0:T(8,128)(2,1)S(1)} %get-tuple-element.31), channel_id=1, source_target_pairs={{32,16},{48,0},{64,48},{80,32},{96,80},{112,64},{128,112},{144,96}... | collective-permute-start | bytes 393224 | tf_op jit(solution)/shard_map/ppermute | solution.py:35
  129.1 8.4 %collective-permute-start.12 = (bf16[128,512]{1,0:T(8,128)(2,1)S(1)}, bf16[128,512]{1,0:T(8,128)(2,1)S(1)}, u32[]{:S(2)}, u32[]{:S(2)}) collective-permute-start(bf16[128,512]{1,0:T(8,128)(2,1)S(1)} %get-tuple-element.32), channel_id=1, source_target_pairs={{64,16},{80,0},{96,48},{112,32},{128,80},{144,64},{160,112},{176,9... | collective-permute-start | bytes 393224 | tf_op jit(solution)/shard_map/ppermute | solution.py:35

commit v4 on v3

--- a/solution.py
+++ b/solution.py
@@ -17,12 +17,14 @@
 GROUPS = KVH // CORES
 HEADS = QH // KVH
 DOCS = 16
-LENGTHS = 3
+KINDS = 3
+LENGTHS = 6
 SPAN = 4 * BLOCK
+CHIPS = 2
 KEYS = SPAN + BLOCK
 SHARDS = 16
-SLICES = 16
-ROWS = 16
+SLICES = 8
+ROWS = 32
 SCALE = 1.0 / math.sqrt(HD)
 LOG2E = math.log2(math.e)
 
@@ -35,6 +37,17 @@
     return lax.ppermute(block, "tok", route)
 
 
+def partner(device):
+    return device ^ (2 if device % CORES else 8)
+
+
+def paired(block, distance=0, across=False):
+    count = lax.axis_size("tok")
+    route = [(partner(i) ^ (1 if across else 0), i) for i in range(count)]
+    route = [(i, j + distance) for i, j in route if j + distance < count]
+    return lax.ppermute(block, "tok", route)
+
+
 def swapped(block):
     count = lax.axis_size("tok")
     return lax.ppermute(block, "tok", [(i, i ^ 1) for i in range(count)])
@@ -46,12 +59,13 @@
 
 
 def attention_kernel(
-    place_ref, q_mine, q_other, u_mine, u_other, far_ref, near_ref, here_ref,
-    log_mine, dq_mine, to_core, here_mine, near_mine, near_other, far_mine, far_other,
-    keys, values, sums, bias, q_rows, u_rows, weight_rows, change_rows,
+    place_ref, q_mine, q_other, u_mine, u_other, *refs
 ):
     group, part = pl.program_id(0), pl.program_id(1)
     core, chip = place_ref[0], place_ref[1]
+    window, refs = refs[:6], refs[6:]
+    log_mine, dq_mine, to_core, here_mine, near_mine, near_other, far_mine, far_other = refs[:8]
+    keys, values, sums, bias, q_rows, u_rows, weight_rows, change_rows = refs[8:]
     first = pl.multiple_of(jnp.where(part == 0, core, 1 - core) * BLOCK, BLOCK)
 
     def stack(q_ref, u_ref):
@@ -62,9 +76,15 @@
 
     @pl.when(part == 0)
     def _():
-        for i, ref in enumerate((far_ref, near_ref, here_ref)):
-            keys[i * CHIP : (i + 1) * CHIP, :] = ref[:, :HD]
-            values[i * CHIP : (i + 1) * CHIP, :] = ref[:, HD:]
+        for i in range(3):
+            rows = slice(i * CHIP, (i + 1) * CHIP)
+            for kind in range(GROUPS):
+
+                @pl.when((place_ref[KINDS + 2 - i] == group) == (kind == 0))
+                def _():
+                    keys[rows, :] = window[2 * i + kind][:, :HD]
+                    values[rows, :] = window[2 * i + kind][:, HD:]
+
         sums[...] = jnp.zeros_like(sums)
         stack(q_mine, u_mine)
 
@@ -158,11 +178,11 @@
                 to_core[:, at + 2 * HD : at + 3 * HD] = terms.astype(jnp.bfloat16)
 
 
-def attention(place, queries, q_other, upstream, u_other, far, near, here):
+def attention(place, queries, q_other, upstream, u_other, *window):
     stacked = HEADS * BLOCK
     mine = pl.BlockSpec((BLOCK, HEADS * HD), lambda g, b, place: (0, place[0] * GROUPS + g))
     other = pl.BlockSpec((BLOCK, HEADS * HD), lambda g, b, place: (0, g))
-    context = pl.BlockSpec((CHIP, 2 * HD), lambda g, b, place: (0, g))
+    context = pl.BlockSpec((CHIP, 2 * HD), lambda g, b, place: (0, 0))
     block = pl.BlockSpec((BLOCK, 2 * HD), lambda g, b, place: (0, g))
     log = pl.BlockSpec((HEADS, BLOCK), lambda g, b, place: (g, 0))
     wide, packed, heads = GROUPS * 2 * HD, GROUPS * 3 * HD, GROUPS * HEADS
@@ -173,7 +193,7 @@
             num_scalar_prefetch=1,
             grid=(GROUPS, CORES),
             in_specs=[
-                mine, other, mine, other, context, context, context,
+                mine, other, mine, other, *[context] * 6,
             ],
             out_specs=[
                 log, other,
@@ -205,7 +225,7 @@
             transcendentals=CHIP * KEYS * GROUPS * HEADS,
         ),
         name="attention",
-    )(place, queries, q_other, upstream, u_other, far, near, here)
+    )(place, queries, q_other, upstream, u_other, *window)
 
 
 def finish_kernel(
@@ -263,57 +283,62 @@
 
 
 def projection_kernel(
-    place_ref, mine_ref, other_ref, own_ref, left_ref, right_ref, far_ref, out_ref, tokens, weight, sems
+    place_ref, *refs
 ):
+    mine_refs, other_refs = refs[:CHIPS], refs[CHIPS : 2 * CHIPS]
+    own_ref, far_ref, mine_ref, theirs_ref, tokens, weight, sems = refs[2 * CHIPS :]
     core, a = place_ref[0], place_ref[2]
-    pieces = ((own_ref, 0), (left_ref, 3), (right_ref, 1), (far_ref, 2))
+    pieces = ((own_ref, a), (far_ref, 1 - a))
 
     copies = [
         pltpu.make_async_copy(
-            ref.at[b], weight.at[lax.rem(a + turn, 4) * 4 + b], sems.at[i, b]
+            ref.at[b], weight.at[place * 4 + b], sems.at[i, b]
         )
-        for i, (ref, turn) in enumerate(pieces)
+        for i, (ref, place) in enumerate(pieces)
         for b in range(4)
     ]
     for copy in copies:
         copy.start()
     mine = pl.multiple_of(core * BLOCK, BLOCK)
-    tokens[pl.ds(mine, BLOCK), :] = mine_ref[...]
-    tokens[pl.ds(BLOCK - mine, BLOCK), :] = other_ref[...]
+    others = pl.multiple_of(BLOCK - mine, BLOCK)
+    for i in range(CHIPS):
+        tokens[pl.ds(i * CHIP + mine, BLOCK), :] = mine_refs[i][...]
+        tokens[pl.ds(i * CHIP + others, BLOCK), :] = other_refs[i][...]
     for copy in copies:
         copy.wait()
-    total = jnp.zeros(out_ref.shape, jnp.float32)
     depth = SLICES * ROWS
-    for z in range(SHARDS):
-        total += jnp.dot(
-            tokens[:, z * depth : (z + 1) * depth],
-            weight[:, z].reshape(depth, out_ref.shape[1]),
-            preferred_element_type=jnp.float32,
-        )
-    out_ref[...] = total.astype(out_ref.dtype)
-
-
-def projection(place, mine, other, own, left, right, far):
+    for i, out_ref in enumerate((mine_ref, theirs_ref)):
+        total = jnp.zeros(out_ref.shape, jnp.float32)
+        for z in range(SHARDS):
+            total += jnp.dot(
+                tokens[i * CHIP : (i + 1) * CHIP, z * depth : (z + 1) * depth],
+                weight[:, z].reshape(depth, out_ref.shape[1]),
+                preferred_element_type=jnp.float32,
+            )
+        out_ref[...] = total.astype(out_ref.dtype)
+
+
+def projection(place, mine, other, own, far):
     width = own.shape[-1]
-    depth = mine.shape[1]
+    depth = mine[0].shape[1]
     vmem = pl.BlockSpec(memory_space=pltpu.VMEM)
     away = pl.BlockSpec(memory_space=pl.ANY)
     return pl.pallas_call(
         projection_kernel,
-        in_specs=[pl.BlockSpec(memory_space=pltpu.SMEM), vmem, vmem, away, away, away, away],
-        out_specs=vmem,
-        out_shape=jax.ShapeDtypeStruct((CHIP, width), jnp.bfloat16),
+        in_specs=[pl.BlockSpec(memory_space=pltpu.SMEM)] + [vmem] * (2 * CHIPS) + [away] * 2,
+        out_specs=[vmem] * 2,
+        out_shape=[jax.ShapeDtypeStruct((CHIP, width), jnp.bfloat16)] * 2,
         scratch_shapes=[
-            pltpu.VMEM((CHIP, depth), jnp.bfloat16),
+            pltpu.VMEM((CHIPS * CHIP, depth), jnp.bfloat16),
             pltpu.VMEM((SLICES, SHARDS, ROWS, width), jnp.bfloat16),
-            pltpu.SemaphoreType.DMA((4, 4)),
+            pltpu.SemaphoreType.DMA((2, 4)),
         ],
         compiler_params=pltpu.CompilerParams(vmem_limit_bytes=32 * 2**20),
         cost_estimate=pl.CostEstimate(
-            flops=2 * CHIP * depth * width, bytes_accessed=6 * 2**20, transcendentals=0
+            flops=2 * CHIPS * CHIP * depth * width, bytes_accessed=10 * 2**20, transcendentals=0
         ),
         name="projection",
-    )(place, mine, other, own, left, right, far)
+    )(place, *mine, *other, own, far)
 
 
 def ring_of(core, x, y, turn, first):
@@ -330,11 +355,10 @@
     return [(x, y, core) for x in range(4) for y in range(4) for core in range(CORES)]
 
 
-def gathered(rows, device):
-    chip, core = device // CORES, device % CORES
-    x, y = chip // 4, chip % 4
-    a, b = jnp.where(core == 0, x, y), jnp.where(core == 0, y, x)
-    piece = lax.dynamic_slice_in_dim(rows, (a * 4 + b) * ROWS, ROWS, 0)
+def gathered(weight, core, a, b, group):
+    piece = lax.dynamic_slice_in_dim(weight, (a * 4 + b) * ROWS, ROWS, 0)
+    piece = piece.reshape(ROWS, 2, KVH, HD)
+    piece = lax.dynamic_slice_in_dim(piece, core * GROUPS + group, 1, 2).reshape(ROWS, 2 * HD)
     piece = jnp.broadcast_to(piece[None], (SHARDS,) + piece.shape)
     piece = lax.all_to_all(piece, "fsdp", 0, 0)
     groups = {}
@@ -343,38 +367,40 @@
         groups[tuple(sorted(members))] = None
     piece = jnp.broadcast_to(piece[None], (4,) + piece.shape)
     own = lax.all_to_all(piece, "tok", 0, 0, axis_index_groups=[list(g) for g in groups])
-
-    def turned(turn):
-        route = [
-            (number(*place), number(*ring_of(place[2], *place[:2], turn, False), place[2]))
-            for place in in_plane()
-        ]
-        return lax.ppermute(own, "tok", route)
-
-    return a, own, turned(1), turned(-1), turned(2)
+    route = [
+        (number(*place), number(*ring_of(place[2], *place[:2], 2, False), place[2]))
+        for place in in_plane()
+    ]
+    return own, lax.ppermute(own, "tok", route)
 
 
 def body(hidden, queries, upstream, context_weight, lengths):
     device = lax.axis_index("tok")
     core, chip = device % CORES, device // CORES
-    ordered = context_weight.reshape(-1, 2, CORES, GROUPS, HD)
-    ordered = lax.dynamic_slice_in_dim(ordered, core, 1, 2)[:, :, 0]
-    ordered = ordered.transpose(0, 2, 1, 3).reshape(-1, GROUPS * 2 * HD)
-    a, own, left, right, opposite = gathered(ordered, device)
-
-    hidden, queries, upstream, _ = lax.optimization_barrier((hidden, queries, upstream, own))
-    other_hidden = swapped(hidden)
+
+    def along(chip):
+        return jnp.where(core == 0, chip // 4, chip % 4)
+
+    a, b = along(chip), jnp.where(core == 0, chip % 4, chip // 4)
+    own, opposite = gathered(context_weight, core, a // 2, b, a % 2)
+
+    tokens, traded = [hidden, paired(hidden)], [swapped(hidden), paired(hidden, across=True)]
+
+    queries, upstream, _ = lax.optimization_barrier((queries, upstream, own))
     q_other = swapped(half(queries, 1 - core, 1))
     u_other = swapped(half(upstream, 1 - core, 1))
-    place = jnp.concatenate([jnp.stack([core, chip, a]).astype(jnp.int32), lengths[0]])
+    kinds = [along(chip) % 2, along(chip + 15) % 2, along(chip + 14) % 2]
+    place = jnp.stack([core, chip, a // 2] + kinds).astype(jnp.int32)
+    place = jnp.concatenate([place, lengths[0]])
     place, q_other, u_other, opposite = lax.optimization_barrier((place, q_other, u_other, opposite))
 
-    here = projection(place, hidden, other_hidden, own, left, right, opposite)
-    near = shifted(here, CORES)
-    far = shifted(here, 2 * CORES)
+    mine, theirs = projection(place, tokens, traded, own, opposite)
+    far = [shifted(mine, 2 * CORES), paired(theirs, 2 * CORES)]
+    near = [shifted(mine, CORES), paired(theirs, CORES)]
+    here = [mine, paired(theirs)]
     (
         log_mine, dq_mine, to_core, here_mine, near_mine, near_other, far_mine, far_other,
-    ) = attention(place, queries, q_other, upstream, u_other, far, near, here)
+    ) = attention(place, queries, q_other, upstream, u_other, *far, *near, *here)
     far_mine, far_other = shifted(far_mine, -2 * CORES), shifted(far_other, -2 * CORES, True)
     near_mine, near_other = shifted(near_mine, -CORES), shifted(near_other, -CORES, True)
     from_core = swapped(to_core)

time: 140 us -> 160 us (1.14)
  starting transfers between devices: 50.2 us -> 61.1 us
  waiting for transfers between devices: 39.1 us -> 43.4 us
  Pallas kernels: 16.8 us -> 19.7 us
    ppermute x3 -> x6, waiting for transfers between devices: 11.9 us -> 27.7 us  [the longest x5 23.7 us: paired(): return lax.ppermute(block, 'tok', route)]
    ppermute x6, waiting for transfers between devices: 18.1 us -> 6.5 us  [shifted(): return lax.ppermute(block, 'tok', route)]
    ppermute x3 -> x6, starting transfers between devices: 8.68 us -> 13.4 us  [the longest x5 11.2 us: paired(): return lax.ppermute(block, 'tok', route)]
    ppermute x6, starting transfers between devices: 17.2 us -> 21.8 us  [shifted(): return lax.ppermute(block, 'tok', route)]
    pallas_call x1, Pallas kernels: 2.4 us -> 4.46 us  [projection(): pl.pallas_call(projection_kernel, in_specs=[pl.BlockSpec(memory_space=plt...]
    dynamic_slice x2, local copies, waits for them, and re-layouts: 1.12 us -> 2.96 us  [half(): return lax.dynamic_slice_in_dim(block, index * size, size, axis)]
    ppermute x4, starting transfers between devices: 20 us -> 21.7 us  [swapped(): return lax.ppermute(block, 'tok', [(i, i ^ 1) for i in range(count)])]
  transfers between devices with their start and end apart: 14 -> 17, of which waited for: 8 -> 9; matrix products, arithmetic and copies ran while one was open for 1% -> 1% of each run, Pallas kernels for 0% -> 0%
where the time goes in v4:
time: 160 us; the launch traced here: 159 us
  starting transfers between devices  61.1 us (38%)
  waiting for transfers between devices  43.4 us (27%)
  blocking collectives  27.9 us (17%)
  Pallas kernels  19.7 us (12%)
  local copies, waits for them, and re-layouts  5.93 us (4%)
    all_to_all x1, blocking collectives, gathered(): piece = lax.all_to_all(piece, 'fsdp', 0, 0)  27.9 us
    ppermute x5, waiting for transfers between devices, paired(): return lax.ppermute(block, 'tok', route)  23.7 us
    ppermute x6, starting transfers between devices, shifted(): return lax.ppermute(block, 'tok', route)  21.8 us
    ppermute x4, starting transfers between devices, swapped(): return lax.ppermute(block, 'tok', [(i, i ^ 1) for i in range(count)])  21.7 us
    pallas_call x1, Pallas kernels, attention(): pl.pallas_call(attention_kernel, grid_spec=pltpu.PrefetchScalarGridSpec(n...  13.4 us
    ppermute x5, starting transfers between devices, paired(): return lax.ppermute(block, 'tok', route)  11.2 us
    all_to_all x1, waiting for transfers between devices, gathered(): lax.all_to_all(piece, 'tok', 0, 0, axis_index_groups=[list(g) for g in gr...  7.95 us
    ppermute x6, waiting for transfers between devices, shifted(): return lax.ppermute(block, 'tok', route)  6.5 us
  transfers between devices with their start and end apart: 17, of which 9 were waited for; matrix products, arithmetic and copies ran while one was open for 1% of the time, Pallas kernels for 0%

profile of v4, /device:TPU:7, one launch (start us, length us, event | category | flops | bytes accessed | tf_op | source)
XLA Modules:
  0.0 159.0 jit_solution(11847151477807051317)
XLA Ops:
  0.6 0.0 copy-start
  0.7 0.9 copy-done
  1.7 0.1 dynamic-slice_reduce_fusion
  1.9 27.9 %all_to_all.10 = bf16[16,32,256]{2,1,0:T(8,128)(2,1)S(1)} all-to-all(bf16[16,32,256]{2,1,0:T(8,128)(2,1)S(1)} %broadcast_in_dim.14), channel_id=1, replica_groups=mesh['tok'=32,'fsdp'=16] {'fsdp'}, dimensions={0} | all-to-all | bytes 524288 | tf_op jit(solution)/shard_map/all_to_all | solution.py:363
  29.7 1.1 broadcast_in_dim.15
  30.8 4.2 %all-to-all-start.1 = ((bf16[4,16,32,256]{3,2,1,0:T(8,128)(2,1)}), bf16[4,16,32,256]{3,2,1,0:T(8,128)(2,1)S(1)}, u32[]{:S(2)}, u32[]{:S(2)}) async-start(bf16[4,16,32,256]{3,2,1,0:T(8,128)(2,1)} %broadcast_in_dim.15), calls=%async_computation.1 | async-start | bytes 2097152 | tf_op jit(solution)/shard_map/all_to_all | solution.py:369
  35.0 0.0 copy-start.1
  35.0 8.0 %all-to-all-done.1.refs_4_ = bf16[4,16,32,256]{3,2,1,0:T(8,128)(2,1)S(1)} async-done(((bf16[4,16,32,256]{3,2,1,0:T(8,128)(2,1)}), bf16[4,16,32,256]{3,2,1,0:T(8,128)(2,1)S(1)}, u32[]{:S(2)}, u32[]{:S(2)}) %all-to-all-start.1) | async-done | bytes 1048608 | tf_op jit(solution)/shard_map/all_to_all | solution.py:369
  43.0 1.1 constant_dynamic-slice_fusion
  44.1 11.3 %collective-permute-start.1 = (bf16[128,2048]{1,0:T(8,128)(2,1)S(1)}, bf16[128,2048]{1,0:T(8,128)(2,1)S(1)}, u32[]{:S(2)}, u32[]{:S(2)}) collective-permute-start(bf16[128,2048]{1,0:T(8,128)(2,1)S(1)} %constant_dynamic-slice_fusion), channel_id=1, source_target_pairs={{0,16},{16,0},{32,48},{48,32},{64,80},{80,64},{96,112},{112,96},{1... | collective-permute-start | bytes 1572872 | tf_op jit(solution)/shard_map/ppermute | solution.py:53
  55.4 2.2 %collective-permute-start.2 = (bf16[4,16,32,256]{3,2,1,0:T(8,128)(2,1)S(1)}, bf16[4,16,32,256]{3,2,1,0:T(8,128)(2,1)}, u32[]{:S(2)}, u32[]{:S(2)}) collective-permute-start(bf16[4,16,32,256]{3,2,1,0:T(8,128)(2,1)S(1)} %all-to-all-done.1.refs_4_), channel_id=1, source_target_pairs={{0,256},{16,80},{32,288},{48,112},{64,320},{80,16},{96,352},{112,4... | collective-permute-start | bytes 3145736 | tf_op jit(solution)/shard_map/ppermute | solution.py:374
  57.6 0.0 copy-done.1
  57.6 3.0 %collective-permute-start.4 = (bf16[128,4096]{1,0:T(8,128)(2,1)S(1)}, bf16[128,4096]{1,0:T(8,128)(2,1)}, u32[]{:S(2)}, u32[]{:S(2)}) collective-permute-start(bf16[128,4096]{1,0:T(8,128)(2,1)S(1)} %copy-done.1), channel_id=1, source_target_pairs={{0,16},{16,0},{32,48},{48,32},{64,80},{80,64},{96,112},{112,96},{1... | collective-permute-start | bytes 3145736 | tf_op jit(solution)/shard_map/ppermute | solution.py:53
  60.6 2.2 %collective-permute-start.3 = (bf16[128,4096]{1,0:T(8,128)(2,1)S(1)}, bf16[128,4096]{1,0:T(8,128)(2,1)}, u32[]{:S(2)}, u32[]{:S(2)}) collective-permute-start(bf16[128,4096]{1,0:T(8,128)(2,1)S(1)} %copy-done.1), channel_id=1, source_target_pairs={{128,0},{48,16},{160,32},{16,48},{192,64},{112,80},{224,96},{80,11... | collective-permute-start | bytes 3145736 | tf_op jit(solution)/shard_map/ppermute | solution.py:48
  62.8 3.3 %collective-permute-start.5 = (bf16[128,4096]{1,0:T(8,128)(2,1)S(1)}, bf16[128,4096]{1,0:T(8,128)(2,1)}, u32[]{:S(2)}, u32[]{:S(2)}) collective-permute-start(bf16[128,4096]{1,0:T(8,128)(2,1)S(1)} %copy-done.1), channel_id=1, source_target_pairs={{144,0},{32,16},{176,32},{0,48},{208,64},{96,80},{240,96},{64,112}... | collective-permute-start | bytes 3145736 | tf_op jit(solution)/shard_map/ppermute | solution.py:48
  66.1 1.9 %constant_dynamic-slice_fusion.1 = bf16[128,2048]{1,0:T(8,128)(2,1)} fusion(bf16[128,4096]{1,0:T(8,128)(2,1)} %q_mine, s32[]{:T(128)S(6)} %select_n.97), kind=kLoop, calls=%fused_computation.3 | loop fusion | bytes 1048580 | tf_op jit(solution)/shard_map/dynamic_slice | solution.py:58
  68.0 0.0 collective-permute-done.1.u_other
  68.0 2.1 %collective-permute-start = (bf16[128,2048]{1,0:T(8,128)(2,1)}, bf16[128,2048]{1,0:T(8,128)(2,1)}, u32[]{:S(2)}, u32[]{:S(2)}) collective-permute-start(bf16[128,2048]{1,0:T(8,128)(2,1)} %constant_dynamic-slice_fusion.1), channel_id=1, source_target_pairs={{0,16},{16,0},{32,48},{48,32},{64,80},{80,64},{96,112},{112,96},{1... | collective-permute-start | bytes 1572872 | tf_op jit(solution)/shard_map/ppermute | solution.py:53
  70.2 0.0 copy-start.4
  70.2 0.6 copy-done.4
  70.9 0.1 concatenate.3.place_ref
  71.0 0.0 copy-start.2
  71.0 0.0 copy-start.3
  71.0 1.2 collective-permute-done.q_other
  72.1 4.0 %collective-permute-done.2.refs_5_ = bf16[4,16,32,256]{3,2,1,0:T(8,128)(2,1)} collective-permute-done((bf16[4,16,32,256]{3,2,1,0:T(8,128)(2,1)S(1)}, bf16[4,16,32,256]{3,2,1,0:T(8,128)(2,1)}, u32[]{:S(2)}, u32[]{:S(2)}) %collective-permute-start.2) | collective-permute-done | bytes 1048608 | tf_op jit(solution)/shard_map/ppermute | solution.py:374
  76.2 0.0 collective-permute-done.4.refs_2_
  76.2 17.4 %collective-permute-done.3.refs_1_ = bf16[128,4096]{1,0:T(8,128)(2,1)} collective-permute-done((bf16[128,4096]{1,0:T(8,128)(2,1)S(1)}, bf16[128,4096]{1,0:T(8,128)(2,1)}, u32[]{:S(2)}, u32[]{:S(2)}) %collective-permute-start.3) | collective-permute-done | bytes 1048608 | tf_op jit(solution)/shard_map/ppermute | solution.py:48
  93.6 0.0 collective-permute-done.5.refs_3_
  93.6 4.5 %projection.1 = (bf16[256,256]{1,0:T(8,128)(2,1)S(1)}, bf16[256,256]{1,0:T(8,128)(2,1)S(1)}) custom-call(s32[22]{0:T(128)S(1)} %concatenate.3.place_ref, bf16[128,4096]{1,0:T(8,128)(2,1)S(1)} %copy-done.1, bf16[128,4096]{1,0:T(8,128)(2,1)} %collective-permute-done.3.refs_1_, bf16[128,4096]{1,0:T(8,128)(2,1)} %collective-permute-done.4.refs_2_, ...), custom_call_target="tpu_custom_call" | custom-call | flops 1073741824 | bytes 10485760 | tf_op jit(solution)/shard_map/projection/pallas_call | solution.py:326
  98.0 2.2 %collective-permute-start.8 = (bf16[256,256]{1,0:T(8,128)(2,1)S(1)}, bf16[256,256]{1,0:T(8,128)(2,1)S(1)}, u32[]{:S(2)}, u32[]{:S(2)}) collective-permute-start(bf16[256,256]{1,0:T(8,128)(2,1)S(1)} %get-tuple-element.25.refs_4_), channel_id=1, source_target_pairs={{0,32},{16,48},{32,64},{48,80},{64,96},{80,112},{96,128},{112,144}... | collective-permute-start | bytes 393224 | tf_op jit(solution)/shard_map/ppermute | solution.py:37
  100.2 4.5 %collective-permute-start.6 = (bf16[256,256]{1,0:T(8,128)(2,1)S(1)}, bf16[256,256]{1,0:T(8,128)(2,1)S(1)}, u32[]{:S(2)}, u32[]{:S(2)}) collective-permute-start(bf16[256,256]{1,0:T(8,128)(2,1)S(1)} %get-tuple-element.25.refs_4_), channel_id=1, source_target_pairs={{0,64},{16,80},{32,96},{48,112},{64,128},{80,144},{96,160},{112,17... | collective-permute-start | bytes 393224 | tf_op jit(solution)/shard_map/ppermute | solution.py:37
  104.8 1.9 %collective-permute-start.10 = (bf16[256,256]{1,0:T(8,128)(2,1)S(1)}, bf16[256,256]{1,0:T(8,128)(2,1)S(1)}, u32[]{:S(2)}, u32[]{:S(2)}) collective-permute-start(bf16[256,256]{1,0:T(8,128)(2,1)S(1)} %get-tuple-element.26), channel_id=1, source_target_pairs={{128,0},{48,16},{160,32},{16,48},{192,64},{112,80},{224,96},{80,11... | collective-permute-start | bytes 393224 | tf_op jit(solution)/shard_map/ppermute | solution.py:48
  106.7 1.9 %collective-permute-start.9 = (bf16[256,256]{1,0:T(8,128)(2,1)S(1)}, bf16[256,256]{1,0:T(8,128)(2,1)S(1)}, u32[]{:S(2)}, u32[]{:S(2)}) collective-permute-start(bf16[256,256]{1,0:T(8,128)(2,1)S(1)} %get-tuple-element.26), channel_id=1, source_target_pairs={{128,32},{48,48},{160,64},{16,80},{192,96},{112,112},{224,128},{80... | collective-permute-start | bytes 393224 | tf_op jit(solution)/shard_map/ppermute | solution.py:48
  108.6 1.9 %collective-permute-start.7 = (bf16[256,256]{1,0:T(8,128)(2,1)S(1)}, bf16[256,256]{1,0:T(8,128)(2,1)S(1)}, u32[]{:S(2)}, u32[]{:S(2)}) collective-permute-start(bf16[256,256]{1,0:T(8,128)(2,1)S(1)} %get-tuple-element.26), channel_id=1, source_target_pairs={{128,64},{48,80},{160,96},{16,112},{192,128},{112,144},{224,160},{... | collective-permute-start | bytes 393224 | tf_op jit(solution)/shard_map/ppermute | solution.py:48
  110.6 0.0 collective-permute-done.8.refs_2_
  110.6 0.0 collective-permute-done.6.refs_0_
  110.6 0.2 collective-permute-done.10.refs_5_
  110.8 5.3 %collective-permute-done.9.refs_3_ = bf16[256,256]{1,0:T(8,128)(2,1)S(1)} collective-permute-done((bf16[256,256]{1,0:T(8,128)(2,1)S(1)}, bf16[256,256]{1,0:T(8,128)(2,1)S(1)}, u32[]{:S(2)}, u32[]{:S(2)}) %collective-permute-start.9) | collective-permute-done | bytes 131104 | tf_op jit(solution)/shard_map/ppermute | solution.py:48
  116.1 0.8 collective-permute-done.7.refs_1_
  116.9 0.0 copy-done.2
  116.9 0.0 copy-done.3
  116.9 13.4 %attention.1 = (f32[16,128]{1,0:T(8,128)S(1)}, bf16[128,2048]{1,0:T(8,128)(2,1)S(1)}, bf16[128,2816]{1,0:T(8,128)(2,1)S(1)}, f32[128,512]{1,0:T(8,128)S(1)}, bf1...) custom-call(s32[22]{0:T(128)S(1)} %concatenate.3.place_ref, ...), custom_call_target="tpu_custom_call" | custom-call | flops 4026531840 | bytes 8388608 | tf_op jit(solution)/shard_map/attention/pallas_call | solution.py:190
  130.3 5.2 %collective-permute-start.11 = (bf16[128,2816]{1,0:T(8,128)(2,1)S(1)}, bf16[128,2816]{1,0:T(8,128)(2,1)S(1)}, u32[]{:S(2)}, u32[]{:S(2)}) collective-permute-start(bf16[128,2816]{1,0:T(8,128)(2,1)S(1)} %get-tuple-element.28), channel_id=1, source_target_pairs={{0,16},{16,0},{32,48},{48,32},{64,80},{80,64},{96,112},{112,96},{1... | collective-permute-start | bytes 2162696 | tf_op jit(solution)/shard_map/ppermute | solution.py:53
  135.5 2.2 %collective-permute-start.12 = (bf16[128,512]{1,0:T(8,128)(2,1)S(1)}, bf16[128,512]{1,0:T(8,128)(2,1)S(1)}, u32[]{:S(2)}, u32[]{:S(2)}) collective-permute-start(bf16[128,512]{1,0:T(8,128)(2,1)S(1)} %get-tuple-element.31), channel_id=1, source_target_pairs={{32,0},{48,16},{64,32},{80,48},{96,64},{112,80},{128,96},{144,112}... | collective-permute-start | bytes 393224 | tf_op jit(solution)/shard_map/ppermute | solution.py:37
  137.8 6.2 %collective-permute-start.13 = (bf16[128,512]{1,0:T(8,128)(2,1)S(1)}, bf16[128,512]{1,0:T(8,128)(2,1)S(1)}, u32[]{:S(2)}, u32[]{:S(2)}) collective-permute-start(bf16[128,512]{1,0:T(8,128)(2,1)S(1)} %get-tuple-element.32), channel_id=1, source_target_pairs={{64,0},{80,16},{96,32},{112,48},{128,64},{144,80},{160,96},{176,11... | collective-permute-start | bytes 393224 | tf_op jit(solution)/shard_map/ppermute | solution.py:37
  143.9 4.8 %collective-permute-start.14 = (bf16[128,512]{1,0:T(8,128)(2,1)S(1)}, bf16[128,512]{1,0:T(8,128)(2,1)S(1)}, u32[]{:S(2)}, u32[]{:S(2)}) collective-permute-start(bf16[128,512]{1,0:T(8,128)(2,1)S(1)} %get-tuple-element.33), channel_id=1, source_target_pairs={{32,16},{48,0},{64,48},{80,32},{96,80},{112,64},{128,112},{144,96}... | collective-permute-start | bytes 393224 | tf_op jit(solution)/shard_map/ppermute | solution.py:37
  148.7 1.9 %collective-permute-start.15 = (bf16[128,512]{1,0:T(8,128)(2,1)S(1)}, bf16[128,512]{1,0:T(8,128)(2,1)S(1)}, u32[]{:S(2)}, u32[]{:S(2)}) collective-permute-start(bf16[128,512]{1,0:T(8,128)(2,1)S(1)} %get-tuple-element.34), channel_id=1, source_target_pairs={{64,16},{80,0},{96,48},{112,32},{128,80},{144,64},{160,112},{176,9... | collective-permute-start | bytes 393224 | tf_op jit(solution)/shard_map/ppermute | solution.py:37
  150.6 0.0 collective-permute-done.12.near_mine
  150.6 0.0 collective-permute-done.13.far_mine
  150.6 1.2 collective-permute-done.14.near_other
  151.9 5.3 %collective-permute-done.15.far_other = bf16[128,512]{1,0:T(8,128)(2,1)S(1)} collective-permute-done((bf16[128,512]{1,0:T(8,128)(2,1)S(1)}, bf16[128,512]{1,0:T(8,128)(2,1)S(1)}, u32[]{:S(2)}, u32[]{:S(2)}) %collective-permute-start.15) | collective-permute-done | bytes 131104 | tf_op jit(solution)/shard_map/ppermute | solution.py:37
  157.1 0.0 collective-permute-done.11.from_core
  157.1 1.8 %finish.1 = (f32[32,128]{1,0:T(8,128)}, bf16[128,4096]{1,0:T(8,128)(2,1)}, bf16[128,1024]{1,0:T(8,128)(2,1)}) custom-call(s32[22]{0:T(128)S(1)} %concatenate.3.place_ref, bf16[128,2048]{1,0:T(8,128)(2,1)S(1)} %get-tuple-element.27.dq_mine, bf16[128,2816]{1,0:T(8,128)(2,1)S(1)} %collective-permute-done.11.from_core, ...), custom_call_target="tpu_custom_call" | custom-call | bytes 4194304 | tf_op jit(solution)/shard_map/finish/pallas_call | solution.py:270
  (4 shorter events, 0.1 us)
Async XLA Ops:
  0.6 1.0 copy-start
  30.8 12.2 %all-to-all-start.1 = ((bf16[4,16,32,256]{3,2,1,0:T(8,128)(2,1)}), bf16[4,16,32,256]{3,2,1,0:T(8,128)(2,1)S(1)}, u32[]{:S(2)}, u32[]{:S(2)}) async-start(bf16[4,16,32,256]{3,2,1,0:T(8,128)(2,1)} %broadcast_in_dim.15), calls=%async_computation.1 | async-start | bytes 2097152 | tf_op jit(solution)/shard_map/all_to_all | solution.py:369
  35.0 22.5 %copy-start.1 = (bf16[128,4096]{1,0:T(8,128)(2,1)S(1)}, bf16[128,4096]{1,0:T(8,128)(2,1)}, u32[]{:S(2)}) copy-start(bf16[128,4096]{1,0:T(8,128)(2,1)} %refs_0_.1) | copy-start | bytes 3145732
  44.1 23.9 %collective-permute-start.1 = (bf16[128,2048]{1,0:T(8,128)(2,1)S(1)}, bf16[128,2048]{1,0:T(8,128)(2,1)S(1)}, u32[]{:S(2)}, u32[]{:S(2)}) collective-permute-start(bf16[128,2048]{1,0:T(8,128)(2,1)S(1)} %constant_dynamic-slice_fusion), channel_id=1, source_target_pairs={{0,16},{16,0},{32,48},{48,32},{64,80},{80,64},{96,112},{112,96},{1... | collective-permute-start | bytes 1572872 | tf_op jit(solution)/shard_map/ppermute | solution.py:53
  55.4 20.8 %collective-permute-start.2 = (bf16[4,16,32,256]{3,2,1,0:T(8,128)(2,1)S(1)}, bf16[4,16,32,256]{3,2,1,0:T(8,128)(2,1)}, u32[]{:S(2)}, u32[]{:S(2)}) collective-permute-start(bf16[4,16,32,256]{3,2,1,0:T(8,128)(2,1)S(1)} %all-to-all-done.1.refs_4_), channel_id=1, source_target_pairs={{0,256},{16,80},{32,288},{48,112},{64,320},{80,16},{96,352},{112,4... | collective-permute-start | bytes 3145736 | tf_op jit(solution)/shard_map/ppermute | solution.py:374
  57.6 18.6 %collective-permute-start.4 = (bf16[128,4096]{1,0:T(8,128)(2,1)S(1)}, bf16[128,4096]{1,0:T(8,128)(2,1)}, u32[]{:S(2)}, u32[]{:S(2)}) collective-permute-start(bf16[128,4096]{1,0:T(8,128)(2,1)S(1)} %copy-done.1), channel_id=1, source_target_pairs={{0,16},{16,0},{32,48},{48,32},{64,80},{80,64},{96,112},{112,96},{1... | collective-permute-start | bytes 3145736 | tf_op jit(solution)/shard_map/ppermute | solution.py:53
  60.6 32.9 %collective-permute-start.3 = (bf16[128,4096]{1,0:T(8,128)(2,1)S(1)}, bf16[128,4096]{1,0:T(8,128)(2,1)}, u32[]{:S(2)}, u32[]{:S(2)}) collective-permute-start(bf16[128,4096]{1,0:T(8,128)(2,1)S(1)} %copy-done.1), channel_id=1, source_target_pairs={{128,0},{48,16},{160,32},{16,48},{192,64},{112,80},{224,96},{80,11... | collective-permute-start | bytes 3145736 | tf_op jit(solution)/shard_map/ppermute | solution.py:48
  62.8 30.7 %collective-permute-start.5 = (bf16[128,4096]{1,0:T(8,128)(2,1)S(1)}, bf16[128,4096]{1,0:T(8,128)(2,1)}, u32[]{:S(2)}, u32[]{:S(2)}) collective-permute-start(bf16[128,4096]{1,0:T(8,128)(2,1)S(1)} %copy-done.1), channel_id=1, source_target_pairs={{144,0},{32,16},{176,32},{0,48},{208,64},{96,80},{240,96},{64,112}... | collective-permute-start | bytes 3145736 | tf_op jit(solution)/shard_map/ppermute | solution.py:48
  68.0 4.1 %collective-permute-start = (bf16[128,2048]{1,0:T(8,128)(2,1)}, bf16[128,2048]{1,0:T(8,128)(2,1)}, u32[]{:S(2)}, u32[]{:S(2)}) collective-permute-start(bf16[128,2048]{1,0:T(8,128)(2,1)} %constant_dynamic-slice_fusion.1), channel_id=1, source_target_pairs={{0,16},{16,0},{32,48},{48,32},{64,80},{80,64},{96,112},{112,96},{1... | collective-permute-start | bytes 1572872 | tf_op jit(solution)/shard_map/ppermute | solution.py:53
  70.2 0.7 copy-start.4
  71.0 45.9 %copy-start.2 = (bf16[128,4096]{1,0:T(8,128)(2,1)S(1)}, bf16[128,4096]{1,0:T(8,128)(2,1)}, u32[]{:S(2)}) copy-start(bf16[128,4096]{1,0:T(8,128)(2,1)} %q_mine) | copy-start | bytes 3145732
  71.0 45.9 %copy-start.3 = (bf16[128,4096]{1,0:T(8,128)(2,1)S(1)}, bf16[128,4096]{1,0:T(8,128)(2,1)}, u32[]{:S(2)}) copy-start(bf16[128,4096]{1,0:T(8,128)(2,1)} %u_mine) | copy-start | bytes 3145732
  98.0 12.5 %collective-permute-start.8 = (bf16[256,256]{1,0:T(8,128)(2,1)S(1)}, bf16[256,256]{1,0:T(8,128)(2,1)S(1)}, u32[]{:S(2)}, u32[]{:S(2)}) collective-permute-start(bf16[256,256]{1,0:T(8,128)(2,1)S(1)} %get-tuple-element.25.refs_4_), channel_id=1, source_target_pairs={{0,32},{16,48},{32,64},{48,80},{64,96},{80,112},{96,128},{112,144}... | collective-permute-start | bytes 393224 | tf_op jit(solution)/shard_map/ppermute | solution.py:37
  100.2 10.3 %collective-permute-start.6 = (bf16[256,256]{1,0:T(8,128)(2,1)S(1)}, bf16[256,256]{1,0:T(8,128)(2,1)S(1)}, u32[]{:S(2)}, u32[]{:S(2)}) collective-permute-start(bf16[256,256]{1,0:T(8,128)(2,1)S(1)} %get-tuple-element.25.refs_4_), channel_id=1, source_target_pairs={{0,64},{16,80},{32,96},{48,112},{64,128},{80,144},{96,160},{112,17... | collective-permute-start | bytes 393224 | tf_op jit(solution)/shard_map/ppermute | solution.py:37
  104.8 6.0 %collective-permute-start.10 = (bf16[256,256]{1,0:T(8,128)(2,1)S(1)}, bf16[256,256]{1,0:T(8,128)(2,1)S(1)}, u32[]{:S(2)}, u32[]{:S(2)}) collective-permute-start(bf16[256,256]{1,0:T(8,128)(2,1)S(1)} %get-tuple-element.26), channel_id=1, source_target_pairs={{128,0},{48,16},{160,32},{16,48},{192,64},{112,80},{224,96},{80,11... | collective-permute-start | bytes 393224 | tf_op jit(solution)/shard_map/ppermute | solution.py:48
  106.7 9.4 %collective-permute-start.9 = (bf16[256,256]{1,0:T(8,128)(2,1)S(1)}, bf16[256,256]{1,0:T(8,128)(2,1)S(1)}, u32[]{:S(2)}, u32[]{:S(2)}) collective-permute-start(bf16[256,256]{1,0:T(8,128)(2,1)S(1)} %get-tuple-element.26), channel_id=1, source_target_pairs={{128,32},{48,48},{160,64},{16,80},{192,96},{112,112},{224,128},{80... | collective-permute-start | bytes 393224 | tf_op jit(solution)/shard_map/ppermute | solution.py:48
  108.6 8.3 %collective-permute-start.7 = (bf16[256,256]{1,0:T(8,128)(2,1)S(1)}, bf16[256,256]{1,0:T(8,128)(2,1)S(1)}, u32[]{:S(2)}, u32[]{:S(2)}) collective-permute-start(bf16[256,256]{1,0:T(8,128)(2,1)S(1)} %get-tuple-element.26), channel_id=1, source_target_pairs={{128,64},{48,80},{160,96},{16,112},{192,128},{112,144},{224,160},{... | collective-permute-start | bytes 393224 | tf_op jit(solution)/shard_map/ppermute | solution.py:48
  130.3 26.9 %collective-permute-start.11 = (bf16[128,2816]{1,0:T(8,128)(2,1)S(1)}, bf16[128,2816]{1,0:T(8,128)(2,1)S(1)}, u32[]{:S(2)}, u32[]{:S(2)}) collective-permute-start(bf16[128,2816]{1,0:T(8,128)(2,1)S(1)} %get-tuple-element.28), channel_id=1, source_target_pairs={{0,16},{16,0},{32,48},{48,32},{64,80},{80,64},{96,112},{112,96},{1... | collective-permute-start | bytes 2162696 | tf_op jit(solution)/shard_map/ppermute | solution.py:53
  135.5 15.1 %collective-permute-start.12 = (bf16[128,512]{1,0:T(8,128)(2,1)S(1)}, bf16[128,512]{1,0:T(8,128)(2,1)S(1)}, u32[]{:S(2)}, u32[]{:S(2)}) collective-permute-start(bf16[128,512]{1,0:T(8,128)(2,1)S(1)} %get-tuple-element.31), channel_id=1, source_target_pairs={{32,0},{48,16},{64,32},{80,48},{96,64},{112,80},{128,96},{144,112}... | collective-permute-start | bytes 393224 | tf_op jit(solution)/shard_map/ppermute | solution.py:37
  137.8 12.9 %collective-permute-start.13 = (bf16[128,512]{1,0:T(8,128)(2,1)S(1)}, bf16[128,512]{1,0:T(8,128)(2,1)S(1)}, u32[]{:S(2)}, u32[]{:S(2)}) collective-permute-start(bf16[128,512]{1,0:T(8,128)(2,1)S(1)} %get-tuple-element.32), channel_id=1, source_target_pairs={{64,0},{80,16},{96,32},{112,48},{128,64},{144,80},{160,96},{176,11... | collective-permute-start | bytes 393224 | tf_op jit(solution)/shard_map/ppermute | solution.py:37
  143.9 7.9 %collective-permute-start.14 = (bf16[128,512]{1,0:T(8,128)(2,1)S(1)}, bf16[128,512]{1,0:T(8,128)(2,1)S(1)}, u32[]{:S(2)}, u32[]{:S(2)}) collective-permute-start(bf16[128,512]{1,0:T(8,128)(2,1)S(1)} %get-tuple-element.33), channel_id=1, source_target_pairs={{32,16},{48,0},{64,48},{80,32},{96,80},{112,64},{128,112},{144,96}... | collective-permute-start | bytes 393224 | tf_op jit(solution)/shard_map/ppermute | solution.py:37
  148.7 8.4 %collective-permute-start.15 = (bf16[128,512]{1,0:T(8,128)(2,1)S(1)}, bf16[128,512]{1,0:T(8,128)(2,1)S(1)}, u32[]{:S(2)}, u32[]{:S(2)}) collective-permute-start(bf16[128,512]{1,0:T(8,128)(2,1)S(1)} %get-tuple-element.34), channel_id=1, source_target_pairs={{64,16},{80,0},{96,48},{112,32},{128,80},{144,64},{160,112},{176,9... | collective-permute-start | bytes 393224 | tf_op jit(solution)/shard_map/ppermute | solution.py:37

commit v5 on v3

--- a/solution.py
+++ b/solution.py
@@ -330,18 +330,21 @@
     return [(x, y, core) for x in range(4) for y in range(4) for core in range(CORES)]
 
 
-def gathered(rows, device):
+def gathered(weight, device):
     chip, core = device // CORES, device % CORES
     x, y = chip // 4, chip % 4
     a, b = jnp.where(core == 0, x, y), jnp.where(core == 0, y, x)
-    piece = lax.dynamic_slice_in_dim(rows, (a * 4 + b) * ROWS, ROWS, 0)
+    piece = lax.dynamic_slice_in_dim(weight, (a * 4 + b) * ROWS, ROWS, 0)
+    piece = piece.reshape(ROWS, 2, CORES, GROUPS, HD)
+    piece = lax.dynamic_slice_in_dim(piece, core, 1, 2)[:, :, 0]
+    piece = piece.transpose(0, 2, 1, 3).reshape(ROWS, GROUPS * 2 * HD)
     piece = jnp.broadcast_to(piece[None], (SHARDS,) + piece.shape)
-    piece = lax.all_to_all(piece, "fsdp", 0, 0)
+    first = lax.all_to_all(piece, "fsdp", 0, 0)
     groups = {}
     for place in in_plane():
         members = [number(*ring_of(place[2], *place[:2], turn, True), place[2]) for turn in range(4)]
         groups[tuple(sorted(members))] = None
-    piece = jnp.broadcast_to(piece[None], (4,) + piece.shape)
+    piece = jnp.broadcast_to(first[None], (4,) + first.shape)
     own = lax.all_to_all(piece, "tok", 0, 0, axis_index_groups=[list(g) for g in groups])
 
     def turned(turn):
@@ -351,18 +354,15 @@
         ]
         return lax.ppermute(own, "tok", route)
 
-    return a, own, turned(1), turned(-1), turned(2)
+    return a, first, own, turned(1), turned(-1), turned(2)
 
 
 def body(hidden, queries, upstream, context_weight, lengths):
     device = lax.axis_index("tok")
     core, chip = device % CORES, device // CORES
-    ordered = context_weight.reshape(-1, 2, CORES, GROUPS, HD)
-    ordered = lax.dynamic_slice_in_dim(ordered, core, 1, 2)[:, :, 0]
-    ordered = ordered.transpose(0, 2, 1, 3).reshape(-1, GROUPS * 2 * HD)
-    a, own, left, right, opposite = gathered(ordered, device)
-
-    hidden, queries, upstream, _ = lax.optimization_barrier((hidden, queries, upstream, own))
+    a, first, own, left, right, opposite = gathered(context_weight, device)
+
+    hidden, queries, upstream, _ = lax.optimization_barrier((hidden, queries, upstream, first))
     other_hidden = swapped(hidden)
     q_other = swapped(half(queries, 1 - core, 1))
     u_other = swapped(half(upstream, 1 - core, 1))

time: 140 us -> 134 us (0.957)
  waiting for transfers between devices: 39.1 us -> 21.8 us
  starting transfers between devices: 50.2 us -> 59.2 us
  local copies, waits for them, and re-layouts: 4.39 us -> 5.89 us
    all_to_all x1, waiting for transfers between devices: 7.95 us -> 0.01 us  [gathered(): lax.all_to_all(piece, 'tok', 0, 0, axis_index_groups=[list(g) for g in gr...]
    ppermute x4, starting transfers between devices: 20 us -> 27.1 us  [swapped(): return lax.ppermute(block, 'tok', [(i, i ^ 1) for i in range(count)])]
    ppermute x6, waiting for transfers between devices: 18.1 us -> 13 us  [shifted(): return lax.ppermute(block, 'tok', route)]
    ppermute x3, waiting for transfers between devices: 11.9 us -> 8.08 us  [turned(): return lax.ppermute(own, 'tok', route)]
    dynamic_slice x2, local copies, waits for them, and re-layouts: 1.12 us -> 3.06 us  [half(): return lax.dynamic_slice_in_dim(block, index * size, size, axis)]
    ppermute x3, starting transfers between devices: 8.68 us -> 10.4 us  [turned(): return lax.ppermute(own, 'tok', route)]
  transfers between devices with their start and end apart: 14 -> 14, of which waited for: 8 -> 7; matrix products, arithmetic and copies ran while one was open for 1% -> 2% of each run, Pallas kernels for 0% -> 0%
where the time goes in v5:
time: 134 us; the launch traced here: 133 us
  starting transfers between devices  59.2 us (44%)
  blocking collectives  27.9 us (21%)
  waiting for transfers between devices  21.8 us (16%)
  Pallas kernels  16.8 us (13%)
  local copies, waits for them, and re-layouts  5.89 us (4%)
    all_to_all x1, blocking collectives, gathered(): first = lax.all_to_all(piece, 'fsdp', 0, 0)  27.9 us
    ppermute x4, starting transfers between devices, swapped(): return lax.ppermute(block, 'tok', [(i, i ^ 1) for i in range(count)])  27.1 us
    ppermute x6, starting transfers between devices, shifted(): return lax.ppermute(block, 'tok', route)  17.4 us
    ppermute x6, waiting for transfers between devices, shifted(): return lax.ppermute(block, 'tok', route)  13 us
    pallas_call x1, Pallas kernels, attention(): pl.pallas_call(attention_kernel, grid_spec=pltpu.PrefetchScalarGridSpec(n...  12.6 us
    ppermute x3, starting transfers between devices, turned(): return lax.ppermute(own, 'tok', route)  10.4 us
    ppermute x3, waiting for transfers between devices, turned(): return lax.ppermute(own, 'tok', route)  8.08 us
    all_to_all x1, starting transfers between devices, gathered(): lax.all_to_all(piece, 'tok', 0, 0, axis_index_groups=[list(g) for g in gr...  4.21 us
  transfers between devices with their start and end apart: 14, of which 7 were waited for; matrix products, arithmetic and copies ran while one was open for 2% of the time, Pallas kernels for 0%

profile of v5, /device:TPU:7, one launch (start us, length us, event | category | flops | bytes accessed | tf_op | source)
XLA Modules:
  0.0 132.6 jit_solution(7681854432107887353)
XLA Ops:
  0.6 0.0 copy-start
  0.7 1.0 copy-done
  1.8 27.9 %all_to_all.10 = bf16[16,16,512]{2,1,0:T(8,128)(2,1)S(1)} all-to-all(bf16[16,16,512]{2,1,0:T(8,128)(2,1)S(1)} %broadcast_in_dim.14), channel_id=1, replica_groups=mesh['tok'=32,'fsdp'=16] {'fsdp'}, dimensions={0} | all-to-all | bytes 524288 | tf_op jit(solution)/shard_map/all_to_all | solution.py:342
  29.7 1.1 broadcast_in_dim.15
  30.8 4.2 %all-to-all-start.1 = ((bf16[4,16,16,512]{3,2,1,0:T(8,128)(2,1)}), bf16[4,16,16,512]{3,2,1,0:T(8,128)(2,1)S(1)}, u32[]{:S(2)}, u32[]{:S(2)}) async-start(bf16[4,16,16,512]{3,2,1,0:T(8,128)(2,1)} %broadcast_in_dim.15), calls=%async_computation.1 | async-start | bytes 2097152 | tf_op jit(solution)/shard_map/all_to_all | solution.py:348
  35.0 0.0 copy-start.1
  35.0 2.0 %constant_dynamic-slice_fusion = bf16[128,2048]{1,0:T(8,128)(2,1)} fusion(bf16[128,4096]{1,0:T(8,128)(2,1)} %u_mine, s32[]{:T(128)S(6)} %select_n.45), kind=kLoop, calls=%fused_computation.1 | loop fusion | bytes 1048580 | tf_op jit(solution)/shard_map/dynamic_slice | solution.py:45
  37.0 8.3 %collective-permute-start.1 = (bf16[128,2048]{1,0:T(8,128)(2,1)}, bf16[128,2048]{1,0:T(8,128)(2,1)S(1)}, u32[]{:S(2)}, u32[]{:S(2)}) collective-permute-start(bf16[128,2048]{1,0:T(8,128)(2,1)} %constant_dynamic-slice_fusion), channel_id=1, source_target_pairs={{0,16},{16,0},{32,48},{48,32},{64,80},{80,64},{96,112},{112,96},{1... | collective-permute-start | bytes 1572872 | tf_op jit(solution)/shard_map/ppermute | solution.py:40
  45.3 0.0 all-to-all-done.1.own_ref
  45.3 5.2 %collective-permute-start.2 = (bf16[4,16,16,512]{3,2,1,0:T(8,128)(2,1)S(1)}, bf16[4,16,16,512]{3,2,1,0:T(8,128)(2,1)S(1)}, u32[]{:S(2)}, u32[]{:S(2)}) collective-permute-start(bf16[4,16,16,512]{3,2,1,0:T(8,128)(2,1)S(1)} %all-to-all-done.1.own_ref), channel_id=1, source_target_pairs={{0,256},{16,80},{32,288},{48,112},{64,320},{80,16},{96,352},{112,4... | collective-permute-start | bytes 3145736 | tf_op jit(solution)/shard_map/ppermute | solution.py:355
  50.5 0.0 copy-done.1
  50.5 7.2 %collective-permute-start.3 = (bf16[128,4096]{1,0:T(8,128)(2,1)S(1)}, bf16[128,4096]{1,0:T(8,128)(2,1)S(1)}, u32[]{:S(2)}, u32[]{:S(2)}) collective-permute-start(bf16[128,4096]{1,0:T(8,128)(2,1)S(1)} %copy-done.1), channel_id=1, source_target_pairs={{0,16},{16,0},{32,48},{48,32},{64,80},{80,64},{96,112},{112,96},{1... | collective-permute-start | bytes 3145736 | tf_op jit(solution)/shard_map/ppermute | solution.py:40
  57.7 2.6 %collective-permute-start.5 = (bf16[4,16,16,512]{3,2,1,0:T(8,128)(2,1)S(1)}, bf16[4,16,16,512]{3,2,1,0:T(8,128)(2,1)S(1)}, u32[]{:S(2)}, u32[]{:S(2)}) collective-permute-start(bf16[4,16,16,512]{3,2,1,0:T(8,128)(2,1)S(1)} %all-to-all-done.1.own_ref), channel_id=1, source_target_pairs={{0,384},{16,112},{32,416},{48,16},{64,448},{80,48},{96,480},{112,8... | collective-permute-start | bytes 3145736 | tf_op jit(solution)/shard_map/ppermute | solution.py:355
  60.4 2.6 %collective-permute-start.4 = (bf16[4,16,16,512]{3,2,1,0:T(8,128)(2,1)S(1)}, bf16[4,16,16,512]{3,2,1,0:T(8,128)(2,1)S(1)}, u32[]{:S(2)}, u32[]{:S(2)}) collective-permute-start(bf16[4,16,16,512]{3,2,1,0:T(8,128)(2,1)S(1)} %all-to-all-done.1.own_ref), channel_id=1, source_target_pairs={{0,128},{16,48},{32,160},{48,80},{64,192},{80,112},{96,224},{112,1... | collective-permute-start | bytes 3145736 | tf_op jit(solution)/shard_map/ppermute | solution.py:355
  63.0 1.1 constant_dynamic-slice_fusion.1
  64.1 0.0 collective-permute-done.1.u_other
  64.1 3.7 %collective-permute-start = (bf16[128,2048]{1,0:T(8,128)(2,1)S(1)}, bf16[128,2048]{1,0:T(8,128)(2,1)S(1)}, u32[]{:S(2)}, u32[]{:S(2)}) collective-permute-start(bf16[128,2048]{1,0:T(8,128)(2,1)S(1)} %constant_dynamic-slice_fusion.1), channel_id=1, source_target_pairs={{0,16},{16,0},{32,48},{48,32},{64,80},{80,64},{96,112},{112,96},{1... | collective-permute-start | bytes 1572872 | tf_op jit(solution)/shard_map/ppermute | solution.py:40
  67.8 0.0 copy-start.4
  67.8 0.6 copy-done.4
  68.5 0.1 pad_add_fusion.place_ref
  68.5 0.0 copy-start.2
  68.5 0.0 copy-start.3
  68.5 0.8 collective-permute-done.q_other
  69.3 0.0 collective-permute-done.2.far_ref
  69.3 0.0 collective-permute-done.3.other_ref
  69.3 5.1 %collective-permute-done.5.right_ref = bf16[4,16,16,512]{3,2,1,0:T(8,128)(2,1)S(1)} collective-permute-done((bf16[4,16,16,512]{3,2,1,0:T(8,128)(2,1)S(1)}, bf16[4,16,16,512]{3,2,1,0:T(8,128)(2,1)S(1)}, u32[]{:S(2)}, u32[]{:S(2)}) %collective-permute-start.5) | collective-permute-done | bytes 1048608 | tf_op jit(solution)/shard_map/ppermute | solution.py:355
  74.4 3.0 %collective-permute-done.4.left_ref = bf16[4,16,16,512]{3,2,1,0:T(8,128)(2,1)S(1)} collective-permute-done((bf16[4,16,16,512]{3,2,1,0:T(8,128)(2,1)S(1)}, bf16[4,16,16,512]{3,2,1,0:T(8,128)(2,1)S(1)}, u32[]{:S(2)}, u32[]{:S(2)}) %collective-permute-start.4) | collective-permute-done | bytes 1048608 | tf_op jit(solution)/shard_map/ppermute | solution.py:355
  77.4 2.4 %projection.1.here_ref = bf16[256,512]{1,0:T(8,128)(2,1)S(1)} custom-call(s32[19]{0:T(128)S(1)} %pad_add_fusion.place_ref, bf16[128,4096]{1,0:T(8,128)(2,1)S(1)} %copy-done.1, bf16[128,4096]{1,0:T(8,128)(2,1)S(1)} %collective-permute-done.3.other_ref, bf16[4,16,16,512]{3,2,1,0:T(8,128)(2,1)S(1)} %all-to-all-done.1.own_ref, ...), custom_call_target="tpu_custom_call" | custom-call | flops 1073741824 | bytes 6291456 | tf_op jit(solution)/shard_map/projection/pallas_call | solution.py:301
  79.8 1.9 %collective-permute-start.7 = (bf16[256,512]{1,0:T(8,128)(2,1)S(1)}, bf16[256,512]{1,0:T(8,128)(2,1)S(1)}, u32[]{:S(2)}, u32[]{:S(2)}) collective-permute-start(bf16[256,512]{1,0:T(8,128)(2,1)S(1)} %projection.1.here_ref), channel_id=1, source_target_pairs={{0,32},{16,48},{32,64},{48,80},{64,96},{80,112},{96,128},{112,144}... | collective-permute-start | bytes 786440 | tf_op jit(solution)/shard_map/ppermute | solution.py:35
  81.7 2.5 %collective-permute-start.6 = (bf16[256,512]{1,0:T(8,128)(2,1)S(1)}, bf16[256,512]{1,0:T(8,128)(2,1)S(1)}, u32[]{:S(2)}, u32[]{:S(2)}) collective-permute-start(bf16[256,512]{1,0:T(8,128)(2,1)S(1)} %projection.1.here_ref), channel_id=1, source_target_pairs={{0,64},{16,80},{32,96},{48,112},{64,128},{80,144},{96,160},{112,17... | collective-permute-start | bytes 786440 | tf_op jit(solution)/shard_map/ppermute | solution.py:35
  84.3 5.4 %collective-permute-done.7.near_ref = bf16[256,512]{1,0:T(8,128)(2,1)S(1)} collective-permute-done((bf16[256,512]{1,0:T(8,128)(2,1)S(1)}, bf16[256,512]{1,0:T(8,128)(2,1)S(1)}, u32[]{:S(2)}, u32[]{:S(2)}) %collective-permute-start.7) | collective-permute-done | bytes 262176 | tf_op jit(solution)/shard_map/ppermute | solution.py:35
  89.6 2.6 %collective-permute-done.6.far_ref = bf16[256,512]{1,0:T(8,128)(2,1)S(1)} collective-permute-done((bf16[256,512]{1,0:T(8,128)(2,1)S(1)}, bf16[256,512]{1,0:T(8,128)(2,1)S(1)}, u32[]{:S(2)}, u32[]{:S(2)}) %collective-permute-start.6) | collective-permute-done | bytes 262176 | tf_op jit(solution)/shard_map/ppermute | solution.py:35
  92.2 0.0 copy-done.2
  92.2 0.0 copy-done.3
  92.2 12.6 %attention.1 = (f32[16,128]{1,0:T(8,128)S(1)}, bf16[128,2048]{1,0:T(8,128)(2,1)S(1)}, bf16[128,2816]{1,0:T(8,128)(2,1)S(1)}, f32[128,512]{1,0:T(8,128)S(1)}, bf1...) custom-call(s32[19]{0:T(128)S(1)} %pad_add_fusion.place_ref, ...), custom_call_target="tpu_custom_call" | custom-call | flops 4026531840 | bytes 8388608 | tf_op jit(solution)/shard_map/attention/pallas_call | solution.py:170
  104.8 7.9 %collective-permute-start.8 = (bf16[128,2816]{1,0:T(8,128)(2,1)S(1)}, bf16[128,2816]{1,0:T(8,128)(2,1)S(1)}, u32[]{:S(2)}, u32[]{:S(2)}) collective-permute-start(bf16[128,2816]{1,0:T(8,128)(2,1)S(1)} %get-tuple-element.26), channel_id=1, source_target_pairs={{0,16},{16,0},{32,48},{48,32},{64,80},{80,64},{96,112},{112,96},{1... | collective-permute-start | bytes 2162696 | tf_op jit(solution)/shard_map/ppermute | solution.py:40
  112.7 3.5 %collective-permute-start.9 = (bf16[128,512]{1,0:T(8,128)(2,1)S(1)}, bf16[128,512]{1,0:T(8,128)(2,1)S(1)}, u32[]{:S(2)}, u32[]{:S(2)}) collective-permute-start(bf16[128,512]{1,0:T(8,128)(2,1)S(1)} %get-tuple-element.29), channel_id=1, source_target_pairs={{32,0},{48,16},{64,32},{80,48},{96,64},{112,80},{128,96},{144,112}... | collective-permute-start | bytes 393224 | tf_op jit(solution)/shard_map/ppermute | solution.py:35
  116.3 2.2 %collective-permute-start.10 = (bf16[128,512]{1,0:T(8,128)(2,1)S(1)}, bf16[128,512]{1,0:T(8,128)(2,1)S(1)}, u32[]{:S(2)}, u32[]{:S(2)}) collective-permute-start(bf16[128,512]{1,0:T(8,128)(2,1)S(1)} %get-tuple-element.30), channel_id=1, source_target_pairs={{64,0},{80,16},{96,32},{112,48},{128,64},{144,80},{160,96},{176,11... | collective-permute-start | bytes 393224 | tf_op jit(solution)/shard_map/ppermute | solution.py:35
  118.5 3.9 %collective-permute-start.11 = (bf16[128,512]{1,0:T(8,128)(2,1)S(1)}, bf16[128,512]{1,0:T(8,128)(2,1)S(1)}, u32[]{:S(2)}, u32[]{:S(2)}) collective-permute-start(bf16[128,512]{1,0:T(8,128)(2,1)S(1)} %get-tuple-element.31), channel_id=1, source_target_pairs={{32,16},{48,0},{64,48},{80,32},{96,80},{112,64},{128,112},{144,96}... | collective-permute-start | bytes 393224 | tf_op jit(solution)/shard_map/ppermute | solution.py:35
  122.3 3.4 %collective-permute-start.12 = (bf16[128,512]{1,0:T(8,128)(2,1)S(1)}, bf16[128,512]{1,0:T(8,128)(2,1)S(1)}, u32[]{:S(2)}, u32[]{:S(2)}) collective-permute-start(bf16[128,512]{1,0:T(8,128)(2,1)S(1)} %get-tuple-element.32), channel_id=1, source_target_pairs={{64,16},{80,0},{96,48},{112,32},{128,80},{144,64},{160,112},{176,9... | collective-permute-start | bytes 393224 | tf_op jit(solution)/shard_map/ppermute | solution.py:35
  125.7 0.0 collective-permute-done.9.near_mine
  125.7 0.0 collective-permute-done.10.far_mine
  125.7 0.5 collective-permute-done.11.near_other
  126.2 4.6 %collective-permute-done.12.far_other = bf16[128,512]{1,0:T(8,128)(2,1)S(1)} collective-permute-done((bf16[128,512]{1,0:T(8,128)(2,1)S(1)}, bf16[128,512]{1,0:T(8,128)(2,1)S(1)}, u32[]{:S(2)}, u32[]{:S(2)}) %collective-permute-start.12) | collective-permute-done | bytes 131104 | tf_op jit(solution)/shard_map/ppermute | solution.py:35
  130.8 0.0 collective-permute-done.8.from_core
  130.8 1.8 %finish.1 = (f32[32,128]{1,0:T(8,128)}, bf16[128,4096]{1,0:T(8,128)(2,1)}, bf16[128,1024]{1,0:T(8,128)(2,1)}) custom-call(s32[19]{0:T(128)S(1)} %pad_add_fusion.place_ref, bf16[128,2048]{1,0:T(8,128)(2,1)S(1)} %get-tuple-element.25.dq_mine, bf16[128,2816]{1,0:T(8,128)(2,1)S(1)} %collective-permute-done.8.from_core, ...), custom_call_target="tpu_custom_call" | custom-call | bytes 4194304 | tf_op jit(solution)/shard_map/finish/pallas_call | solution.py:250
  (7 shorter events, 0.1 us)
Async XLA Ops:
  0.6 1.0 copy-start
  30.8 14.5 %all-to-all-start.1 = ((bf16[4,16,16,512]{3,2,1,0:T(8,128)(2,1)}), bf16[4,16,16,512]{3,2,1,0:T(8,128)(2,1)S(1)}, u32[]{:S(2)}, u32[]{:S(2)}) async-start(bf16[4,16,16,512]{3,2,1,0:T(8,128)(2,1)} %broadcast_in_dim.15), calls=%async_computation.1 | async-start | bytes 2097152 | tf_op jit(solution)/shard_map/all_to_all | solution.py:348
  35.0 15.5 %copy-start.1 = (bf16[128,4096]{1,0:T(8,128)(2,1)S(1)}, bf16[128,4096]{1,0:T(8,128)(2,1)}, u32[]{:S(2)}) copy-start(bf16[128,4096]{1,0:T(8,128)(2,1)} %mine_ref) | copy-start | bytes 3145732
  37.0 27.1 %collective-permute-start.1 = (bf16[128,2048]{1,0:T(8,128)(2,1)}, bf16[128,2048]{1,0:T(8,128)(2,1)S(1)}, u32[]{:S(2)}, u32[]{:S(2)}) collective-permute-start(bf16[128,2048]{1,0:T(8,128)(2,1)} %constant_dynamic-slice_fusion), channel_id=1, source_target_pairs={{0,16},{16,0},{32,48},{48,32},{64,80},{80,64},{96,112},{112,96},{1... | collective-permute-start | bytes 1572872 | tf_op jit(solution)/shard_map/ppermute | solution.py:40
  45.3 24.0 %collective-permute-start.2 = (bf16[4,16,16,512]{3,2,1,0:T(8,128)(2,1)S(1)}, bf16[4,16,16,512]{3,2,1,0:T(8,128)(2,1)S(1)}, u32[]{:S(2)}, u32[]{:S(2)}) collective-permute-start(bf16[4,16,16,512]{3,2,1,0:T(8,128)(2,1)S(1)} %all-to-all-done.1.own_ref), channel_id=1, source_target_pairs={{0,256},{16,80},{32,288},{48,112},{64,320},{80,16},{96,352},{112,4... | collective-permute-start | bytes 3145736 | tf_op jit(solution)/shard_map/ppermute | solution.py:355
  50.5 18.8 %collective-permute-start.3 = (bf16[128,4096]{1,0:T(8,128)(2,1)S(1)}, bf16[128,4096]{1,0:T(8,128)(2,1)S(1)}, u32[]{:S(2)}, u32[]{:S(2)}) collective-permute-start(bf16[128,4096]{1,0:T(8,128)(2,1)S(1)} %copy-done.1), channel_id=1, source_target_pairs={{0,16},{16,0},{32,48},{48,32},{64,80},{80,64},{96,112},{112,96},{1... | collective-permute-start | bytes 3145736 | tf_op jit(solution)/shard_map/ppermute | solution.py:40
  57.7 16.7 %collective-permute-start.5 = (bf16[4,16,16,512]{3,2,1,0:T(8,128)(2,1)S(1)}, bf16[4,16,16,512]{3,2,1,0:T(8,128)(2,1)S(1)}, u32[]{:S(2)}, u32[]{:S(2)}) collective-permute-start(bf16[4,16,16,512]{3,2,1,0:T(8,128)(2,1)S(1)} %all-to-all-done.1.own_ref), channel_id=1, source_target_pairs={{0,384},{16,112},{32,416},{48,16},{64,448},{80,48},{96,480},{112,8... | collective-permute-start | bytes 3145736 | tf_op jit(solution)/shard_map/ppermute | solution.py:355
  60.4 17.0 %collective-permute-start.4 = (bf16[4,16,16,512]{3,2,1,0:T(8,128)(2,1)S(1)}, bf16[4,16,16,512]{3,2,1,0:T(8,128)(2,1)S(1)}, u32[]{:S(2)}, u32[]{:S(2)}) collective-permute-start(bf16[4,16,16,512]{3,2,1,0:T(8,128)(2,1)S(1)} %all-to-all-done.1.own_ref), channel_id=1, source_target_pairs={{0,128},{16,48},{32,160},{48,80},{64,192},{80,112},{96,224},{112,1... | collective-permute-start | bytes 3145736 | tf_op jit(solution)/shard_map/ppermute | solution.py:355
  64.1 5.2 %collective-permute-start = (bf16[128,2048]{1,0:T(8,128)(2,1)S(1)}, bf16[128,2048]{1,0:T(8,128)(2,1)S(1)}, u32[]{:S(2)}, u32[]{:S(2)}) collective-permute-start(bf16[128,2048]{1,0:T(8,128)(2,1)S(1)} %constant_dynamic-slice_fusion.1), channel_id=1, source_target_pairs={{0,16},{16,0},{32,48},{48,32},{64,80},{80,64},{96,112},{112,96},{1... | collective-permute-start | bytes 1572872 | tf_op jit(solution)/shard_map/ppermute | solution.py:40
  67.8 0.7 copy-start.4
  68.5 23.7 %copy-start.2 = (bf16[128,4096]{1,0:T(8,128)(2,1)S(1)}, bf16[128,4096]{1,0:T(8,128)(2,1)}, u32[]{:S(2)}) copy-start(bf16[128,4096]{1,0:T(8,128)(2,1)} %q_mine) | copy-start | bytes 3145732
  68.5 23.7 %copy-start.3 = (bf16[128,4096]{1,0:T(8,128)(2,1)S(1)}, bf16[128,4096]{1,0:T(8,128)(2,1)}, u32[]{:S(2)}) copy-start(bf16[128,4096]{1,0:T(8,128)(2,1)} %u_mine) | copy-start | bytes 3145732
  79.8 9.8 %collective-permute-start.7 = (bf16[256,512]{1,0:T(8,128)(2,1)S(1)}, bf16[256,512]{1,0:T(8,128)(2,1)S(1)}, u32[]{:S(2)}, u32[]{:S(2)}) collective-permute-start(bf16[256,512]{1,0:T(8,128)(2,1)S(1)} %projection.1.here_ref), channel_id=1, source_target_pairs={{0,32},{16,48},{32,64},{48,80},{64,96},{80,112},{96,128},{112,144}... | collective-permute-start | bytes 786440 | tf_op jit(solution)/shard_map/ppermute | solution.py:35
  81.7 10.5 %collective-permute-start.6 = (bf16[256,512]{1,0:T(8,128)(2,1)S(1)}, bf16[256,512]{1,0:T(8,128)(2,1)S(1)}, u32[]{:S(2)}, u32[]{:S(2)}) collective-permute-start(bf16[256,512]{1,0:T(8,128)(2,1)S(1)} %projection.1.here_ref), channel_id=1, source_target_pairs={{0,64},{16,80},{32,96},{48,112},{64,128},{80,144},{96,160},{112,17... | collective-permute-start | bytes 786440 | tf_op jit(solution)/shard_map/ppermute | solution.py:35
  104.8 26.0 %collective-permute-start.8 = (bf16[128,2816]{1,0:T(8,128)(2,1)S(1)}, bf16[128,2816]{1,0:T(8,128)(2,1)S(1)}, u32[]{:S(2)}, u32[]{:S(2)}) collective-permute-start(bf16[128,2816]{1,0:T(8,128)(2,1)S(1)} %get-tuple-element.26), channel_id=1, source_target_pairs={{0,16},{16,0},{32,48},{48,32},{64,80},{80,64},{96,112},{112,96},{1... | collective-permute-start | bytes 2162696 | tf_op jit(solution)/shard_map/ppermute | solution.py:40
  112.7 13.0 %collective-permute-start.9 = (bf16[128,512]{1,0:T(8,128)(2,1)S(1)}, bf16[128,512]{1,0:T(8,128)(2,1)S(1)}, u32[]{:S(2)}, u32[]{:S(2)}) collective-permute-start(bf16[128,512]{1,0:T(8,128)(2,1)S(1)} %get-tuple-element.29), channel_id=1, source_target_pairs={{32,0},{48,16},{64,32},{80,48},{96,64},{112,80},{128,96},{144,112}... | collective-permute-start | bytes 393224 | tf_op jit(solution)/shard_map/ppermute | solution.py:35
  116.3 9.5 %collective-permute-start.10 = (bf16[128,512]{1,0:T(8,128)(2,1)S(1)}, bf16[128,512]{1,0:T(8,128)(2,1)S(1)}, u32[]{:S(2)}, u32[]{:S(2)}) collective-permute-start(bf16[128,512]{1,0:T(8,128)(2,1)S(1)} %get-tuple-element.30), channel_id=1, source_target_pairs={{64,0},{80,16},{96,32},{112,48},{128,64},{144,80},{160,96},{176,11... | collective-permute-start | bytes 393224 | tf_op jit(solution)/shard_map/ppermute | solution.py:35
  118.5 7.7 %collective-permute-start.11 = (bf16[128,512]{1,0:T(8,128)(2,1)S(1)}, bf16[128,512]{1,0:T(8,128)(2,1)S(1)}, u32[]{:S(2)}, u32[]{:S(2)}) collective-permute-start(bf16[128,512]{1,0:T(8,128)(2,1)S(1)} %get-tuple-element.31), channel_id=1, source_target_pairs={{32,16},{48,0},{64,48},{80,32},{96,80},{112,64},{128,112},{144,96}... | collective-permute-start | bytes 393224 | tf_op jit(solution)/shard_map/ppermute | solution.py:35
  122.3 8.4 %collective-permute-start.12 = (bf16[128,512]{1,0:T(8,128)(2,1)S(1)}, bf16[128,512]{1,0:T(8,128)(2,1)S(1)}, u32[]{:S(2)}, u32[]{:S(2)}) collective-permute-start(bf16[128,512]{1,0:T(8,128)(2,1)S(1)} %get-tuple-element.32), channel_id=1, source_target_pairs={{64,16},{80,0},{96,48},{112,32},{128,80},{144,64},{160,112},{176,9... | collective-permute-start | bytes 393224 | tf_op jit(solution)/shard_map/ppermute | solution.py:35

commit v6 on v5

--- a/solution.py
+++ b/solution.py
@@ -23,6 +23,7 @@
 SHARDS = 16
 SLICES = 16
 ROWS = 16
+PARTS = 2
 SCALE = 1.0 / math.sqrt(HD)
 LOG2E = math.log2(math.e)
 
@@ -268,23 +269,31 @@
     core, a = place_ref[0], place_ref[2]
     pieces = ((own_ref, 0), (left_ref, 3), (right_ref, 1), (far_ref, 2))
 
+    step = SHARDS // PARTS
     copies = [
-        pltpu.make_async_copy(
-            ref.at[b], weight.at[lax.rem(a + turn, 4) * 4 + b], sems.at[i, b]
-        )
-        for i, (ref, turn) in enumerate(pieces)
-        for b in range(4)
+        [
+            pltpu.make_async_copy(
+                ref.at[b, pl.ds(part * step, step)],
+                weight.at[lax.rem(a + turn, 4) * 4 + b, pl.ds(part * step, step)],
+                sems.at[part, i, b],
+            )
+            for i, (ref, turn) in enumerate(pieces)
+            for b in range(4)
+        ]
+        for part in range(PARTS)
     ]
-    for copy in copies:
-        copy.start()
+    for part in copies:
+        for copy in part:
+            copy.start()
     mine = pl.multiple_of(core * BLOCK, BLOCK)
     tokens[pl.ds(mine, BLOCK), :] = mine_ref[...]
     tokens[pl.ds(BLOCK - mine, BLOCK), :] = other_ref[...]
-    for copy in copies:
-        copy.wait()
     total = jnp.zeros(out_ref.shape, jnp.float32)
     depth = SLICES * ROWS
     for z in range(SHARDS):
+        if z % step == 0:
+            for copy in copies[z // step]:
+                copy.wait()
         total += jnp.dot(
             tokens[:, z * depth : (z + 1) * depth],
             weight[:, z].reshape(depth, out_ref.shape[1]),
@@ -306,7 +315,7 @@
         scratch_shapes=[
             pltpu.VMEM((CHIP, depth), jnp.bfloat16),
             pltpu.VMEM((SLICES, SHARDS, ROWS, width), jnp.bfloat16),
-            pltpu.SemaphoreType.DMA((4, 4)),
+            pltpu.SemaphoreType.DMA((PARTS, 4, 4)),
         ],
         compiler_params=pltpu.CompilerParams(vmem_limit_bytes=32 * 2**20),
         cost_estimate=pl.CostEstimate(

time: 134 us -> 139 us (1.037)
  Pallas kernels: 16.8 us -> 22.1 us
    pallas_call x1, Pallas kernels: 2.4 us -> 7.73 us  [projection(): pl.pallas_call(projection_kernel, in_specs=[pl.BlockSpec(memory_space=plt...]
where the time goes in v6:
time: 139 us; the launch traced here: 138 us
  starting transfers between devices  59.2 us (43%)
  blocking collectives  27.9 us (20%)
  Pallas kernels  22.1 us (16%)
  waiting for transfers between devices  21.8 us (16%)
  local copies, waits for them, and re-layouts  5.89 us (4%)
    all_to_all x1, blocking collectives, gathered(): first = lax.all_to_all(piece, 'fsdp', 0, 0)  27.9 us
    ppermute x4, starting transfers between devices, swapped(): return lax.ppermute(block, 'tok', [(i, i ^ 1) for i in range(count)])  27.1 us
    ppermute x6, starting transfers between devices, shifted(): return lax.ppermute(block, 'tok', route)  17.4 us
    ppermute x6, waiting for transfers between devices, shifted(): return lax.ppermute(block, 'tok', route)  13 us
    pallas_call x1, Pallas kernels, attention(): pl.pallas_call(attention_kernel, grid_spec=pltpu.PrefetchScalarGridSpec(n...  12.6 us
    ppermute x3, starting transfers between devices, turned(): return lax.ppermute(own, 'tok', route)  10.4 us
    ppermute x3, waiting for transfers between devices, turned(): return lax.ppermute(own, 'tok', route)  8.08 us
    pallas_call x1, Pallas kernels, projection(): pl.pallas_call(projection_kernel, in_specs=[pl.BlockSpec(memory_space=plt...  7.73 us
  transfers between devices with their start and end apart: 14, of which 7 were waited for; matrix products, arithmetic and copies ran while one was open for 2% of the time, Pallas kernels for 0%

profile of v6, /device:TPU:7, one launch (start us, length us, event | category | flops | bytes accessed | tf_op | source)
XLA Modules:
  0.0 137.9 jit_solution(14478554035888617354)
XLA Ops:
  0.6 0.0 copy-start
  0.7 1.0 copy-done
  1.8 27.9 %all_to_all.10 = bf16[16,16,512]{2,1,0:T(8,128)(2,1)S(1)} all-to-all(bf16[16,16,512]{2,1,0:T(8,128)(2,1)S(1)} %broadcast_in_dim.14), channel_id=1, replica_groups=mesh['tok'=32,'fsdp'=16] {'fsdp'}, dimensions={0} | all-to-all | bytes 524288 | tf_op jit(solution)/shard_map/all_to_all | solution.py:351
  29.7 1.1 broadcast_in_dim.15
  30.8 4.2 %all-to-all-start.1 = ((bf16[4,16,16,512]{3,2,1,0:T(8,128)(2,1)}), bf16[4,16,16,512]{3,2,1,0:T(8,128)(2,1)S(1)}, u32[]{:S(2)}, u32[]{:S(2)}) async-start(bf16[4,16,16,512]{3,2,1,0:T(8,128)(2,1)} %broadcast_in_dim.15), calls=%async_computation.1 | async-start | bytes 2097152 | tf_op jit(solution)/shard_map/all_to_all | solution.py:357
  35.0 0.0 copy-start.1
  35.0 2.0 %constant_dynamic-slice_fusion = bf16[128,2048]{1,0:T(8,128)(2,1)} fusion(bf16[128,4096]{1,0:T(8,128)(2,1)} %u_mine, s32[]{:T(128)S(6)} %select_n.45), kind=kLoop, calls=%fused_computation.1 | loop fusion | bytes 1048580 | tf_op jit(solution)/shard_map/dynamic_slice | solution.py:46
  37.0 8.3 %collective-permute-start.1 = (bf16[128,2048]{1,0:T(8,128)(2,1)}, bf16[128,2048]{1,0:T(8,128)(2,1)S(1)}, u32[]{:S(2)}, u32[]{:S(2)}) collective-permute-start(bf16[128,2048]{1,0:T(8,128)(2,1)} %constant_dynamic-slice_fusion), channel_id=1, source_target_pairs={{0,16},{16,0},{32,48},{48,32},{64,80},{80,64},{96,112},{112,96},{1... | collective-permute-start | bytes 1572872 | tf_op jit(solution)/shard_map/ppermute | solution.py:41
  45.3 0.0 all-to-all-done.1.own_ref
  45.3 5.2 %collective-permute-start.2 = (bf16[4,16,16,512]{3,2,1,0:T(8,128)(2,1)S(1)}, bf16[4,16,16,512]{3,2,1,0:T(8,128)(2,1)S(1)}, u32[]{:S(2)}, u32[]{:S(2)}) collective-permute-start(bf16[4,16,16,512]{3,2,1,0:T(8,128)(2,1)S(1)} %all-to-all-done.1.own_ref), channel_id=1, source_target_pairs={{0,256},{16,80},{32,288},{48,112},{64,320},{80,16},{96,352},{112,4... | collective-permute-start | bytes 3145736 | tf_op jit(solution)/shard_map/ppermute | solution.py:364
  50.5 0.0 copy-done.1
  50.5 7.2 %collective-permute-start.3 = (bf16[128,4096]{1,0:T(8,128)(2,1)S(1)}, bf16[128,4096]{1,0:T(8,128)(2,1)S(1)}, u32[]{:S(2)}, u32[]{:S(2)}) collective-permute-start(bf16[128,4096]{1,0:T(8,128)(2,1)S(1)} %copy-done.1), channel_id=1, source_target_pairs={{0,16},{16,0},{32,48},{48,32},{64,80},{80,64},{96,112},{112,96},{1... | collective-permute-start | bytes 3145736 | tf_op jit(solution)/shard_map/ppermute | solution.py:41
  57.7 2.6 %collective-permute-start.5 = (bf16[4,16,16,512]{3,2,1,0:T(8,128)(2,1)S(1)}, bf16[4,16,16,512]{3,2,1,0:T(8,128)(2,1)S(1)}, u32[]{:S(2)}, u32[]{:S(2)}) collective-permute-start(bf16[4,16,16,512]{3,2,1,0:T(8,128)(2,1)S(1)} %all-to-all-done.1.own_ref), channel_id=1, source_target_pairs={{0,384},{16,112},{32,416},{48,16},{64,448},{80,48},{96,480},{112,8... | collective-permute-start | bytes 3145736 | tf_op jit(solution)/shard_map/ppermute | solution.py:364
  60.4 2.6 %collective-permute-start.4 = (bf16[4,16,16,512]{3,2,1,0:T(8,128)(2,1)S(1)}, bf16[4,16,16,512]{3,2,1,0:T(8,128)(2,1)S(1)}, u32[]{:S(2)}, u32[]{:S(2)}) collective-permute-start(bf16[4,16,16,512]{3,2,1,0:T(8,128)(2,1)S(1)} %all-to-all-done.1.own_ref), channel_id=1, source_target_pairs={{0,128},{16,48},{32,160},{48,80},{64,192},{80,112},{96,224},{112,1... | collective-permute-start | bytes 3145736 | tf_op jit(solution)/shard_map/ppermute | solution.py:364
  63.0 1.1 constant_dynamic-slice_fusion.1
  64.1 0.0 collective-permute-done.1.u_other
  64.1 3.7 %collective-permute-start = (bf16[128,2048]{1,0:T(8,128)(2,1)S(1)}, bf16[128,2048]{1,0:T(8,128)(2,1)S(1)}, u32[]{:S(2)}, u32[]{:S(2)}) collective-permute-start(bf16[128,2048]{1,0:T(8,128)(2,1)S(1)} %constant_dynamic-slice_fusion.1), channel_id=1, source_target_pairs={{0,16},{16,0},{32,48},{48,32},{64,80},{80,64},{96,112},{112,96},{1... | collective-permute-start | bytes 1572872 | tf_op jit(solution)/shard_map/ppermute | solution.py:41
  67.8 0.0 copy-start.4
  67.8 0.6 copy-done.4
  68.5 0.1 pad_add_fusion.place_ref
  68.5 0.0 copy-start.2
  68.5 0.0 copy-start.3
  68.5 0.8 collective-permute-done.q_other
  69.3 0.0 collective-permute-done.2.far_ref
  69.3 0.0 collective-permute-done.3.other_ref
  69.3 5.1 %collective-permute-done.5.right_ref = bf16[4,16,16,512]{3,2,1,0:T(8,128)(2,1)S(1)} collective-permute-done((bf16[4,16,16,512]{3,2,1,0:T(8,128)(2,1)S(1)}, bf16[4,16,16,512]{3,2,1,0:T(8,128)(2,1)S(1)}, u32[]{:S(2)}, u32[]{:S(2)}) %collective-permute-start.5) | collective-permute-done | bytes 1048608 | tf_op jit(solution)/shard_map/ppermute | solution.py:364
  74.4 3.0 %collective-permute-done.4.left_ref = bf16[4,16,16,512]{3,2,1,0:T(8,128)(2,1)S(1)} collective-permute-done((bf16[4,16,16,512]{3,2,1,0:T(8,128)(2,1)S(1)}, bf16[4,16,16,512]{3,2,1,0:T(8,128)(2,1)S(1)}, u32[]{:S(2)}, u32[]{:S(2)}) %collective-permute-start.4) | collective-permute-done | bytes 1048608 | tf_op jit(solution)/shard_map/ppermute | solution.py:364
  77.4 7.7 %projection.1.here_ref = bf16[256,512]{1,0:T(8,128)(2,1)S(1)} custom-call(s32[19]{0:T(128)S(1)} %pad_add_fusion.place_ref, bf16[128,4096]{1,0:T(8,128)(2,1)S(1)} %copy-done.1, bf16[128,4096]{1,0:T(8,128)(2,1)S(1)} %collective-permute-done.3.other_ref, bf16[4,16,16,512]{3,2,1,0:T(8,128)(2,1)S(1)} %all-to-all-done.1.own_ref, ...), custom_call_target="tpu_custom_call" | custom-call | flops 1073741824 | bytes 6291456 | tf_op jit(solution)/shard_map/projection/pallas_call | solution.py:310
  85.1 1.9 %collective-permute-start.7 = (bf16[256,512]{1,0:T(8,128)(2,1)S(1)}, bf16[256,512]{1,0:T(8,128)(2,1)S(1)}, u32[]{:S(2)}, u32[]{:S(2)}) collective-permute-start(bf16[256,512]{1,0:T(8,128)(2,1)S(1)} %projection.1.here_ref), channel_id=1, source_target_pairs={{0,32},{16,48},{32,64},{48,80},{64,96},{80,112},{96,128},{112,144}... | collective-permute-start | bytes 786440 | tf_op jit(solution)/shard_map/ppermute | solution.py:36
  87.1 2.5 %collective-permute-start.6 = (bf16[256,512]{1,0:T(8,128)(2,1)S(1)}, bf16[256,512]{1,0:T(8,128)(2,1)S(1)}, u32[]{:S(2)}, u32[]{:S(2)}) collective-permute-start(bf16[256,512]{1,0:T(8,128)(2,1)S(1)} %projection.1.here_ref), channel_id=1, source_target_pairs={{0,64},{16,80},{32,96},{48,112},{64,128},{80,144},{96,160},{112,17... | collective-permute-start | bytes 786440 | tf_op jit(solution)/shard_map/ppermute | solution.py:36
  89.6 5.4 %collective-permute-done.7.near_ref = bf16[256,512]{1,0:T(8,128)(2,1)S(1)} collective-permute-done((bf16[256,512]{1,0:T(8,128)(2,1)S(1)}, bf16[256,512]{1,0:T(8,128)(2,1)S(1)}, u32[]{:S(2)}, u32[]{:S(2)}) %collective-permute-start.7) | collective-permute-done | bytes 262176 | tf_op jit(solution)/shard_map/ppermute | solution.py:36
  94.9 2.6 %collective-permute-done.6.far_ref = bf16[256,512]{1,0:T(8,128)(2,1)S(1)} collective-permute-done((bf16[256,512]{1,0:T(8,128)(2,1)S(1)}, bf16[256,512]{1,0:T(8,128)(2,1)S(1)}, u32[]{:S(2)}, u32[]{:S(2)}) %collective-permute-start.6) | collective-permute-done | bytes 262176 | tf_op jit(solution)/shard_map/ppermute | solution.py:36
  97.5 0.0 copy-done.2
  97.5 0.0 copy-done.3
  97.5 12.6 %attention.1 = (f32[16,128]{1,0:T(8,128)S(1)}, bf16[128,2048]{1,0:T(8,128)(2,1)S(1)}, bf16[128,2816]{1,0:T(8,128)(2,1)S(1)}, f32[128,512]{1,0:T(8,128)S(1)}, bf1...) custom-call(s32[19]{0:T(128)S(1)} %pad_add_fusion.place_ref, ...), custom_call_target="tpu_custom_call" | custom-call | flops 4026531840 | bytes 8388608 | tf_op jit(solution)/shard_map/attention/pallas_call | solution.py:171
  110.1 7.9 %collective-permute-start.8 = (bf16[128,2816]{1,0:T(8,128)(2,1)S(1)}, bf16[128,2816]{1,0:T(8,128)(2,1)S(1)}, u32[]{:S(2)}, u32[]{:S(2)}) collective-permute-start(bf16[128,2816]{1,0:T(8,128)(2,1)S(1)} %get-tuple-element.26), channel_id=1, source_target_pairs={{0,16},{16,0},{32,48},{48,32},{64,80},{80,64},{96,112},{112,96},{1... | collective-permute-start | bytes 2162696 | tf_op jit(solution)/shard_map/ppermute | solution.py:41
  118.0 3.5 %collective-permute-start.9 = (bf16[128,512]{1,0:T(8,128)(2,1)S(1)}, bf16[128,512]{1,0:T(8,128)(2,1)S(1)}, u32[]{:S(2)}, u32[]{:S(2)}) collective-permute-start(bf16[128,512]{1,0:T(8,128)(2,1)S(1)} %get-tuple-element.29), channel_id=1, source_target_pairs={{32,0},{48,16},{64,32},{80,48},{96,64},{112,80},{128,96},{144,112}... | collective-permute-start | bytes 393224 | tf_op jit(solution)/shard_map/ppermute | solution.py:36
  121.6 2.2 %collective-permute-start.10 = (bf16[128,512]{1,0:T(8,128)(2,1)S(1)}, bf16[128,512]{1,0:T(8,128)(2,1)S(1)}, u32[]{:S(2)}, u32[]{:S(2)}) collective-permute-start(bf16[128,512]{1,0:T(8,128)(2,1)S(1)} %get-tuple-element.30), channel_id=1, source_target_pairs={{64,0},{80,16},{96,32},{112,48},{128,64},{144,80},{160,96},{176,11... | collective-permute-start | bytes 393224 | tf_op jit(solution)/shard_map/ppermute | solution.py:36
  123.8 3.9 %collective-permute-start.11 = (bf16[128,512]{1,0:T(8,128)(2,1)S(1)}, bf16[128,512]{1,0:T(8,128)(2,1)S(1)}, u32[]{:S(2)}, u32[]{:S(2)}) collective-permute-start(bf16[128,512]{1,0:T(8,128)(2,1)S(1)} %get-tuple-element.31), channel_id=1, source_target_pairs={{32,16},{48,0},{64,48},{80,32},{96,80},{112,64},{128,112},{144,96}... | collective-permute-start | bytes 393224 | tf_op jit(solution)/shard_map/ppermute | solution.py:36
  127.6 3.4 %collective-permute-start.12 = (bf16[128,512]{1,0:T(8,128)(2,1)S(1)}, bf16[128,512]{1,0:T(8,128)(2,1)S(1)}, u32[]{:S(2)}, u32[]{:S(2)}) collective-permute-start(bf16[128,512]{1,0:T(8,128)(2,1)S(1)} %get-tuple-element.32), channel_id=1, source_target_pairs={{64,16},{80,0},{96,48},{112,32},{128,80},{144,64},{160,112},{176,9... | collective-permute-start | bytes 393224 | tf_op jit(solution)/shard_map/ppermute | solution.py:36
  131.0 0.0 collective-permute-done.9.near_mine
  131.1 0.0 collective-permute-done.10.far_mine
  131.1 0.5 collective-permute-done.11.near_other
  131.5 4.6 %collective-permute-done.12.far_other = bf16[128,512]{1,0:T(8,128)(2,1)S(1)} collective-permute-done((bf16[128,512]{1,0:T(8,128)(2,1)S(1)}, bf16[128,512]{1,0:T(8,128)(2,1)S(1)}, u32[]{:S(2)}, u32[]{:S(2)}) %collective-permute-start.12) | collective-permute-done | bytes 131104 | tf_op jit(solution)/shard_map/ppermute | solution.py:36
  136.1 0.0 collective-permute-done.8.from_core
  136.1 1.8 %finish.1 = (f32[32,128]{1,0:T(8,128)}, bf16[128,4096]{1,0:T(8,128)(2,1)}, bf16[128,1024]{1,0:T(8,128)(2,1)}) custom-call(s32[19]{0:T(128)S(1)} %pad_add_fusion.place_ref, bf16[128,2048]{1,0:T(8,128)(2,1)S(1)} %get-tuple-element.25.dq_mine, bf16[128,2816]{1,0:T(8,128)(2,1)S(1)} %collective-permute-done.8.from_core, ...), custom_call_target="tpu_custom_call" | custom-call | bytes 4194304 | tf_op jit(solution)/shard_map/finish/pallas_call | solution.py:251
  (7 shorter events, 0.1 us)
Async XLA Ops:
  0.6 1.0 copy-start
  30.8 14.5 %all-to-all-start.1 = ((bf16[4,16,16,512]{3,2,1,0:T(8,128)(2,1)}), bf16[4,16,16,512]{3,2,1,0:T(8,128)(2,1)S(1)}, u32[]{:S(2)}, u32[]{:S(2)}) async-start(bf16[4,16,16,512]{3,2,1,0:T(8,128)(2,1)} %broadcast_in_dim.15), calls=%async_computation.1 | async-start | bytes 2097152 | tf_op jit(solution)/shard_map/all_to_all | solution.py:357
  35.0 15.5 %copy-start.1 = (bf16[128,4096]{1,0:T(8,128)(2,1)S(1)}, bf16[128,4096]{1,0:T(8,128)(2,1)}, u32[]{:S(2)}) copy-start(bf16[128,4096]{1,0:T(8,128)(2,1)} %mine_ref) | copy-start | bytes 3145732
  37.0 27.1 %collective-permute-start.1 = (bf16[128,2048]{1,0:T(8,128)(2,1)}, bf16[128,2048]{1,0:T(8,128)(2,1)S(1)}, u32[]{:S(2)}, u32[]{:S(2)}) collective-permute-start(bf16[128,2048]{1,0:T(8,128)(2,1)} %constant_dynamic-slice_fusion), channel_id=1, source_target_pairs={{0,16},{16,0},{32,48},{48,32},{64,80},{80,64},{96,112},{112,96},{1... | collective-permute-start | bytes 1572872 | tf_op jit(solution)/shard_map/ppermute | solution.py:41
  45.3 24.0 %collective-permute-start.2 = (bf16[4,16,16,512]{3,2,1,0:T(8,128)(2,1)S(1)}, bf16[4,16,16,512]{3,2,1,0:T(8,128)(2,1)S(1)}, u32[]{:S(2)}, u32[]{:S(2)}) collective-permute-start(bf16[4,16,16,512]{3,2,1,0:T(8,128)(2,1)S(1)} %all-to-all-done.1.own_ref), channel_id=1, source_target_pairs={{0,256},{16,80},{32,288},{48,112},{64,320},{80,16},{96,352},{112,4... | collective-permute-start | bytes 3145736 | tf_op jit(solution)/shard_map/ppermute | solution.py:364
  50.5 18.8 %collective-permute-start.3 = (bf16[128,4096]{1,0:T(8,128)(2,1)S(1)}, bf16[128,4096]{1,0:T(8,128)(2,1)S(1)}, u32[]{:S(2)}, u32[]{:S(2)}) collective-permute-start(bf16[128,4096]{1,0:T(8,128)(2,1)S(1)} %copy-done.1), channel_id=1, source_target_pairs={{0,16},{16,0},{32,48},{48,32},{64,80},{80,64},{96,112},{112,96},{1... | collective-permute-start | bytes 3145736 | tf_op jit(solution)/shard_map/ppermute | solution.py:41
  57.7 16.7 %collective-permute-start.5 = (bf16[4,16,16,512]{3,2,1,0:T(8,128)(2,1)S(1)}, bf16[4,16,16,512]{3,2,1,0:T(8,128)(2,1)S(1)}, u32[]{:S(2)}, u32[]{:S(2)}) collective-permute-start(bf16[4,16,16,512]{3,2,1,0:T(8,128)(2,1)S(1)} %all-to-all-done.1.own_ref), channel_id=1, source_target_pairs={{0,384},{16,112},{32,416},{48,16},{64,448},{80,48},{96,480},{112,8... | collective-permute-start | bytes 3145736 | tf_op jit(solution)/shard_map/ppermute | solution.py:364
  60.4 17.0 %collective-permute-start.4 = (bf16[4,16,16,512]{3,2,1,0:T(8,128)(2,1)S(1)}, bf16[4,16,16,512]{3,2,1,0:T(8,128)(2,1)S(1)}, u32[]{:S(2)}, u32[]{:S(2)}) collective-permute-start(bf16[4,16,16,512]{3,2,1,0:T(8,128)(2,1)S(1)} %all-to-all-done.1.own_ref), channel_id=1, source_target_pairs={{0,128},{16,48},{32,160},{48,80},{64,192},{80,112},{96,224},{112,1... | collective-permute-start | bytes 3145736 | tf_op jit(solution)/shard_map/ppermute | solution.py:364
  64.1 5.2 %collective-permute-start = (bf16[128,2048]{1,0:T(8,128)(2,1)S(1)}, bf16[128,2048]{1,0:T(8,128)(2,1)S(1)}, u32[]{:S(2)}, u32[]{:S(2)}) collective-permute-start(bf16[128,2048]{1,0:T(8,128)(2,1)S(1)} %constant_dynamic-slice_fusion.1), channel_id=1, source_target_pairs={{0,16},{16,0},{32,48},{48,32},{64,80},{80,64},{96,112},{112,96},{1... | collective-permute-start | bytes 1572872 | tf_op jit(solution)/shard_map/ppermute | solution.py:41
  67.8 0.7 copy-start.4
  68.5 29.0 %copy-start.2 = (bf16[128,4096]{1,0:T(8,128)(2,1)S(1)}, bf16[128,4096]{1,0:T(8,128)(2,1)}, u32[]{:S(2)}) copy-start(bf16[128,4096]{1,0:T(8,128)(2,1)} %q_mine) | copy-start | bytes 3145732
  68.5 29.0 %copy-start.3 = (bf16[128,4096]{1,0:T(8,128)(2,1)S(1)}, bf16[128,4096]{1,0:T(8,128)(2,1)}, u32[]{:S(2)}) copy-start(bf16[128,4096]{1,0:T(8,128)(2,1)} %u_mine) | copy-start | bytes 3145732
  85.1 9.8 %collective-permute-start.7 = (bf16[256,512]{1,0:T(8,128)(2,1)S(1)}, bf16[256,512]{1,0:T(8,128)(2,1)S(1)}, u32[]{:S(2)}, u32[]{:S(2)}) collective-permute-start(bf16[256,512]{1,0:T(8,128)(2,1)S(1)} %projection.1.here_ref), channel_id=1, source_target_pairs={{0,32},{16,48},{32,64},{48,80},{64,96},{80,112},{96,128},{112,144}... | collective-permute-start | bytes 786440 | tf_op jit(solution)/shard_map/ppermute | solution.py:36
  87.1 10.5 %collective-permute-start.6 = (bf16[256,512]{1,0:T(8,128)(2,1)S(1)}, bf16[256,512]{1,0:T(8,128)(2,1)S(1)}, u32[]{:S(2)}, u32[]{:S(2)}) collective-permute-start(bf16[256,512]{1,0:T(8,128)(2,1)S(1)} %projection.1.here_ref), channel_id=1, source_target_pairs={{0,64},{16,80},{32,96},{48,112},{64,128},{80,144},{96,160},{112,17... | collective-permute-start | bytes 786440 | tf_op jit(solution)/shard_map/ppermute | solution.py:36
  110.1 26.0 %collective-permute-start.8 = (bf16[128,2816]{1,0:T(8,128)(2,1)S(1)}, bf16[128,2816]{1,0:T(8,128)(2,1)S(1)}, u32[]{:S(2)}, u32[]{:S(2)}) collective-permute-start(bf16[128,2816]{1,0:T(8,128)(2,1)S(1)} %get-tuple-element.26), channel_id=1, source_target_pairs={{0,16},{16,0},{32,48},{48,32},{64,80},{80,64},{96,112},{112,96},{1... | collective-permute-start | bytes 2162696 | tf_op jit(solution)/shard_map/ppermute | solution.py:41
  118.0 13.0 %collective-permute-start.9 = (bf16[128,512]{1,0:T(8,128)(2,1)S(1)}, bf16[128,512]{1,0:T(8,128)(2,1)S(1)}, u32[]{:S(2)}, u32[]{:S(2)}) collective-permute-start(bf16[128,512]{1,0:T(8,128)(2,1)S(1)} %get-tuple-element.29), channel_id=1, source_target_pairs={{32,0},{48,16},{64,32},{80,48},{96,64},{112,80},{128,96},{144,112}... | collective-permute-start | bytes 393224 | tf_op jit(solution)/shard_map/ppermute | solution.py:36
  121.6 9.5 %collective-permute-start.10 = (bf16[128,512]{1,0:T(8,128)(2,1)S(1)}, bf16[128,512]{1,0:T(8,128)(2,1)S(1)}, u32[]{:S(2)}, u32[]{:S(2)}) collective-permute-start(bf16[128,512]{1,0:T(8,128)(2,1)S(1)} %get-tuple-element.30), channel_id=1, source_target_pairs={{64,0},{80,16},{96,32},{112,48},{128,64},{144,80},{160,96},{176,11... | collective-permute-start | bytes 393224 | tf_op jit(solution)/shard_map/ppermute | solution.py:36
  123.8 7.7 %collective-permute-start.11 = (bf16[128,512]{1,0:T(8,128)(2,1)S(1)}, bf16[128,512]{1,0:T(8,128)(2,1)S(1)}, u32[]{:S(2)}, u32[]{:S(2)}) collective-permute-start(bf16[128,512]{1,0:T(8,128)(2,1)S(1)} %get-tuple-element.31), channel_id=1, source_target_pairs={{32,16},{48,0},{64,48},{80,32},{96,80},{112,64},{128,112},{144,96}... | collective-permute-start | bytes 393224 | tf_op jit(solution)/shard_map/ppermute | solution.py:36
  127.6 8.4 %collective-permute-start.12 = (bf16[128,512]{1,0:T(8,128)(2,1)S(1)}, bf16[128,512]{1,0:T(8,128)(2,1)S(1)}, u32[]{:S(2)}, u32[]{:S(2)}) collective-permute-start(bf16[128,512]{1,0:T(8,128)(2,1)S(1)} %get-tuple-element.32), channel_id=1, source_target_pairs={{64,16},{80,0},{96,48},{112,32},{128,80},{144,64},{160,112},{176,9... | collective-permute-start | bytes 393224 | tf_op jit(solution)/shard_map/ppermute | solution.py:36
